TPU v7x, 32 devices: a whole 2x2x4 slice. The times are simulated.
32 devices in a mesh: section: 2 (over x), rep: 16 (over z, y, core).
Axes of the slice: x: 2, y: 2, z: 4, core: 2. Of those that a mesh axis runs over, the one named last changes fastest.
Arguments:
- layer_in: bfloat16 [2, 64, 4096], P('section', 'rep'), may hold values from -6 to 6
- next_in: bfloat16 [2, 64, 4096], P('section', 'rep'), may hold values from -6 to 6
- returned: bfloat16 [2, 128, 4096], P('section', 'rep'), may hold values from -6 to 6
- norm_gain: float32 [2, 4096], P('section'), may hold values from 0.25 to 1.75
- gate_weight: bfloat16 [2, 4096, 14336], P('section', None, 'rep'), may hold values from -0.09375 to 0.09375
- up_weight: bfloat16 [2, 4096, 14336], P('section', None, 'rep'), may hold values from -0.09375 to 0.09375
- down_weight: bfloat16 [2, 14336, 4096], P('section', 'rep'), may hold values from -0.046875 to 0.046875
- wiring: int32 [2, 16, 16], P('section'), may hold values from 0 to 2, as said below
Outputs:
- forwarded: bfloat16 [2, 128, 4096], P('section', 'rep')
- input_grad: bfloat16 [2, 64, 4096], P('section', 'rep')
- next_out: bfloat16 [2, 64, 4096], P('section', 'rep')
Inputs may be any that keep to these rules, and one draw needn't show every extreme that they name: For every position p and row group r the entries wiring[p, r, :] sum to 2. For every position p and receiver j the column wiring[p, :, j] sums to at most 4, and in every position some column sums to exactly 4. In every position some row group sends all its 2 blocks to one receiver, and some receiver gets none.
All inputs are finite; a program needn't handle non-finite values.
Results may differ from a plain program's by a relative error of at most 0.035.
Values may be sent and summed in bfloat16 or wider, within the bound.
A program may use at most 128 MiB of HBM per device.

v0:
```python
import jax
import jax.numpy as jnp
from jax import lax
from jax.sharding import PartitionSpec as P

BLK = 2


epsilon = 1e-05
step_rate = 0.5


def passed_along(value, axis, by):
    peers = lax.axis_size(axis)
    return lax.ppermute(value, axis, [(i, (i + by) % peers) for i in range(peers)])


def route_tables(wiring_section, replicas, blocks_dev, capacity):
    row_total = jnp.cumsum(wiring_section, axis=1)
    column_total = jnp.cumsum(wiring_section, axis=0)
    row_start = row_total - wiring_section
    column_start = column_total - wiring_section
    slot_ids = jnp.arange(capacity, dtype=jnp.int32)
    block_ids = jnp.arange(blocks_dev, dtype=jnp.int32)
    member_ids = jnp.arange(replicas, dtype=jnp.int32)
    sender = jnp.sum(
        (column_total.T[:, :, None] <= slot_ids[None, None, :]).astype(jnp.int32), axis=1
    )
    slot_live = slot_ids[None, :] < column_total[replicas - 1][:, None]
    sender = jnp.minimum(sender, replicas - 1)
    within = slot_ids[None, :] - column_start[sender, member_ids[:, None]]
    within = jnp.where(slot_live, within, 0)
    local_source = sender * blocks_dev + within
    global_source = sender * blocks_dev + row_start[sender, member_ids[:, None]] + within
    target_member = jnp.sum(
        (row_total[:, None, :] <= block_ids[None, :, None]).astype(jnp.int32), axis=2
    )
    target_member = jnp.minimum(target_member, replicas - 1)
    block_offset = block_ids[None, :] - row_start[member_ids[:, None], target_member]
    global_target = (
        target_member * capacity + column_start[member_ids[:, None], target_member] + block_offset
    )
    local_target = target_member * blocks_dev + block_offset
    return (
        wiring_section,
        row_start,
        column_start,
        slot_live,
        local_source,
        global_source,
        global_target,
        local_target,
    )


def gather_rows(local_rows):
    return lax.all_gather(local_rows, "rep", axis=0, tiled=True)


def reduce_rows(term_rows):
    return lax.psum_scatter(
        term_rows.astype(jnp.bfloat16), "rep", scatter_dimension=0, tiled=True
    ).astype(jnp.float32)


def route_blocks(buffer_rows):
    return lax.all_to_all(buffer_rows, "rep", split_axis=0, concat_axis=0, tiled=True)


def pass_section(slot_rows, offset_by):
    return passed_along(slot_rows, "section", offset_by)


def normalize(layer_rows, gain_row):
    values = layer_rows.astype(jnp.float32)
    row_scale = lax.rsqrt(jnp.mean(values * values, axis=1, keepdims=True) + epsilon)
    normed_local = (values * row_scale * gain_row[None, :]).astype(jnp.bfloat16)
    return (values, row_scale, gather_rows(normed_local))


def down_terms(hidden, down_local, values, position):
    term_rows = jnp.dot(hidden, down_local, preferred_element_type=jnp.float32)
    row_count = values.shape[0]
    own_part = lax.dynamic_slice_in_dim(term_rows, position * row_count, row_count, 0) + values
    return lax.dynamic_update_slice_in_dim(term_rows, own_part, position * row_count, 0)


def local_forward(layer_rows, gain_row, gate_local, up_local, down_local, position):
    values, row_scale, normed = normalize(layer_rows, gain_row)
    gate_act = jnp.dot(normed, gate_local, preferred_element_type=jnp.float32)
    up_act = jnp.dot(normed, up_local, preferred_element_type=jnp.float32)
    hidden = (jax.nn.silu(gate_act) * up_act).astype(jnp.bfloat16)
    term_rows = down_terms(hidden, down_local, values, position)
    return (term_rows, values, row_scale, normed, gate_act, up_act, hidden)


def values_rows_term(values, row_scale, scaled_grad):
    return values * row_scale**3 * jnp.mean(values * scaled_grad, axis=1, keepdims=True)


def per_device(layer_in, next_in, returned, norm_gain, gate_weight, up_weight, down_weight, wiring):
    replicas = lax.axis_size("rep")
    position = lax.axis_index("rep")
    partner_offset = lax.axis_size("section") // 2
    row_count = layer_in.shape[1]
    feature_count = layer_in.shape[2]
    blocks_dev = row_count // BLK
    capacity = returned.shape[1] // BLK
    token_count = row_count * replicas
    gain_row = norm_gain[0]
    gate_local = gate_weight[0]
    up_local = up_weight[0]
    down_local = down_weight[0]
    zero_value = jnp.zeros((), jnp.bfloat16)
    block_ids = jnp.arange(blocks_dev, dtype=jnp.int32)
    (
        counts,
        row_start,
        column_start,
        slot_live,
        local_source,
        global_source,
        global_target,
        local_target,
    ) = route_tables(wiring[0], replicas, blocks_dev, capacity)
    term_rows, values, row_scale, normed, gate_act, up_act, hidden = local_forward(
        layer_in[0], gain_row, gate_local, up_local, down_local, position
    )
    out_rows = reduce_rows(term_rows).astype(jnp.bfloat16)
    own_blocks = out_rows.reshape(blocks_dev, BLK, feature_count)
    my_start = lax.dynamic_index_in_dim(row_start, position, 0, keepdims=False)
    my_counts = lax.dynamic_index_in_dim(counts, position, 0, keepdims=False)
    pick_index = jnp.minimum(my_start[:, None] + block_ids[None, :], blocks_dev - 1)
    keep_mask = block_ids[None, :] < my_counts[:, None]
    outgoing = jnp.take(own_blocks, pick_index.reshape(-1), axis=0).reshape(
        replicas, blocks_dev, BLK, feature_count
    )
    outgoing = jnp.where(keep_mask[:, :, None, None], outgoing, zero_value)
    incoming = route_blocks(outgoing.reshape(replicas, row_count, feature_count))
    incoming = incoming.reshape(replicas * blocks_dev, BLK, feature_count)
    my_source = lax.dynamic_index_in_dim(local_source, position, 0, keepdims=False)
    my_live = lax.dynamic_index_in_dim(slot_live, position, 0, keepdims=False)
    slot_blocks = jnp.where(
        my_live[:, None, None], jnp.take(incoming, my_source, axis=0), zero_value
    )
    slot_rows = slot_blocks.reshape(capacity * BLK, feature_count)
    forwarded = pass_section(slot_rows, 1)
    later_slots = pass_section(returned[0], -1)
    back_blocks = later_slots.reshape(capacity, BLK, feature_count)
    column_offsets = lax.dynamic_index_in_dim(column_start, position, 1, keepdims=False)
    column_counts = lax.dynamic_index_in_dim(counts, position, 1, keepdims=False)
    pick_back = jnp.minimum(column_offsets[:, None] + block_ids[None, :], capacity - 1)
    keep_back = block_ids[None, :] < column_counts[:, None]
    returning = jnp.take(back_blocks, pick_back.reshape(-1), axis=0).reshape(
        replicas, blocks_dev, BLK, feature_count
    )
    returning = jnp.where(keep_back[:, :, None, None], returning, zero_value)
    arrived = route_blocks(returning.reshape(replicas, row_count, feature_count))
    arrived = arrived.reshape(replicas * blocks_dev, BLK, feature_count)
    my_target = lax.dynamic_index_in_dim(local_target, position, 0, keepdims=False)
    cotangent_own = jnp.take(arrived, my_target, axis=0).reshape(row_count, feature_count)
    cotangent_all = gather_rows(cotangent_own)
    rows_contract = (((0,), (0,)), ((), ()))
    cols_contract = (((1,), (1,)), ((), ()))
    update_factor = step_rate / token_count
    grad_down = lax.dot_general(
        hidden, cotangent_all, rows_contract, preferred_element_type=jnp.float32
    )
    updated_down = (down_local.astype(jnp.float32) - update_factor * grad_down).astype(jnp.bfloat16)
    mate_down = passed_along(updated_down, "section", partner_offset)
    dhidden = lax.dot_general(
        cotangent_all, down_local, cols_contract, preferred_element_type=jnp.float32
    )
    sigmoid_gate = jax.nn.sigmoid(gate_act)
    silu_gate = gate_act * sigmoid_gate
    grad_gate_act = (
        dhidden * up_act * sigmoid_gate * (1.0 + gate_act * (1.0 - sigmoid_gate))
    ).astype(jnp.bfloat16)
    grad_up_act = (dhidden * silu_gate).astype(jnp.bfloat16)
    dterm_rows = lax.dot_general(
        grad_gate_act, gate_local, cols_contract, preferred_element_type=jnp.float32
    )
    dterm_rows = dterm_rows + lax.dot_general(
        grad_up_act, up_local, cols_contract, preferred_element_type=jnp.float32
    )
    dnormed = reduce_rows(dterm_rows)
    scaled_grad = gain_row[None, :] * dnormed
    input_grad = (
        cotangent_own.astype(jnp.float32)
        + row_scale * scaled_grad
        - values_rows_term(values, row_scale, scaled_grad)
    ).astype(jnp.bfloat16)
    grad_gate = lax.dot_general(
        normed, grad_gate_act, rows_contract, preferred_element_type=jnp.float32
    )
    grad_up = lax.dot_general(
        normed, grad_up_act, rows_contract, preferred_element_type=jnp.float32
    )
    updated_gate = (gate_local.astype(jnp.float32) - update_factor * grad_gate).astype(jnp.bfloat16)
    updated_up = (up_local.astype(jnp.float32) - update_factor * grad_up).astype(jnp.bfloat16)
    next_values, next_scale, next_normed = normalize(next_in[0], gain_row)
    own_gate_next = jnp.dot(next_normed, updated_gate, preferred_element_type=jnp.float32)
    own_up_next = jnp.dot(next_normed, updated_up, preferred_element_type=jnp.float32)
    mate_pair = passed_along(jnp.stack((updated_gate, updated_up)), "section", partner_offset)
    mate_gate_next = jnp.dot(next_normed, mate_pair[0], preferred_element_type=jnp.float32)
    mate_up_next = jnp.dot(next_normed, mate_pair[1], preferred_element_type=jnp.float32)
    gate_next = 0.5 * (own_gate_next + mate_gate_next)
    up_next = 0.5 * (own_up_next + mate_up_next)
    hidden_next = (jax.nn.silu(gate_next) * up_next).astype(jnp.bfloat16)
    averaged_down = (
        (updated_down.astype(jnp.float32) + mate_down.astype(jnp.float32)) * 0.5
    ).astype(jnp.bfloat16)
    term_next = down_terms(hidden_next, averaged_down, next_values, position)
    next_rows = reduce_rows(term_next).astype(jnp.bfloat16)
    return (forwarded[None], input_grad[None], next_rows[None])


def solution(mesh):
    in_specs = (
        P("section", "rep", None),
        P("section", "rep", None),
        P("section", "rep", None),
        P("section", None),
        P("section", None, "rep"),
        P("section", None, "rep"),
        P("section", "rep", None),
        P("section", None, None),
    )
    out_specs = (P("section", "rep", None), P("section", "rep", None), P("section", "rep", None))
    return jax.shard_map(
        per_device, mesh=mesh, in_specs=in_specs, out_specs=out_specs, check_vma=False
    )
```

profile of v0, /device:TPU:0, one launch (start us, length us, event | category | flops | bytes accessed | tf_op | source)
XLA Modules:
  0.0 725.3 jit_solution(3110457943252556763)
XLA Ops:
  7.2 3.0 collective-permute-start.1
  10.2 0.7 reduce_window_sum.22
  10.9 0.9 reduce_window_sum.23
  11.9 0.7 bitcast_subtract_fusion
  12.6 0.9 dynamic-slice_reduce_fusion.1
  14.4 0.7 gather_fusion.3
  15.8 0.5 multiply_multiply_fusion
  16.5 0.4 copy-done.15
  17.1 1.6 gather_fusion.4
  18.7 0.2 gather.37
  18.9 1.2 select_select_fusion
  20.1 5.9 all-to-all-start.1
  26.1 26.9 %all-gather = bf16[16,4,4096]{2,1,0:T(4,128)(2,1)S(1)} all-gather(bf16[1,4,4096]{2,1,0:T(4,128)(2,1)S(1)} %get-tuple-element.10), channel_id=1, replica_groups=mesh['section'=2,'rep'=16] {'rep'}, dimensions={0}, use_global_device_ids=true | all-gather | bytes 557056 | tf_op jit(solution)/shard_map/all_gather | solution.py:57
  53.2 4.3 fusion.9
  57.5 0.3 reshape.323
  57.8 0.6 gather_fusion.5
  58.5 0.5 copy-done.6
  59.1 21.0 %all-gather.1 = bf16[16,4,4096]{2,1,0:T(4,128)(2,1)S(1)} all-gather(bf16[1,4,4096]{2,1,0:T(4,128)(2,1)S(1)} %fusion.61), channel_id=1, replica_groups=mesh['section'=2,'rep'=16] {'rep'}, dimensions={0}, use_global_device_ids=true | all-gather | bytes 557056 | tf_op jit(solution)/shard_map/all_gather | solution.py:57
  80.2 5.6 fusion.3
  85.8 4.6 multiply_convert_fusion.4
  90.4 5.1 subtract_convert_fusion.2
  95.6 2.1 subtract_convert_fusion.1
  97.7 12.1 %pad_maximum_fusion = bf16[2,4096,896]{2,1,0:T(8,128)(2,1)} fusion(bf16[1,4096,896]{2,1,0:T(8,128)(2,1)S(1)} %bitcast.138, bf16[1,4096,896]{2,1,0:T(8,128)(2,1)} %bitcast.141), kind=kLoop, calls=%fused_computation.6 | loop fusion | flops 7340032 | bytes 29360128 | tf_op jit(solution)/shard_map/stack | solution.py:204
  109.8 0.5 collective-permute-start.2
  110.4 5.1 subtract_convert_fusion
  115.4 1.5 collective-permute-start.3
  116.9 18.9 %all-gather.2 = bf16[16,4,4096]{2,1,0:T(4,128)(2,1)S(1)} all-gather(bf16[1,4,4096]{2,1,0:T(4,128)(2,1)S(1)} %get-tuple-element.9), channel_id=1, replica_groups=mesh['section'=2,'rep'=16] {'rep'}, dimensions={0}, use_global_device_ids=true | all-gather | bytes 557056 | tf_op jit(solution)/shard_map/all_gather | solution.py:57
  135.8 0.9 reshape.375
  136.8 0.6 min.77
  137.4 0.7 copy.59
  138.1 0.7 fusion.53
  138.8 0.7 copy.58
  139.8 0.5 copy-done.10
  140.4 0.8 gather_fusion
  141.4 0.7 slice_bitcast_fusion.16
  142.1 0.7 select_add_fusion
  143.0 0.5 copy-done.19
  143.7 4.7 fusion.5
  148.4 0.8 convert_element_type.90
  149.3 2.4 fusion.7
  151.6 4.5 fusion.62
  156.2 1.2 fusion.63
  157.4 0.6 slice-done.3
  158.1 3.2 fusion.19
  161.2 267.0 %collective-permute-done.2 = bf16[2,4096,896]{2,1,0:T(8,128)(2,1)} collective-permute-done((bf16[2,4096,896]{2,1,0:T(8,128)(2,1)}, bf16[2,4096,896]{2,1,0:T(8,128)(2,1)}, u32[]{:S(2)}, u32[]{:S(2)}) %collective-permute-start.2) | collective-permute-done | bytes 14680096 | tf_op jit(solution)/shard_map/ppermute | solution.py:15
  428.2 4.3 fusion.23
  432.6 152.3 %collective-permute-done.3 = bf16[896,4096]{1,0:T(8,128)(2,1)} collective-permute-done((bf16[896,4096]{1,0:T(8,128)(2,1)}, bf16[896,4096]{1,0:T(8,128)(2,1)}, u32[]{:S(2)}, u32[]{:S(2)}) %collective-permute-start.3) | collective-permute-done | bytes 7340064 | tf_op jit(solution)/shard_map/ppermute | solution.py:15
  585.0 11.0 %fusion = f32[64,4096]{1,0:T(8,128)S(1)} fusion(bf16[896,4096]{1,0:T(8,128)(2,1)} %collective-permute-done.3, bf16[896,4096]{1,0:T(8,128)(2,1)} %subtract_convert_fusion, f32[64,896]{1,0:T(8,128)S(1)} %fusion.23, f32[64,896]{1,0:T(8,128)S(1)} %fusion.63, bf16[64,4096]{1,0:T(8,128)(2,1)S(1)} %copy-done.2, bf16[2,4096,896]{2,1,0:T(8,128)(2,1)} %collective-permute-done.2), kind=kOutput, calls=%fused_computation.11 | convolution fusion | flops 958332928 | bytes 24051712 | tf_op jit(solution)/shard_map/dot_general | solution.py:82
  596.1 0.8 convert_element_type.111
  597.3 0.6 dynamic-slice.2
  598.6 90.6 %all-reduce.6.cloned.1.call-done = (bf16[64,4096]{1,0:T(8,128)(2,1)}, bf16[64,4096]{1,0:T(8,128)(2,1)}, bf16[64,4096]{1,0:T(8,128)(2,1)}) async-done(((bf16[64,4096]{1,0:T(8,128)(2,1)}, bf16[64,4096]{1,0:T(8,128)(2,1)}, bf16[64,4096]{1,0:T(8,128)(2,1)}), (bf16[64,4096]{1,0:T(8,128)(2,1)}, bf16[64,4096]{1,0:T(8,128)(2,1)}, bf16[64,4096]{1,0:T(8,128)(2,1)})) %all-reduce.6.cloned.1.call-update) | async-done | bytes 1572880
  689.2 1.0 fusion.40
  690.2 0.9 constant_dynamic-slice_fusion.5
  691.1 1.6 gather_fusion.1
  693.0 1.2 select_select_fusion.1
  694.2 3.7 all-to-all-start
  698.0 1.6 fusion.43
  699.6 12.8 %all-to-all-done = bf16[16,4,4096]{2,1,0:T(4,128)(2,1)S(1)} async-done(((bf16[16,4,4096]{2,1,0:T(4,128)(2,1)}), bf16[16,4,4096]{2,1,0:T(4,128)(2,1)S(1)}, u32[]{:S(2)}, u32[]{:S(2)}) %all-to-all-start) | async-done | bytes 524320 | tf_op jit(solution)/shard_map/all_to_all | solution.py:67
  712.4 0.3 reshape.321
  712.7 0.7 gather_fusion.2
  713.5 1.5 collective-permute-start
  715.0 1.5 dynamic-slice_bitcast_fusion
  716.5 1.3 collective-permute-done
  717.8 0.6 copy.72
  (147 shorter events, 4.4 us)
Async XLA Ops:
  7.2 8.5 %copy-start.3 = (bf16[1,4,4096]{2,1,0:T(4,128)(2,1)S(1)}, bf16[1,4,4096]{2,1,0:T(4,128)(2,1)}, u32[]{:S(2)}) copy-start(bf16[1,4,4096]{2,1,0:T(4,128)(2,1)} %param.8) | copy-start | bytes 98308
  7.2 9.2 %copy-start.4 = (bf16[1,4,4096]{2,1,0:T(4,128)(2,1)S(1)}, bf16[1,4,4096]{2,1,0:T(4,128)(2,1)}, u32[]{:S(2)}) copy-start(bf16[1,4,4096]{2,1,0:T(4,128)(2,1)} %param.9) | copy-start | bytes 98308
  7.2 9.7 %copy-start.8 = (f32[1,4096]{1,0:T(1,128)S(1)}, f32[1,4096]{1,0:T(1,128)}, u32[]{:S(2)}) copy-start(f32[1,4096]{1,0:T(1,128)} %param.11) | copy-start | bytes 49156
  7.2 9.8 %collective-permute-start.1 = (bf16[8,4096]{1,0:T(8,128)(2,1)}, bf16[8,4096]{1,0:T(8,128)(2,1)S(1)}, u32[]{:S(2)}, u32[]{:S(2)}) collective-permute-start(bf16[8,4096]{1,0:T(8,128)(2,1)} %bitcast.149), channel_id=1, source_target_pairs={{0,16},{16,0},{1,17},{17,1},{2,18},{18,2},{3,19},{19,3},{4,20},{20... | collective-permute-start | bytes 196616 | tf_op jit(solution)/shard_map/ppermute | solution.py:15
  10.9 128.6 %copy-start.9 = (s32[16,16]{1,0:T(8,128)}, s32[16,16]{1,0:T(8,128)S(1)}, u32[]{:S(2)}) copy-start(s32[16,16]{1,0:T(8,128)S(1)} %reduce_window_sum.22) | copy-start | bytes 3076
  15.6 42.8 %copy-start.13 = (pred[4]{0:T(512)(128)(4,1)}, pred[4]{0:T(512)(128)(4,1)S(1)}, u32[]{:S(2)}) copy-start(pred[4]{0:T(512)(128)(4,1)S(1)} %broadcast_in_dim.165) | copy-start | bytes 16
  16.3 0.6 copy-start.15
  20.1 37.4 %all-to-all-start.1 = ((bf16[16,4,4096]{2,1,0:T(4,128)(2,1)}), bf16[16,4,4096]{2,1,0:T(4,128)(2,1)S(1)}, u32[]{:S(2)}, u32[]{:S(2)}) async-start(bf16[16,4,4096]{2,1,0:T(4,128)(2,1)} %select_select_fusion), calls=%async_computation.1 | async-start | bytes 1048576 | tf_op jit(solution)/shard_map/all_to_all | solution.py:67
  26.1 663.2 %all-reduce.6.cloned.1.call-start = ((), (), s32[]{:S(2)}) async-start(), calls=%async_computation.2 | async-start | bytes 3145728
  58.4 0.6 copy-start.6
  80.2 10.2 %slice-start = ((s8[7340032]{0:T(1024)(128)(4,1)}), s8[4194304]{0:T(1024)(128)(4,1)S(1)}, s32[]{:S(2)}) async-start(s8[7340032]{0:T(1024)(128)(4,1)} %bitcast.128), calls=%async_computation.3 | async-start | bytes 8388608
  80.2 15.4 %slice-start.6 = ((s8[7340032]{0:T(1024)(128)(4,1)}), s8[4194304]{0:T(1024)(128)(4,1)S(1)}, s32[]{:S(2)}) async-start(s8[7340032]{0:T(1024)(128)(4,1)} %bitcast.134), calls=%async_computation.9 | async-start | bytes 8388608
  85.8 4.6 slice-start.1
  85.8 9.8 %slice-start.7 = ((s8[7340032]{0:T(1024)(128)(4,1)}), s8[3145728]{0:T(1024)(128)(4,1)S(1)}, s32[]{:S(2)}) async-start(s8[7340032]{0:T(1024)(128)(4,1)} %bitcast.134), calls=%async_computation.10 | async-start | bytes 6291456
  95.6 14.8 %slice-start.4 = ((s8[7340032]{0:T(1024)(128)(4,1)}), s8[4194304]{0:T(1024)(128)(4,1)S(1)}, s32[]{:S(2)}) async-start(s8[7340032]{0:T(1024)(128)(4,1)} %bitcast.132), calls=%async_computation.7 | async-start | bytes 8388608
  97.7 12.1 %copy-start = (bf16[4096,896]{1,0:T(8,128)(2,1)}, bf16[4096,896]{1,0:T(8,128)(2,1)S(1)}, u32[]{:S(2)}) copy-start(bf16[4096,896]{1,0:T(8,128)(2,1)S(1)} %subtract_convert_fusion.1) | copy-start | bytes 22020100
  97.7 12.6 %slice-start.5 = ((s8[7340032]{0:T(1024)(128)(4,1)}), s8[3145728]{0:T(1024)(128)(4,1)S(1)}, s32[]{:S(2)}) async-start(s8[7340032]{0:T(1024)(128)(4,1)} %bitcast.132), calls=%async_computation.8 | async-start | bytes 6291456
  109.8 318.4 %collective-permute-start.2 = (bf16[2,4096,896]{2,1,0:T(8,128)(2,1)}, bf16[2,4096,896]{2,1,0:T(8,128)(2,1)}, u32[]{:S(2)}, u32[]{:S(2)}) collective-permute-start(bf16[2,4096,896]{2,1,0:T(8,128)(2,1)} %pad_maximum_fusion), channel_id=1, source_target_pairs={{0,16},{16,0},{1,17},{17,1},{2,18},{18,2},{3,19},{19,3},{4,20},{20... | collective-permute-start | bytes 44040200 | tf_op jit(solution)/shard_map/ppermute | solution.py:15
  115.4 469.5 %collective-permute-start.3 = (bf16[896,4096]{1,0:T(8,128)(2,1)}, bf16[896,4096]{1,0:T(8,128)(2,1)}, u32[]{:S(2)}, u32[]{:S(2)}) collective-permute-start(bf16[896,4096]{1,0:T(8,128)(2,1)} %subtract_convert_fusion), channel_id=1, source_target_pairs={{0,16},{16,0},{1,17},{17,1},{2,18},{18,2},{3,19},{19,3},{4,20},{20... | collective-permute-start | bytes 22020104 | tf_op jit(solution)/shard_map/ppermute | solution.py:15
  139.7 0.6 copy-start.10
  140.4 8.8 %slice-start.8 = ((s8[7340032]{0:T(1024)(128)(4,1)}), s8[3145728]{0:T(1024)(128)(4,1)S(1)}, s32[]{:S(2)}) async-start(s8[7340032]{0:T(1024)(128)(4,1)} %bitcast.136), calls=%async_computation.11 | async-start | bytes 6291456
  142.1 0.9 copy-start.21
  143.0 0.5 copy-start.19
  143.7 5.6 slice-start.9
  148.3 3.3 copy-start.1
  148.4 7.7 %slice-start.10 = ((s8[7340032]{0:T(1024)(128)(4,1)}), s8[4194304]{0:T(1024)(128)(4,1)S(1)}, s32[]{:S(2)}) async-start(s8[7340032]{0:T(1024)(128)(4,1)} %bitcast.139), calls=%async_computation.13 | async-start | bytes 8388608
  149.3 6.9 slice-start.11
  151.6 5.8 slice-start.2
  156.2 1.9 slice-start.3
  158.1 426.9 %copy-start.2 = (bf16[64,4096]{1,0:T(8,128)(2,1)S(1)}, bf16[64,4096]{1,0:T(8,128)(2,1)}, u32[]{:S(2)}) copy-start(bf16[64,4096]{1,0:T(8,128)(2,1)} %reshape.375) | copy-start | bytes 1572868
  432.6 163.4 %copy-start.5 = (bf16[1,4,4096]{2,1,0:T(4,128)(2,1)S(1)}, bf16[1,4,4096]{2,1,0:T(4,128)(2,1)}, u32[]{:S(2)}) copy-start(bf16[1,4,4096]{2,1,0:T(4,128)(2,1)} %param.9) | copy-start | bytes 98308
  432.6 164.4 %copy-start.22 = (s32[16]{0:T(128)S(1)}, s32[16]{0:T(128)}, u32[]{:S(2)}) copy-start(s32[16]{0:T(128)} %copy-done.21) | copy-start | bytes 196
  432.6 164.7 %copy-start.23 = (u32[32]{0:T(128)S(1)}, u32[32]{0:T(128)}, u32[]{:S(2)}) copy-start(u32[32]{0:T(128)} %constant.169) | copy-start | bytes 388
  432.6 166.0 %copy-start.18 = (s32[32,1]{0,1:T(1,128)S(1)}, s32[32,1]{0,1:T(1,128)}, u32[]{:S(2)}) copy-start(s32[32,1]{0,1:T(1,128)} %min.77) | copy-start | bytes 388
  432.6 166.0 %copy-start.20 = (s32[4]{0:T(128)S(1)}, s32[4]{0:T(128)}, u32[]{:S(2)}) copy-start(s32[4]{0:T(128)} %copy-done.19) | copy-start | bytes 52
  432.6 260.3 %copy-start.11 = (pred[16,4]{1,0:T(8,128)(4,1)S(1)}, pred[16,4]{1,0:T(8,128)(4,1)}, u32[]{:S(2)}) copy-start(pred[16,4]{1,0:T(8,128)(4,1)} %copy.59) | copy-start | bytes 196
  432.6 260.3 %copy-start.12 = (pred[16,4]{1,0:T(8,128)(4,1)S(1)}, pred[16,4]{1,0:T(8,128)(4,1)}, u32[]{:S(2)}) copy-start(pred[16,4]{1,0:T(8,128)(4,1)} %copy.58) | copy-start | bytes 196
  596.0 102.0 %copy-start.7 = (bf16[4,4096]{1,0:T(4,128)(2,1)S(1)}, bf16[4,4096]{1,0:T(4,128)(2,1)}, u32[]{:S(2)}) copy-start(bf16[4,4096]{1,0:T(4,128)(2,1)} %copy-done.6) | copy-start | bytes 98308
  596.0 102.0 %copy-start.14 = (pred[4]{0:T(512)(128)(4,1)S(1)}, pred[4]{0:T(512)(128)(4,1)}, u32[]{:S(2)}) copy-start(pred[4]{0:T(512)(128)(4,1)} %copy-done.13) | copy-start | bytes 16
  596.0 102.0 %copy-start.16 = (f32[4]{0:T(128)S(1)}, f32[4]{0:T(128)}, u32[]{:S(2)}) copy-start(f32[4]{0:T(128)} %copy-done.15) | copy-start | bytes 52
  596.0 102.0 %copy-start.17 = (f32[4]{0:T(128)S(1)}, f32[4]{0:T(128)}, u32[]{:S(2)}) copy-start(f32[4]{0:T(128)} %get-tuple-element.13) | copy-start | bytes 52
  694.2 18.2 %all-to-all-start = ((bf16[16,4,4096]{2,1,0:T(4,128)(2,1)}), bf16[16,4,4096]{2,1,0:T(4,128)(2,1)S(1)}, u32[]{:S(2)}, u32[]{:S(2)}) async-start(bf16[16,4,4096]{2,1,0:T(4,128)(2,1)} %select_select_fusion.1), calls=%async_computation | async-start | bytes 1048576 | tf_op jit(solution)/shard_map/all_to_all | solution.py:67
  713.5 4.3 collective-permute-start
Sparse Core Ops, SparseCore 0:
  597.1 92.1 all-reduce.5
where the time goes:
time: 726 us; the launch traced here: 725 us
  waiting for transfers between devices  524 us (72%)
  blocking collectives  66.8 us (9%)
  matrix products  58 us (8%)
  other arithmetic  23.4 us (3%)
  local copies, waits for them, and re-layouts  21.2 us (3%)
  starting transfers between devices  16.3 us (2%)
  between operations  15.4 us (2%)
    ppermute x4, waiting for transfers between devices, passed_along(): lax.ppermute(value, axis, [(i, (i + by) % peers) for i in range(peers)])  421 us
    unnamed x2, waiting for transfers between devices  90.6 us
    all_gather x3, blocking collectives, gather_rows(): return lax.all_gather(local_rows, 'rep', axis=0, tiled=True)  66.8 us
    dot_general x2, matrix products, down_terms(): term_rows = jnp.dot(hidden, down_local, preferred_element_type=jnp.float32)  15.7 us
  transfers between devices with their start and end apart: 7, of which 5 were waited for; matrix products, arithmetic and copies ran while one was open for 7% of the time, Pallas kernels for 0%

commit v1 on v0

v1 whole, which is shorter than its diff:
```python
import jax
import jax.numpy as jnp
from jax import lax
from jax.sharding import PartitionSpec as P

BLK = 2
epsilon = 1e-05
step_rate = 0.5
F32 = jnp.float32
BF16 = jnp.bfloat16


def passed_along(value, by):
    peers = lax.axis_size("section")
    return lax.ppermute(value, "section", [(i, (i + by) % peers) for i in range(peers)])


def route_select(counts, replicas, blocks_dev, capacity):
    blocks = replicas * blocks_dev
    row_total = jnp.cumsum(counts, axis=1)
    column_start = jnp.cumsum(counts, axis=0) - counts
    row_start = row_total - counts
    block_ids = jnp.arange(blocks_dev, dtype=jnp.int32)
    inside = (block_ids[None, :, None] >= row_start[:, None, :]) & (
        block_ids[None, :, None] < row_total[:, None, :]
    )
    member_ids = jnp.arange(replicas, dtype=jnp.int32)
    slot = member_ids[None, None, :] * capacity + (
        column_start[:, None, :] + block_ids[None, :, None] - row_start[:, None, :]
    )
    target = jnp.sum(jnp.where(inside, slot, 0), axis=2).reshape(blocks)
    return target


def row_one_hot(target, slots):
    rows = jnp.arange(slots * BLK, dtype=jnp.int32)
    target_rows = (target[:, None] * BLK + jnp.arange(BLK, dtype=jnp.int32)[None, :]).reshape(-1)
    return (rows[:, None] == target_rows[None, :]).astype(BF16)


def mm(a, b):
    return jnp.dot(a, b, preferred_element_type=F32)


def mm_t(a, b):
    return lax.dot_general(a, b, (((1,), (1,)), ((), ())), preferred_element_type=F32)


def normalize(layer_rows, gain_row):
    values = layer_rows.astype(F32)
    row_scale = lax.rsqrt(jnp.mean(values * values, axis=1, keepdims=True) + epsilon)
    return values, row_scale, (values * row_scale * gain_row[None, :]).astype(BF16)


def low_rank(coefs, factors):
    high = coefs.astype(BF16)
    low = (coefs - high.astype(F32)).astype(BF16)
    return mm(jnp.concatenate((high, low), 1), jnp.concatenate((factors, factors), 0))


def scatter_terms(terms):
    got = lax.all_to_all(terms, "rep", split_axis=0, concat_axis=0, tiled=True)
    return jnp.sum(got.astype(F32), axis=0)


def per_device(layer_in, next_in, returned, norm_gain, gate_weight, up_weight, down_weight, wiring):
    replicas = lax.axis_size("rep")
    position = lax.axis_index("rep")
    partner_offset = lax.axis_size("section") // 2
    rows = layer_in.shape[1]
    features = layer_in.shape[2]
    blocks_dev = rows // BLK
    slot_rows = returned.shape[1]
    capacity = slot_rows // BLK
    tokens = rows * replicas
    gain = norm_gain[0]
    gate, up, down = gate_weight[0], up_weight[0], down_weight[0]
    factor = step_rate / tokens

    values, row_scale, normed_own = normalize(layer_in[0], gain)
    next_values, _, next_own = normalize(next_in[0], gain)
    next_mate = passed_along(next_own, partner_offset)
    later = passed_along(returned[0], -1)
    packed = jnp.concatenate((normed_own, next_own, next_mate, later), 0)
    target = route_select(wiring[0], replicas, blocks_dev, capacity)
    select = row_one_hot(target, replicas * capacity)
    everything = lax.all_gather(packed, "rep", axis=0, tiled=False)
    normed = everything[:, :rows].reshape(tokens, features)
    nexts = jnp.concatenate(
        (
            everything[:, rows : 2 * rows].reshape(tokens, features),
            everything[:, 2 * rows : 3 * rows].reshape(tokens, features),
        ),
        0,
    )
    slots = everything[:, 3 * rows :].reshape(replicas * slot_rows, features)
    cotangent = lax.dot_general(
        select, slots, (((0,), (0,)), ((), ())), preferred_element_type=F32
    ).astype(BF16)

    lhs = jnp.concatenate((normed, nexts), 0)
    gate_all = mm(lhs, gate)
    up_all = mm(lhs, up)
    gate_act, up_act = gate_all[:tokens], up_all[:tokens]
    sigmoid = jax.nn.sigmoid(gate_act)
    silu = gate_act * sigmoid
    hidden = (silu * up_act).astype(BF16)
    dhidden = mm_t(cotangent, down)
    d_gate = (dhidden * up_act * sigmoid * (1.0 + gate_act * (1.0 - sigmoid))).astype(BF16)
    d_up = (dhidden * silu).astype(BF16)

    coefs = factor * mm_t(nexts, normed)
    next_gate = 0.5 * (gate_all[tokens:] - low_rank(coefs, d_gate))
    next_up = 0.5 * (up_all[tokens:] - low_rank(coefs, d_up))
    to_mate = jnp.stack((next_gate[tokens:], next_up[tokens:])).astype(BF16)
    from_mate = passed_along(to_mate, partner_offset).astype(F32)

    dterm = (mm_t(d_gate, gate) + mm_t(d_up, up)).astype(BF16)
    term = mm(hidden, down)
    own = lax.dynamic_slice_in_dim(term, position * rows, rows, 0) + values
    term = lax.dynamic_update_slice_in_dim(term, own, position * rows, 0).astype(BF16)
    slot_term = mm(select, term).astype(BF16)
    first = scatter_terms(
        jnp.concatenate(
            (
                slot_term.reshape(replicas, slot_rows, features),
                dterm.reshape(replicas, rows, features),
            ),
            1,
        )
    )

    gate_next = next_gate[:tokens] + from_mate[0]
    up_next = next_up[:tokens] + from_mate[1]
    hidden_own = (jax.nn.silu(gate_next) * up_next).astype(BF16)
    hidden_mate = passed_along(hidden_own, partner_offset)
    hidden_both = jnp.concatenate((hidden_own, hidden_mate), 0)
    down_coefs = factor * mm_t(hidden_both, hidden)
    term_next = (0.5 * (mm(hidden_both, down) - low_rank(down_coefs, cotangent))).astype(BF16)
    term_next = term_next.reshape(2, replicas, rows, features).transpose(1, 0, 2, 3)
    second = scatter_terms(term_next.reshape(replicas, 2 * rows, features))
    mate_sum = passed_along(second[rows:], partner_offset)
    next_out = (second[:rows] + mate_sum + next_values).astype(BF16)

    forwarded = passed_along(first[:slot_rows].astype(BF16), 1)
    dnormed = first[slot_rows:]
    scaled = gain[None, :] * dnormed
    cotangent_own = lax.dynamic_slice_in_dim(cotangent, position * rows, rows, 0)
    input_grad = (
        cotangent_own.astype(F32)
        + row_scale * scaled
        - values * row_scale**3 * jnp.mean(values * scaled, axis=1, keepdims=True)
    ).astype(BF16)
    return (forwarded[None], input_grad[None], next_out[None])


def solution(mesh):
    in_specs = (
        P("section", "rep", None),
        P("section", "rep", None),
        P("section", "rep", None),
        P("section", None),
        P("section", None, "rep"),
        P("section", None, "rep"),
        P("section", "rep", None),
        P("section", None, None),
    )
    out_specs = (P("section", "rep", None), P("section", "rep", None), P("section", "rep", None))
    return jax.shard_map(
        per_device, mesh=mesh, in_specs=in_specs, out_specs=out_specs, check_vma=False
    )
```

time: 726 us -> 193 us (0.27)
  the two profiles are of different devices: /device:TPU:0 before, /device:TPU:16 now
where the time goes in v1:
time: 193 us; the launch traced here: 192 us
  waiting for transfers between devices  114 us (59%)
  matrix products  27.4 us (14%)
  starting transfers between devices  17.2 us (9%)
  between operations  14.4 us (7%)
  other arithmetic  10.7 us (6%)
  local copies, waits for them, and re-layouts  8.39 us (4%)
    all_to_all x2, waiting for transfers between devices, scatter_terms(): got = lax.all_to_all(terms, 'rep', split_axis=0, concat_axis=0, tiled=True)  60.5 us
    all_gather x1, waiting for transfers between devices, per_device(): everything = lax.all_gather(packed, 'rep', axis=0, tiled=False)  42.4 us
    dot_general x8, matrix products, mm(): return jnp.dot(a, b, preferred_element_type=F32)  17.3 us
    ppermute x6, waiting for transfers between devices, passed_along(): lax.ppermute(value, 'section', [(i, (i + by) % peers) for i in range(peer...  11.4 us
    all_to_all x2, starting transfers between devices, scatter_terms(): got = lax.all_to_all(terms, 'rep', split_axis=0, concat_axis=0, tiled=True)  8.92 us
    ppermute x6, starting transfers between devices, passed_along(): lax.ppermute(value, 'section', [(i, (i + by) % peers) for i in range(peer...  8.22 us
    dot_general x5, matrix products, mm_t(): lax.dot_general(a, b, (((1,), (1,)), ((), ())), preferred_element_type=F32)  7.76 us
  transfers between devices with their start and end apart: 9, of which 7 were waited for; matrix products, arithmetic and copies ran while one was open for 10% of the time, Pallas kernels for 0%

profile of v1, /device:TPU:16, one launch (start us, length us, event | category | flops | bytes accessed | tf_op | source)
XLA Modules:
  0.0 192.3 jit_solution(17131094673995531546)
XLA Ops:
  7.2 0.0 all-gather.4.cloned.1.call-start
  7.2 1.6 collective-permute-start.1
  8.8 0.9 fusion.53
  9.7 0.9 fusion.57
  10.6 0.9 fusion.59
  11.5 0.6 collective-permute-start
  12.1 3.4 %collective-permute-done = bf16[4,4096]{1,0:T(4,128)(2,1)S(1)} collective-permute-done((bf16[4,4096]{1,0:T(4,128)(2,1)S(1)}, bf16[4,4096]{1,0:T(4,128)(2,1)S(1)}, u32[]{:S(2)}, u32[]{:S(2)}) %collective-permute-start) | collective-permute-done | bytes 32800 | tf_op jit(solution)/shard_map/ppermute | solution.py:15
  15.5 0.8 maximum_bitcast_fusion
  16.3 0.0 all-gather.4.cloned.1.call-update
  16.3 0.9 reduce_window_sum.22
  17.1 0.7 reduce_window_sum.23
  17.9 0.7 bitcast_subtract_fusion.1
  18.6 0.1 select_reduce_fusion
  18.7 0.1 copy.14
  18.8 0.1 mul.145
  18.9 0.1 iota_add_fusion
  19.0 0.1 add.101
  19.1 42.4 %all-gather.4.cloned.1.call-done = bf16[16,20,4096]{2,1,0:T(8,128)(2,1)} async-done(((bf16[1,20,4096]{2,1,0:T(8,128)(2,1)}), bf16[16,20,4096]{2,1,0:T(8,128)(2,1)}) %all-gather.4.cloned.1.call-update) | async-done | bytes 2621456 | tf_op jit(solution)/shard_map/all_gather | solution.py:87
  61.5 2.7 %fusion.79 = (bf16[16,4,4096]{2,1,0:T(4,128)(2,1)S(1)}, bf16[16,4,4096]{2,1,0:T(4,128)(2,1)S(1)}, bf16[16,4,4096]{2,1,0:T(4,128)(2,1)S(1)}) fusion(bf16[16,20,4096]{2,1,0:T(8,128)(2,1)} %all-gather.4.cloned.1.call-done), kind=kLoop, calls=%fused_computation.120 | loop fusion | bytes 3145728 | tf_op jit(solution)/shard_map/slice | solution.py:92
  64.2 0.1 reshape.110
  64.3 0.1 reshape.109
  64.4 0.1 reshape.108
  64.6 0.5 fusion.80
  65.1 0.0 slice-start.4
  65.2 0.0 slice-start.5
  65.2 5.1 %fusion.8 = f32[192,896]{1,0:T(8,128)S(1)} fusion(bf16[192,4096]{1,0:T(8,128)(2,1)S(1)} %constant_dynamic-update-slice_fusion, bf16[1,4096,896]{2,1,0:T(8,128)(2,1)} %param.13), kind=kOutput, calls=%fused_computation.8 | convolution fusion | flops 1409286144 | bytes 9601024 | tf_op jit(solution)/shard_map/dot_general | solution.py:42
  70.3 0.1 slice-done.5
  70.4 1.8 fusion.12
  72.3 2.3 %convolution_convert_fusion.1 = bf16[64,4096]{1,0:T(8,128)(2,1)S(1)} fusion(bf16[16,20,4096]{2,1,0:T(8,128)(2,1)} %all-gather.4.cloned.1.call-done, s32[64]{0:T(128)S(1)} %add.101), kind=kOutput, calls=%fused_computation.21 | convolution fusion | flops 67379200 | bytes 1573120 | tf_op jit(solution)/shard_map/dot_general | solution.py:97
  74.6 0.0 slice-start.3
  74.6 2.4 %multiply_convert_fusion.2 = (bf16[64,896]{1,0:T(8,128)(2,1)S(1)}, bf16[64,896]{1,0:T(8,128)(2,1)S(1)}, bf16[64,896]{1,0:T(8,128)(2,1)S(1)}) fusion(f32[192,896]{1,0:T(8,128)S(1)} %fusion.8, f32[192,896]{1,0:T(8,128)S(1)} %fusion.12, bf16[64,4096]{1,0:T(8,128)(2,1)S(1)} %convolution_convert_fusion.1, bf16[1,896,4096]{2,1,0:T(8,128)(2,1)S(1)} %bitcast.90), kind=kOutput, calls=%fused_computation.58 | convolution fusion | flops 470622208 | bytes 8667136 | tf_op jit(solution)/shard_map/dot_general | solution.py:46
  77.0 0.3 fusion.31
  77.2 0.3 fusion.30
  77.6 1.5 collective-permute-start.3
  79.1 2.3 %fusion.6 = f32[64,4096]{1,0:T(8,128)S(1)} fusion(bf16[64,896]{1,0:T(8,128)(2,1)S(1)} %get-tuple-element.10, bf16[1,4096,896]{2,1,0:T(8,128)(2,1)S(1)} %bitcast.92), kind=kOutput, calls=%fused_computation.6 | convolution fusion | flops 469762048 | bytes 8503296 | tf_op jit(solution)/shard_map/dot_general | solution.py:46
  81.4 3.9 %collective-permute-done.3 = bf16[2,64,896]{2,1,0:T(8,128)(2,1)S(1)} collective-permute-done((bf16[2,64,896]{2,1,0:T(8,128)(2,1)S(1)}, bf16[2,64,896]{2,1,0:T(8,128)(2,1)S(1)}, u32[]{:S(2)}, u32[]{:S(2)}) %collective-permute-start.3) | collective-permute-done | bytes 229408 | tf_op jit(solution)/shard_map/ppermute | solution.py:15
  85.4 0.1 fusion.42
  85.5 1.5 collective-permute-start.4
  87.0 2.3 %fusion.27 = bf16[64,4096]{1,0:T(8,128)(2,1)S(1)} fusion(f32[64,4096]{1,0:T(8,128)S(1)} %fusion.6, bf16[64,896]{1,0:T(8,128)(2,1)S(1)} %get-tuple-element.9, bf16[1,4096,896]{2,1,0:T(8,128)(2,1)S(1)} %bitcast.94), kind=kOutput, calls=%fused_computation.20 | convolution fusion | flops 470286336 | bytes 9027584 | tf_op jit(solution)/shard_map/dot_general | solution.py:46
  89.4 1.0 reshape.113
  90.4 0.2 subtract_convert_fusion
  90.6 0.5 fusion.35
  91.1 4.6 %fusion.20 = bf16[128,4096]{1,0:T(8,128)(2,1)S(1)} fusion(f32[128,4096]{1,0:T(8,128)S(1)} %fusion.35, bf16[1,896,4096]{2,1,0:T(8,128)(2,1)} %param.14, bf16[64,896]{1,0:T(8,128)(2,1)S(1)} %collective-permute-done.4, bf16[64,896]{1,0:T(8,128)(2,1)S(1)} %fusion.42), kind=kOutput, calls=%fused_computation.16 | convolution fusion | flops 941555712 | bytes 10715136 | tf_op jit(solution)/shard_map/dot_general | solution.py:42
  95.6 0.4 reshape.114
  96.1 0.6 copy.15
  96.7 1.6 copy.16
  98.2 4.3 %all-to-all-start.1 = ((bf16[16,8,4096]{2,1,0:T(8,128)(2,1)}), bf16[16,8,4096]{2,1,0:T(8,128)(2,1)S(1)}, u32[]{:S(2)}, u32[]{:S(2)}) async-start(bf16[16,8,4096]{2,1,0:T(8,128)(2,1)} %copy.16), calls=%async_computation.1 | async-start | bytes 2097152 | tf_op jit(solution)/shard_map/all_to_all | solution.py:62
  102.5 4.5 %fusion.4 = f32[64,4096]{1,0:T(8,128)S(1)} fusion(bf16[64,896]{1,0:T(8,128)(2,1)S(1)} %get-tuple-element.8, bf16[1,896,4096]{2,1,0:T(8,128)(2,1)} %param.14), kind=kOutput, calls=%fused_computation.4 | convolution fusion | flops 469762048 | bytes 8503296 | tf_op jit(solution)/shard_map/dot_general | solution.py:42
  107.1 0.4 fusion.23
  107.5 0.6 copy-done.1
  108.1 1.6 pad_maximum_fusion
  109.7 18.0 %all-to-all-done.1 = bf16[16,8,4096]{2,1,0:T(8,128)(2,1)S(1)} async-done(((bf16[16,8,4096]{2,1,0:T(8,128)(2,1)}), bf16[16,8,4096]{2,1,0:T(8,128)(2,1)S(1)}, u32[]{:S(2)}, u32[]{:S(2)}) %all-to-all-start.1) | async-done | bytes 1048608 | tf_op jit(solution)/shard_map/all_to_all | solution.py:62
  127.7 4.6 %all-to-all-start = ((bf16[16,12,4096]{2,1,0:T(8,128)(2,1)}), bf16[16,12,4096]{2,1,0:T(8,128)(2,1)S(1)}, u32[]{:S(2)}, u32[]{:S(2)}) async-start(bf16[16,12,4096]{2,1,0:T(8,128)(2,1)} %pad_maximum_fusion), calls=%async_computation | async-start | bytes 4194304 | tf_op jit(solution)/shard_map/all_to_all | solution.py:62
  132.3 0.1 convert_reduce_fusion.1
  132.5 1.5 collective-permute-start.5
  134.0 2.8 %collective-permute-done.5 = f32[4,4096]{1,0:T(4,128)S(1)} collective-permute-done((f32[4,4096]{1,0:T(4,128)S(1)}, f32[4,4096]{1,0:T(4,128)S(1)}, u32[]{:S(2)}, u32[]{:S(2)}) %collective-permute-start.5) | collective-permute-done | bytes 65568 | tf_op jit(solution)/shard_map/ppermute | solution.py:15
  136.8 0.6 fusion.65
  137.4 42.5 %all-to-all-done = bf16[16,12,4096]{2,1,0:T(8,128)(2,1)S(1)} async-done(((bf16[16,12,4096]{2,1,0:T(8,128)(2,1)}), bf16[16,12,4096]{2,1,0:T(8,128)(2,1)S(1)}, u32[]{:S(2)}, u32[]{:S(2)}) %all-to-all-start) | async-done | bytes 1572896 | tf_op jit(solution)/shard_map/all_to_all | solution.py:62
  179.9 0.4 convert_reduce_fusion
  180.3 0.1 fusion.64
  180.5 1.5 collective-permute-start.2
  182.0 1.6 fusion.71
  183.6 1.3 collective-permute-done.2
  184.8 0.6 copy.21
  (36 shorter events, 0.3 us)
Async XLA Ops:
  7.2 54.3 %all-gather.4.cloned.1.call-start = ((), (), s32[]{:S(2)}) async-start(), calls=%async_computation.2 | async-start | bytes 3342336 | tf_op jit(solution)/shard_map/all_gather | solution.py:87
  7.2 8.3 %collective-permute-start.1 = (bf16[8,4096]{1,0:T(8,128)(2,1)}, bf16[8,4096]{1,0:T(8,128)(2,1)S(1)}, u32[]{:S(2)}, u32[]{:S(2)}) collective-permute-start(bf16[8,4096]{1,0:T(8,128)(2,1)} %bitcast.102), channel_id=1, source_target_pairs={{0,16},{16,0},{1,17},{17,1},{2,18},{18,2},{3,19},{19,3},{4,20},{20... | collective-permute-start | bytes 196616 | tf_op jit(solution)/shard_map/ppermute | solution.py:15
  11.5 4.0 %collective-permute-start = (bf16[4,4096]{1,0:T(4,128)(2,1)S(1)}, bf16[4,4096]{1,0:T(4,128)(2,1)S(1)}, u32[]{:S(2)}, u32[]{:S(2)}) collective-permute-start(bf16[4,4096]{1,0:T(4,128)(2,1)S(1)} %get-tuple-element.14), channel_id=1, source_target_pairs={{0,16},{16,0},{1,17},{17,1},{2,18},{18,2},{3,19},{19,3},{4,20},{20... | collective-permute-start | bytes 98312 | tf_op jit(solution)/shard_map/ppermute | solution.py:15
  65.1 5.2 %slice-start.4 = ((s8[7340032]{0:T(1024)(128)(4,1)}), s8[4194304]{0:T(1024)(128)(4,1)S(1)}, s32[]{:S(2)}) async-start(s8[7340032]{0:T(1024)(128)(4,1)} %bitcast.93), calls=%async_computation.7 | async-start | bytes 8388608
  65.2 5.2 %slice-start.5 = ((s8[7340032]{0:T(1024)(128)(4,1)}), s8[3145728]{0:T(1024)(128)(4,1)S(1)}, s32[]{:S(2)}) async-start(s8[7340032]{0:T(1024)(128)(4,1)} %bitcast.93), calls=%async_computation.8 | async-start | bytes 6291456
  65.2 9.3 %slice-start = ((s8[7340032]{0:T(1024)(128)(4,1)}), s8[4194304]{0:T(1024)(128)(4,1)S(1)}, s32[]{:S(2)}) async-start(s8[7340032]{0:T(1024)(128)(4,1)} %bitcast.89), calls=%async_computation.3 | async-start | bytes 8388608
  70.4 4.1 %slice-start.1 = ((s8[7340032]{0:T(1024)(128)(4,1)}), s8[3145728]{0:T(1024)(128)(4,1)S(1)}, s32[]{:S(2)}) async-start(s8[7340032]{0:T(1024)(128)(4,1)} %bitcast.89), calls=%async_computation.4 | async-start | bytes 6291456
  72.2 6.8 %slice-start.2 = ((s8[7340032]{0:T(1024)(128)(4,1)}), s8[4194304]{0:T(1024)(128)(4,1)S(1)}, s32[]{:S(2)}) async-start(s8[7340032]{0:T(1024)(128)(4,1)} %bitcast.91), calls=%async_computation.5 | async-start | bytes 8388608
  74.6 16.0 %copy-start = (bf16[64,4096]{1,0:T(8,128)(2,1)}, bf16[64,4096]{1,0:T(8,128)(2,1)S(1)}, u32[]{:S(2)}) copy-start(bf16[64,4096]{1,0:T(8,128)(2,1)S(1)} %convolution_convert_fusion.1) | copy-start | bytes 1572868
  74.6 4.5 %slice-start.3 = ((s8[7340032]{0:T(1024)(128)(4,1)}), s8[3145728]{0:T(1024)(128)(4,1)S(1)}, s32[]{:S(2)}) async-start(s8[7340032]{0:T(1024)(128)(4,1)} %bitcast.91), calls=%async_computation.6 | async-start | bytes 6291456
  77.6 7.8 %collective-permute-start.3 = (bf16[2,64,896]{2,1,0:T(8,128)(2,1)S(1)}, bf16[2,64,896]{2,1,0:T(8,128)(2,1)S(1)}, u32[]{:S(2)}, u32[]{:S(2)}) collective-permute-start(bf16[2,64,896]{2,1,0:T(8,128)(2,1)S(1)} %pad_maximum_fusion.1), channel_id=1, source_target_pairs={{0,16},{16,0},{1,17},{17,1},{2,18},{18,2},{3,19},{19,3},{4,20},{20... | collective-permute-start | bytes 688136 | tf_op jit(solution)/shard_map/ppermute | solution.py:15
  85.5 4.9 %collective-permute-start.4 = (bf16[64,896]{1,0:T(8,128)(2,1)S(1)}, bf16[64,896]{1,0:T(8,128)(2,1)S(1)}, u32[]{:S(2)}, u32[]{:S(2)}) collective-permute-start(bf16[64,896]{1,0:T(8,128)(2,1)S(1)} %fusion.42), channel_id=1, source_target_pairs={{0,16},{16,0},{1,17},{17,1},{2,18},{18,2},{3,19},{19,3},{4,20},{20... | collective-permute-start | bytes 344072 | tf_op jit(solution)/shard_map/ppermute | solution.py:15
  98.2 29.5 %all-to-all-start.1 = ((bf16[16,8,4096]{2,1,0:T(8,128)(2,1)}), bf16[16,8,4096]{2,1,0:T(8,128)(2,1)S(1)}, u32[]{:S(2)}, u32[]{:S(2)}) async-start(bf16[16,8,4096]{2,1,0:T(8,128)(2,1)} %copy.16), calls=%async_computation.1 | async-start | bytes 2097152 | tf_op jit(solution)/shard_map/all_to_all | solution.py:62
  102.5 4.5 %copy-start.2 = (bf16[1,4,4096]{2,1,0:T(4,128)(2,1)S(1)}, bf16[1,4,4096]{2,1,0:T(4,128)(2,1)}, u32[]{:S(2)}) copy-start(bf16[1,4,4096]{2,1,0:T(4,128)(2,1)} %param.8) | copy-start | bytes 98308
  107.0 1.0 copy-start.1
  109.7 27.1 %copy-start.3 = (bf16[1,4,4096]{2,1,0:T(4,128)(2,1)S(1)}, bf16[1,4,4096]{2,1,0:T(4,128)(2,1)}, u32[]{:S(2)}) copy-start(bf16[1,4,4096]{2,1,0:T(4,128)(2,1)} %param.9) | copy-start | bytes 98308
  127.7 52.3 %all-to-all-start = ((bf16[16,12,4096]{2,1,0:T(8,128)(2,1)}), bf16[16,12,4096]{2,1,0:T(8,128)(2,1)S(1)}, u32[]{:S(2)}, u32[]{:S(2)}) async-start(bf16[16,12,4096]{2,1,0:T(8,128)(2,1)} %pad_maximum_fusion), calls=%async_computation | async-start | bytes 4194304 | tf_op jit(solution)/shard_map/all_to_all | solution.py:62
  132.3 48.0 %copy-start.4 = (f32[1,4096]{1,0:T(1,128)S(1)}, f32[1,4096]{1,0:T(1,128)}, u32[]{:S(2)}) copy-start(f32[1,4096]{1,0:T(1,128)} %param.11) | copy-start | bytes 49156
  132.5 4.3 %collective-permute-start.5 = (f32[4,4096]{1,0:T(4,128)S(1)}, f32[4,4096]{1,0:T(4,128)S(1)}, u32[]{:S(2)}, u32[]{:S(2)}) collective-permute-start(f32[4,4096]{1,0:T(4,128)S(1)} %slice.92), channel_id=1, source_target_pairs={{0,16},{16,0},{1,17},{17,1},{2,18},{18,2},{3,19},{19,3},{4,20},{20... | collective-permute-start | bytes 196616 | tf_op jit(solution)/shard_map/ppermute | solution.py:15
  180.5 4.3 %collective-permute-start.2 = (bf16[8,4096]{1,0:T(8,128)(2,1)S(1)}, bf16[8,4096]{1,0:T(8,128)(2,1)S(1)}, u32[]{:S(2)}, u32[]{:S(2)}) collective-permute-start(bf16[8,4096]{1,0:T(8,128)(2,1)S(1)} %slice.140), channel_id=1, source_target_pairs={{0,16},{16,0},{1,17},{17,1},{2,18},{18,2},{3,19},{19,3},{4,20},{20... | collective-permute-start | bytes 196616 | tf_op jit(solution)/shard_map/ppermute | solution.py:15
Sparse Core Ops, SparseCore 0:
  16.4 45.0 all-gather.3

commit v2 on v1

--- a/solution.py
+++ b/solution.py
@@ -1,6 +1,10 @@
+import functools
+
 import jax
 import jax.numpy as jnp
 from jax import lax
+from jax.experimental import pallas as pl
+from jax.experimental.pallas import tpu as pltpu
 from jax.sharding import PartitionSpec as P
 
 BLK = 2
@@ -8,6 +12,190 @@
 step_rate = 0.5
 F32 = jnp.float32
 BF16 = jnp.bfloat16
+
+
+QUARTERS = 4
+CORES = 2
+DEPTH_Z = 4
+
+
+def place(ny):
+    me = lax.axis_index("rep")
+
+    def index(z, y, core):
+        return (z * ny + y) * CORES + core
+
+    return me // (CORES * ny), (me // CORES) % ny, me % CORES, index
+
+
+def greet(ny, z, y, core, index):
+    barrier = pltpu.get_barrier_semaphore()
+    peers = [index((z + d) % DEPTH_Z, y, core) for d in range(1, DEPTH_Z)]
+    peers += [index(z, (y + d) % ny, core) for d in range(1, ny)]
+    peers += [index(z, y, 1 - core)]
+    for peer in peers:
+        pl.semaphore_signal(
+            barrier, inc=1, device_id={"rep": peer}, device_id_type=pl.DeviceIdType.MESH
+        )
+    pl.semaphore_wait(barrier, len(peers))
+
+
+def remote(src, dst, send, recv, peer):
+    return pltpu.make_async_remote_copy(
+        src_ref=src,
+        dst_ref=dst,
+        send_sem=send,
+        recv_sem=recv,
+        device_id={"rep": peer},
+        device_id_type=pl.DeviceIdType.MESH,
+    )
+
+
+def gather_kernel(ny, x_ref, out_ref, send, recv):
+    z, y, core, index = place(ny)
+    greet(ny, z, y, core, index)
+    me = index(z, y, core)
+    sibling = index(z, y, 1 - core)
+    out_ref[me] = x_ref[...]
+    started = []
+
+    def push(shard, peer):
+        copy = remote(
+            out_ref.at[shard], out_ref.at[shard], send.at[len(started)], recv.at[shard], peer
+        )
+        copy.start()
+        started.append(copy)
+
+    def arrive(shard):
+        remote(
+            out_ref.at[shard], out_ref.at[shard], send.at[0], recv.at[shard], sibling
+        ).wait_recv()
+
+    z_order = [1, DEPTH_Z - 1] + list(range(2, DEPTH_Z - 1))
+    for dz in z_order:
+        push(me, index((z + dz) % DEPTH_Z, y, core))
+    for dz in [0] + z_order:
+        shard = index((z + dz) % DEPTH_Z, y, core)
+        if dz:
+            arrive(shard)
+        for dy in range(1, ny):
+            push(shard, index(z, (y + dy) % ny, core))
+        push(shard, sibling)
+    for dz in [0] + z_order:
+        for dy in range(1, ny):
+            shard = index((z + dz) % DEPTH_Z, (y + dy) % ny, core)
+            arrive(shard)
+            push(shard, sibling)
+    for dz in [0] + z_order:
+        for dy in range(ny):
+            arrive(index((z + dz) % DEPTH_Z, (y + dy) % ny, 1 - core))
+    for copy in started:
+        copy.wait_send()
+
+
+def gather_shards(shard):
+    replicas = lax.axis_size("rep")
+    ny = replicas // (CORES * DEPTH_Z)
+    copies = DEPTH_Z - 1 + DEPTH_Z * ny + DEPTH_Z * (ny - 1)
+    return pl.pallas_call(
+        functools.partial(gather_kernel, ny),
+        out_shape=jax.ShapeDtypeStruct((replicas,) + shard.shape, shard.dtype),
+        in_specs=[pl.BlockSpec(memory_space=pltpu.VMEM)],
+        out_specs=pl.BlockSpec(memory_space=pltpu.VMEM),
+        scratch_shapes=[
+            pltpu.SemaphoreType.DMA((copies,)),
+            pltpu.SemaphoreType.DMA((replicas,)),
+        ],
+        compiler_params=pltpu.CompilerParams(
+            collective_id=0, has_side_effects=True, vmem_limit_bytes=32 * 2**20
+        ),
+    )(shard)
+
+
+def sum_kernel(
+    ny, t_ref, out_ref, from_core, part, from_y, summed, from_z, send, recv_core, recv_y, recv_z
+):
+    z, y, core, index = place(ny)
+    greet(ny, z, y, core, index)
+    sibling = index(z, y, 1 - core)
+    started = []
+
+    def push(src, dst, recv, peer):
+        copy = remote(src, dst, send.at[len(started)], recv, peer)
+        copy.start()
+        started.append(copy)
+        return copy
+
+    y_order = list(range(1, ny)) + [0]
+    z_order = list(range(2, DEPTH_Z - 1)) + [1, DEPTH_Z - 1, 0]
+    core_copies = {}
+    for dy in y_order:
+        yy = (y + dy) % ny
+        core_copies[dy] = push(
+            t_ref.at[1 - core, yy], from_core.at[yy], recv_core.at[dy], sibling
+        )
+    y_copies = []
+    for dy in y_order[:-1]:
+        yy = (y + dy) % ny
+        core_copies[dy].wait_recv()
+        part[dy - 1] = (t_ref[core, yy].astype(F32) + from_core[yy].astype(F32)).astype(BF16)
+        y_copies.append(
+            push(part.at[dy - 1], from_y.at[dy - 1], recv_y.at[dy - 1], index(z, yy, core))
+        )
+    core_copies[0].wait_recv()
+    for copy in y_copies:
+        copy.wait_recv()
+    z_copies = []
+    total = None
+    for dz in z_order:
+        zz = (z + dz) % DEPTH_Z
+        total = t_ref[core, y, zz].astype(F32) + from_core[y, zz].astype(F32)
+        for dy in range(1, ny):
+            total = total + from_y[dy - 1, zz].astype(F32)
+        if dz:
+            summed[dz - 1] = total.astype(BF16)
+            z_copies.append(
+                push(
+                    summed.at[dz - 1], from_z.at[dz - 1], recv_z.at[dz - 1], index(zz, y, core)
+                )
+            )
+    out_ref[...] = total
+    for dz, copy in zip(z_order, z_copies):
+        copy.wait_recv()
+        out_ref[...] += from_z[dz - 1].astype(F32)
+    for copy in started:
+        copy.wait_send()
+
+
+def sum_shards(terms, collective_id):
+    replicas, rows, features = terms.shape
+    ny = replicas // (CORES * DEPTH_Z)
+    width = features // QUARTERS
+    tall = rows * QUARTERS
+    laid = terms.reshape(DEPTH_Z, ny, CORES, rows, QUARTERS, width)
+    laid = laid.transpose(2, 1, 0, 4, 3, 5).reshape(CORES, ny, DEPTH_Z, tall, width)
+    copies = ny + ny - 1 + DEPTH_Z - 1
+    total = pl.pallas_call(
+        functools.partial(sum_kernel, ny),
+        out_shape=jax.ShapeDtypeStruct((tall, width), F32),
+        in_specs=[pl.BlockSpec(memory_space=pltpu.VMEM)],
+        out_specs=pl.BlockSpec(memory_space=pltpu.VMEM),
+        scratch_shapes=[
+            pltpu.VMEM((ny, DEPTH_Z, tall, width), BF16),
+            pltpu.VMEM((ny - 1, DEPTH_Z, tall, width), BF16),
+            pltpu.VMEM((ny - 1, DEPTH_Z, tall, width), BF16),
+            pltpu.VMEM((DEPTH_Z - 1, tall, width), BF16),
+            pltpu.VMEM((DEPTH_Z - 1, tall, width), BF16),
+            pltpu.SemaphoreType.DMA((copies,)),
+            pltpu.SemaphoreType.DMA((ny,)),
+            pltpu.SemaphoreType.DMA((ny - 1,)),
+            pltpu.SemaphoreType.DMA((DEPTH_Z - 1,)),
+        ],
+        compiler_params=pltpu.CompilerParams(
+            collective_id=collective_id, has_side_effects=True, vmem_limit_bytes=32 * 2**20
+        ),
+    )(laid)
+    return total.reshape(QUARTERS, rows, width).transpose(1, 0, 2).reshape(rows, features)
 
 
 def passed_along(value, by):
@@ -56,11 +244,6 @@
     high = coefs.astype(BF16)
     low = (coefs - high.astype(F32)).astype(BF16)
     return mm(jnp.concatenate((high, low), 1), jnp.concatenate((factors, factors), 0))
-
-
-def scatter_terms(terms):
-    got = lax.all_to_all(terms, "rep", split_axis=0, concat_axis=0, tiled=True)
-    return jnp.sum(got.astype(F32), axis=0)
 
 
 def per_device(layer_in, next_in, returned, norm_gain, gate_weight, up_weight, down_weight, wiring):
@@ -84,7 +267,12 @@
     packed = jnp.concatenate((normed_own, next_own, next_mate, later), 0)
     target = route_select(wiring[0], replicas, blocks_dev, capacity)
     select = row_one_hot(target, replicas * capacity)
-    everything = lax.all_gather(packed, "rep", axis=0, tiled=False)
+    groups = packed.shape[0] // rows
+    width = features // QUARTERS
+    shard = packed.reshape(groups, rows, QUARTERS, width).transpose(0, 2, 1, 3)
+    everything = gather_shards(shard.reshape(groups * QUARTERS * rows, width))
+    everything = everything.reshape(replicas, groups, QUARTERS, rows, width)
+    everything = everything.transpose(0, 1, 3, 2, 4).reshape(replicas, groups * rows, features)
     normed = everything[:, :rows].reshape(tokens, features)
     nexts = jnp.concatenate(
         (
@@ -120,14 +308,15 @@
     own = lax.dynamic_slice_in_dim(term, position * rows, rows, 0) + values
     term = lax.dynamic_update_slice_in_dim(term, own, position * rows, 0).astype(BF16)
     slot_term = mm(select, term).astype(BF16)
-    first = scatter_terms(
+    first = sum_shards(
         jnp.concatenate(
             (
                 slot_term.reshape(replicas, slot_rows, features),
                 dterm.reshape(replicas, rows, features),
             ),
             1,
-        )
+        ),
+        1,
     )
 
     gate_next = next_gate[:tokens] + from_mate[0]
@@ -138,7 +327,7 @@
     down_coefs = factor * mm_t(hidden_both, hidden)
     term_next = (0.5 * (mm(hidden_both, down) - low_rank(down_coefs, cotangent))).astype(BF16)
     term_next = term_next.reshape(2, replicas, rows, features).transpose(1, 0, 2, 3)
-    second = scatter_terms(term_next.reshape(replicas, 2 * rows, features))
+    second = sum_shards(term_next.reshape(replicas, 2 * rows, features), 2)
     mate_sum = passed_along(second[rows:], partner_offset)
     next_out = (second[:rows] + mate_sum + next_values).astype(BF16)
 

time: 193 us -> 138 us (0.72)
  the two profiles are of different devices: /device:TPU:16 before, /device:TPU:0 now
where the time goes in v2:
time: 138 us
  Pallas kernels  65.8 us (48%)
  matrix products  23 us (17%)
  local copies, waits for them, and re-layouts  22.9 us (17%)
  other arithmetic  9.73 us (7%)
  waiting for transfers between devices  8.23 us (6%)
  starting transfers between devices  6.88 us (5%)
    pallas_call x2, Pallas kernels, sum_shards(): pl.pallas_call(functools.partial(sum_kernel, ny), out_shape=jax.ShapeDtyp...  41.6 us
    pallas_call x1, Pallas kernels, gather_shards(): pl.pallas_call(functools.partial(gather_kernel, ny), out_shape=jax.ShapeD...  24.2 us
    dot_general x8, matrix products, mm(): return jnp.dot(a, b, preferred_element_type=F32)  14.2 us
    ppermute x6, waiting for transfers between devices, passed_along(): lax.ppermute(value, 'section', [(i, (i + by) % peers) for i in range(peer...  8.23 us
    dot_general x5, matrix products, mm_t(): lax.dot_general(a, b, (((1,), (1,)), ((), ())), preferred_element_type=F32)  7.98 us
    reshape x2, local copies, waits for them, and re-layouts, per_device(): everything = everything.reshape(replicas, groups, QUARTERS, rows, width)  7.63 us
    ppermute x6, starting transfers between devices, passed_along(): lax.ppermute(value, 'section', [(i, (i + by) % peers) for i in range(peer...  6.88 us
    reshape x1, local copies, waits for them, and re-layouts, per_device(): everything.transpose(0, 1, 3, 2, 4)  4.46 us
  transfers between devices with their start and end apart: 6, of which 3 were waited for; matrix products, arithmetic and copies ran while one was open for 15% of the time, Pallas kernels for 30%

profile of v2, /device:TPU:0, one launch (start us, length us, event | category | flops | bytes accessed | tf_op | source)
XLA Modules:
  0.0 137.7 jit_solution(18193456583143734747)
XLA Ops:
  0.6 0.9 fusion.54
  1.5 0.9 fusion.58
  2.5 0.9 fusion.60
  3.4 3.0 %collective-permute-start = (bf16[4,4096]{1,0:T(4,128)(2,1)S(1)}, bf16[4,4096]{1,0:T(4,128)(2,1)S(1)}, u32[]{:S(2)}, u32[]{:S(2)}) collective-permute-start(bf16[4,4096]{1,0:T(4,128)(2,1)S(1)} %get-tuple-element.16), channel_id=1, source_target_pairs={{0,16},{16,0},{1,17},{17,1},{2,18},{18,2},{3,19},{19,3},{4,20},{20... | collective-permute-start | bytes 98312 | tf_op jit(solution)/shard_map/ppermute | solution.py:203
  6.4 0.9 reduce_window_sum.22
  7.3 0.7 reduce_window_sum.23
  8.0 0.7 bitcast_subtract_fusion.1
  8.7 0.1 select_reduce_fusion
  9.1 0.1 add.101
  9.2 1.6 %collective-permute-done.1 = bf16[8,4096]{1,0:T(8,128)(2,1)S(1)} collective-permute-done((bf16[8,4096]{1,0:T(8,128)(2,1)}, bf16[8,4096]{1,0:T(8,128)(2,1)S(1)}, u32[]{:S(2)}, u32[]{:S(2)}) %collective-permute-start.1) | collective-permute-done | bytes 65568 | tf_op jit(solution)/shard_map/ppermute | solution.py:203
  10.9 0.1 reshape.137
  11.2 24.2 %shard_map.103 = bf16[16,80,1024]{2,1,0:T(8,128)(2,1)S(1)} custom-call(bf16[80,1024]{1,0:T(8,128)(2,1)S(1)} %reshape.138.x_ref), custom_call_target="tpu_custom_call" | custom-call | tf_op jit(solution)/shard_map/pallas_call | solution.py:100
  35.4 3.0 %reshape.139 = bf16[16,5,4,4,1024]{4,3,2,1,0:T(4,128)(2,1)} reshape(bf16[16,80,1024]{2,1,0:T(8,128)(2,1)S(1)} %shard_map.103) | data formatting | bytes 5242880 | tf_op jit(solution)/shard_map/reshape | solution.py:274
  38.4 4.6 %copy.52 = bf16[16,5,4,4,1024]{4,2,0,3,1:T(4,128)(2,1)} copy(bf16[16,5,4,4,1024]{4,3,2,1,0:T(4,128)(2,1)} %reshape.139) | data formatting | bytes 5242880 | tf_op jit(solution)/shard_map/reshape | solution.py:274
  43.0 4.5 %reshape.140 = bf16[16,20,4096]{2,0,1:T(8,128)(2,1)S(1)} reshape(bf16[16,5,4,4,1024]{4,3,0,2,1:T(4,128)(2,1)} %bitcast.117) | data formatting | bytes 5242880 | tf_op jit(solution)/shard_map/reshape | solution.py:275
  47.5 1.0 fusion.80
  48.5 0.6 copy-done
  49.1 0.4 copy.37
  49.5 0.1 reshape.143
  49.7 0.5 copy-done.1
  50.2 0.4 copy.36
  50.6 0.1 reshape.142
  50.7 0.4 copy.35
  51.1 0.1 reshape.141
  51.3 0.5 fusion.82
  51.9 5.2 %fusion.8 = f32[192,896]{1,0:T(8,128)S(1)} fusion(bf16[192,4096]{1,0:T(8,128)(2,1)S(1)} %constant_dynamic-update-slice_fusion, bf16[1,4096,896]{2,1,0:T(8,128)(2,1)} %param.13), kind=kOutput, calls=%fused_computation.8 | convolution fusion | flops 1409286144 | bytes 9601024 | tf_op jit(solution)/shard_map/dot_general | solution.py:230
  57.2 1.8 %fusion.12 = f32[192,896]{1,0:T(8,128)S(1)} fusion(bf16[192,4096]{1,0:T(8,128)(2,1)S(1)} %constant_dynamic-update-slice_fusion, bf16[1,4096,896]{2,1,0:T(8,128)(2,1)S(1)} %bitcast.121), kind=kOutput, calls=%fused_computation.12 | convolution fusion | flops 1409286144 | bytes 9601024 | tf_op jit(solution)/shard_map/dot_general | solution.py:230
  59.0 0.3 slice-done.2
  59.4 0.8 convolution_convert_fusion.1
  60.2 0.2 slice-done.1
  60.4 2.4 %multiply_convert_fusion.2 = (bf16[64,896]{1,0:T(8,128)(2,1)S(1)}, bf16[64,896]{1,0:T(8,128)(2,1)S(1)}, bf16[64,896]{1,0:T(8,128)(2,1)S(1)}) fusion(f32[192,896]{1,0:T(8,128)S(1)} %fusion.8, f32[192,896]{1,0:T(8,128)S(1)} %fusion.12, bf16[64,4096]{1,0:T(8,128)(2,1)S(1)} %convolution_convert_fusion.1, bf16[1,896,4096]{2,1,0:T(8,128)(2,1)S(1)} %bitcast.116), kind=kOutput, calls=%fused_computation.59 | convolution fusion | flops 470622208 | bytes 8667136 | tf_op jit(solution)/shard_map/dot_general | solution.py:234
  62.8 2.3 %fusion.6 = f32[64,4096]{1,0:T(8,128)S(1)} fusion(bf16[64,896]{1,0:T(8,128)(2,1)S(1)} %get-tuple-element.10, bf16[1,4096,896]{2,1,0:T(8,128)(2,1)S(1)} %bitcast.119), kind=kOutput, calls=%fused_computation.6 | convolution fusion | flops 469762048 | bytes 8503296 | tf_op jit(solution)/shard_map/dot_general | solution.py:234
  65.1 0.2 fusion.30
  65.4 0.3 fusion.29
  65.7 0.8 pad_maximum_fusion.1
  66.5 0.6 collective-permute-start.3
  67.1 1.4 %fusion.4 = f32[64,4096]{1,0:T(8,128)S(1)} fusion(bf16[64,896]{1,0:T(8,128)(2,1)S(1)} %get-tuple-element.8, bf16[1,896,4096]{2,1,0:T(8,128)(2,1)S(1)} %bitcast.116), kind=kOutput, calls=%fused_computation.4 | convolution fusion | flops 469762048 | bytes 8503296 | tf_op jit(solution)/shard_map/dot_general | solution.py:230
  68.6 0.4 convolution_convert_fusion
  69.0 0.9 copy.39
  69.9 2.6 %fusion.26 = bf16[64,4096]{1,0:T(8,128)(2,1)S(1)} fusion(f32[64,4096]{1,0:T(8,128)S(1)} %fusion.6, bf16[64,896]{1,0:T(8,128)(2,1)S(1)} %get-tuple-element.9, bf16[1,4096,896]{2,1,0:T(8,128)(2,1)S(1)} %bitcast.121), kind=kOutput, calls=%fused_computation.19 | convolution fusion | flops 470286336 | bytes 9027584 | tf_op jit(solution)/shard_map/dot_general | solution.py:234
  72.5 0.4 concatenate.40
  72.9 0.4 copy.40
  73.3 1.0 pad_maximum_fusion
  74.3 0.5 copy.41.t_ref
  74.8 23.3 %shard_map.104 = f32[48,1024]{1,0:T(8,128)S(1)} custom-call(bf16[2,2,4,48,1024]{4,3,2,1,0:T(8,128)(2,1)S(1)} %copy.41.t_ref), custom_call_target="tpu_custom_call" | custom-call | tf_op jit(solution)/shard_map/pallas_call | solution.py:178
  98.2 0.6 slice.139
  98.9 1.4 %collective-permute-start.2 = (bf16[8,4096]{1,0:T(8,128)(2,1)}, bf16[8,4096]{1,0:T(8,128)(2,1)S(1)}, u32[]{:S(2)}, u32[]{:S(2)}) collective-permute-start(bf16[8,4096]{1,0:T(8,128)(2,1)} %bitcast.17), channel_id=1, source_target_pairs={{0,16},{16,0},{1,17},{17,1},{2,18},{18,2},{3,19},{19,3},{4,20},{20... | collective-permute-start | bytes 196616 | tf_op jit(solution)/shard_map/ppermute | solution.py:203
  100.3 0.1 fusion.65
  100.4 1.0 convert_element_type.103
  101.5 0.7 collective-permute-start.4
  102.2 4.2 %collective-permute-done.4 = bf16[64,896]{1,0:T(8,128)(2,1)S(1)} collective-permute-done((bf16[64,896]{1,0:T(8,128)(2,1)S(1)}, bf16[64,896]{1,0:T(8,128)(2,1)S(1)}, u32[]{:S(2)}, u32[]{:S(2)}) %collective-permute-start.4) | collective-permute-done | bytes 114720 | tf_op jit(solution)/shard_map/ppermute | solution.py:203
  106.3 0.2 subtract_convert_fusion
  106.5 0.5 fusion.34
  107.0 4.4 %fusion.20 = bf16[128,4096]{1,0:T(8,128)(2,1)S(1)} fusion(f32[128,4096]{1,0:T(8,128)S(1)} %fusion.34, bf16[1,896,4096]{2,1,0:T(8,128)(2,1)} %param.14, bf16[64,896]{1,0:T(8,128)(2,1)S(1)} %collective-permute-done.4, bf16[64,896]{1,0:T(8,128)(2,1)S(1)} %fusion.43), kind=kOutput, calls=%fused_computation.16 | convolution fusion | flops 941555712 | bytes 10715136 | tf_op jit(solution)/shard_map/dot_general | solution.py:230
  111.4 0.4 reshape.147
  111.8 0.6 copy.54
  112.4 0.8 reshape_reshape.3
  113.2 0.6 copy.53
  113.8 18.2 %shard_map.105 = f32[32,1024]{1,0:T(8,128)S(1)} custom-call(bf16[2,2,4,32,1024]{4,3,2,1,0:T(8,128)(2,1)S(1)} %bitcast.113), custom_call_target="tpu_custom_call" | custom-call | tf_op jit(solution)/shard_map/pallas_call | solution.py:178
  132.1 1.1 collective-permute-start.5
  133.2 0.7 fusion.72
  134.0 2.5 %collective-permute-done.5 = f32[4,4096]{1,0:T(4,128)S(1)} collective-permute-done((f32[4,4096]{1,0:T(4,128)S(1)}, f32[4,4096]{1,0:T(4,128)S(1)}, u32[]{:S(2)}, u32[]{:S(2)}) %collective-permute-start.5) | collective-permute-done | bytes 65568 | tf_op jit(solution)/shard_map/ppermute | solution.py:203
  136.4 0.6 fusion.66
  137.1 0.6 copy.60
  (51 shorter events, 1.0 us)
Async XLA Ops:
  3.4 5.9 %collective-permute-start = (bf16[4,4096]{1,0:T(4,128)(2,1)S(1)}, bf16[4,4096]{1,0:T(4,128)(2,1)S(1)}, u32[]{:S(2)}, u32[]{:S(2)}) collective-permute-start(bf16[4,4096]{1,0:T(4,128)(2,1)S(1)} %get-tuple-element.16), channel_id=1, source_target_pairs={{0,16},{16,0},{1,17},{17,1},{2,18},{18,2},{3,19},{19,3},{4,20},{20... | collective-permute-start | bytes 98312 | tf_op jit(solution)/shard_map/ppermute | solution.py:203
  6.4 4.5 %collective-permute-start.1 = (bf16[8,4096]{1,0:T(8,128)(2,1)}, bf16[8,4096]{1,0:T(8,128)(2,1)S(1)}, u32[]{:S(2)}, u32[]{:S(2)}) collective-permute-start(bf16[8,4096]{1,0:T(8,128)(2,1)} %bitcast.139), channel_id=1, source_target_pairs={{0,16},{16,0},{1,17},{17,1},{2,18},{18,2},{3,19},{19,3},{4,20},{20... | collective-permute-start | bytes 196616 | tf_op jit(solution)/shard_map/ppermute | solution.py:203
  47.5 1.6 %copy-start = (bf16[16,20,4096]{2,0,1:T(8,128)(2,1)}, bf16[16,20,4096]{2,0,1:T(8,128)(2,1)S(1)}, u32[]{:S(2)}) copy-start(bf16[16,20,4096]{2,0,1:T(8,128)(2,1)S(1)} %reshape.140) | copy-start | bytes 7864324
  49.1 1.0 copy-start.1
  51.3 5.9 %slice-start.5 = ((s8[7340032]{0:T(1024)(128)(4,1)}), s8[4194304]{0:T(1024)(128)(4,1)S(1)}, s32[]{:S(2)}) async-start(s8[7340032]{0:T(1024)(128)(4,1)} %bitcast.120), calls=%async_computation.5 | async-start | bytes 8388608
  51.9 5.3 %slice-start.6 = ((s8[7340032]{0:T(1024)(128)(4,1)}), s8[3145728]{0:T(1024)(128)(4,1)S(1)}, s32[]{:S(2)}) async-start(s8[7340032]{0:T(1024)(128)(4,1)} %bitcast.120), calls=%async_computation.6 | async-start | bytes 6291456
  51.9 8.3 %slice-start = ((s8[7340032]{0:T(1024)(128)(4,1)}), s8[4194304]{0:T(1024)(128)(4,1)S(1)}, s32[]{:S(2)}) async-start(s8[7340032]{0:T(1024)(128)(4,1)} %bitcast.115), calls=%async_computation | async-start | bytes 8388608
  51.9 10.8 %slice-start.3 = ((s8[7340032]{0:T(1024)(128)(4,1)}), s8[4194304]{0:T(1024)(128)(4,1)S(1)}, s32[]{:S(2)}) async-start(s8[7340032]{0:T(1024)(128)(4,1)} %bitcast.118), calls=%async_computation.3 | async-start | bytes 8388608
  57.2 2.2 %slice-start.2 = ((bf16[16,20,4096]{2,0,1:T(8,128)(2,1)}), bf16[16,8,4096]{2,0,1:T(8,128)(2,1)S(1)}, s32[]{:S(2)}) async-start(bf16[16,20,4096]{2,0,1:T(8,128)(2,1)} %copy-done), calls=%async_computation.2 | async-start | bytes 2097152 | tf_op jit(solution)/shard_map/slice | solution.py:284
  57.2 3.2 %slice-start.1 = ((s8[7340032]{0:T(1024)(128)(4,1)}), s8[3145728]{0:T(1024)(128)(4,1)S(1)}, s32[]{:S(2)}) async-start(s8[7340032]{0:T(1024)(128)(4,1)} %bitcast.115), calls=%async_computation.1 | async-start | bytes 6291456
  57.2 5.5 %slice-start.4 = ((s8[7340032]{0:T(1024)(128)(4,1)}), s8[3145728]{0:T(1024)(128)(4,1)S(1)}, s32[]{:S(2)}) async-start(s8[7340032]{0:T(1024)(128)(4,1)} %bitcast.118), calls=%async_computation.4 | async-start | bytes 6291456
  65.6 2.9 %copy-start.2 = (f32[128,896]{1,0:T(8,128)}, f32[128,896]{1,0:T(8,128)S(1)}, u32[]{:S(2)}) copy-start(f32[128,896]{1,0:T(8,128)S(1)} %fusion.29) | copy-start | bytes 1376260
  66.5 33.9 %collective-permute-start.3 = (bf16[2,64,896]{2,1,0:T(8,128)(2,1)}, bf16[2,64,896]{2,1,0:T(8,128)(2,1)}, u32[]{:S(2)}, u32[]{:S(2)}) collective-permute-start(bf16[2,64,896]{2,1,0:T(8,128)(2,1)} %pad_maximum_fusion.1), channel_id=1, source_target_pairs={{0,16},{16,0},{1,17},{17,1},{2,18},{18,2},{3,19},{19,3},{4,20},{20... | collective-permute-start | bytes 688136 | tf_op jit(solution)/shard_map/ppermute | solution.py:203
  67.1 1.5 %copy-start.4 = (bf16[1,4,4096]{2,1,0:T(4,128)(2,1)S(1)}, bf16[1,4,4096]{2,1,0:T(4,128)(2,1)}, u32[]{:S(2)}) copy-start(bf16[1,4,4096]{2,1,0:T(4,128)(2,1)} %param.8) | copy-start | bytes 98308
  74.3 25.9 %copy-start.6 = (f32[1,4096]{1,0:T(1,128)S(1)}, f32[1,4096]{1,0:T(1,128)}, u32[]{:S(2)}) copy-start(f32[1,4096]{1,0:T(1,128)} %param.11) | copy-start | bytes 49156
  74.8 26.6 %copy-start.3 = (f32[128,896]{1,0:T(8,128)S(1)}, f32[128,896]{1,0:T(8,128)}, u32[]{:S(2)}) copy-start(f32[128,896]{1,0:T(8,128)} %copy-done.2) | copy-start | bytes 1376260
  98.9 35.1 %collective-permute-start.2 = (bf16[8,4096]{1,0:T(8,128)(2,1)}, bf16[8,4096]{1,0:T(8,128)(2,1)S(1)}, u32[]{:S(2)}, u32[]{:S(2)}) collective-permute-start(bf16[8,4096]{1,0:T(8,128)(2,1)} %bitcast.17), channel_id=1, source_target_pairs={{0,16},{16,0},{1,17},{17,1},{2,18},{18,2},{3,19},{19,3},{4,20},{20... | collective-permute-start | bytes 196616 | tf_op jit(solution)/shard_map/ppermute | solution.py:203
  101.5 4.9 %collective-permute-start.4 = (bf16[64,896]{1,0:T(8,128)(2,1)S(1)}, bf16[64,896]{1,0:T(8,128)(2,1)S(1)}, u32[]{:S(2)}, u32[]{:S(2)}) collective-permute-start(bf16[64,896]{1,0:T(8,128)(2,1)S(1)} %fusion.43), channel_id=1, source_target_pairs={{0,16},{16,0},{1,17},{17,1},{2,18},{18,2},{3,19},{19,3},{4,20},{20... | collective-permute-start | bytes 344072 | tf_op jit(solution)/shard_map/ppermute | solution.py:203
  113.2 23.2 %copy-start.5 = (bf16[1,4,4096]{2,1,0:T(4,128)(2,1)S(1)}, bf16[1,4,4096]{2,1,0:T(4,128)(2,1)}, u32[]{:S(2)}) copy-start(bf16[1,4,4096]{2,1,0:T(4,128)(2,1)} %param.9) | copy-start | bytes 98308
  132.1 4.3 %collective-permute-start.5 = (f32[4,4096]{1,0:T(4,128)S(1)}, f32[4,4096]{1,0:T(4,128)S(1)}, u32[]{:S(2)}, u32[]{:S(2)}) collective-permute-start(f32[4,4096]{1,0:T(4,128)S(1)} %bitcast.138), channel_id=1, source_target_pairs={{0,16},{16,0},{1,17},{17,1},{2,18},{18,2},{3,19},{19,3},{4,20},{20... | collective-permute-start | bytes 196616 | tf_op jit(solution)/shard_map/ppermute | solution.py:203

commit v3 on v2

v3 whole, which is shorter than its diff:
```python
import functools

import jax
import jax.numpy as jnp
from jax import lax
from jax.experimental import pallas as pl
from jax.experimental.pallas import tpu as pltpu
from jax.sharding import PartitionSpec as P

BLK = 2
epsilon = 1e-05
step_rate = 0.5
F32 = jnp.float32
BF16 = jnp.bfloat16


QUARTERS = 4
CORES = 2
DEPTH_Z = 4


def place(ny):
    me = lax.axis_index("rep")

    def index(z, y, core):
        return (z * ny + y) * CORES + core

    return me // (CORES * ny), (me // CORES) % ny, me % CORES, index


def greet(ny, z, y, core, index, across=()):
    barrier = pltpu.get_barrier_semaphore()
    peers = [{"rep": index((z + d) % DEPTH_Z, y, core)} for d in range(1, DEPTH_Z)]
    peers += [{"rep": index(z, (y + d) % ny, core)} for d in range(1, ny)]
    peers += [{"rep": index(z, y, 1 - core)}]
    peers += [{"section": section} for section in across]
    for peer in peers:
        pl.semaphore_signal(
            barrier, inc=1, device_id=peer, device_id_type=pl.DeviceIdType.MESH
        )
    pl.semaphore_wait(barrier, len(peers))


def remote(src, dst, send, recv, peer):
    return pltpu.make_async_remote_copy(
        src_ref=src,
        dst_ref=dst,
        send_sem=send,
        recv_sem=recv,
        device_id=peer if isinstance(peer, dict) else {"rep": peer},
        device_id_type=pl.DeviceIdType.MESH,
    )


def gather_kernel(ny, a_ref, b_ref, a_out, b_out, send, recv):
    z, y, core, index = place(ny)
    greet(ny, z, y, core, index)
    me = index(z, y, core)
    sibling = index(z, y, 1 - core)
    a_out[me] = a_ref[...]
    b_out[me] = b_ref[...]
    outs = (a_out, b_out)
    started = []

    def push(shard, peer):
        for k, out in enumerate(outs):
            copy = remote(
                out.at[shard], out.at[shard], send.at[len(started)], recv.at[k, shard], peer
            )
            copy.start()
            started.append(copy)

    def arrive(shard):
        for k, out in enumerate(outs):
            remote(
                out.at[shard], out.at[shard], send.at[0], recv.at[k, shard], sibling
            ).wait_recv()

    z_order = [1, DEPTH_Z - 1] + list(range(2, DEPTH_Z - 1))
    for dz in z_order:
        push(me, index((z + dz) % DEPTH_Z, y, core))
    for dz in [0] + z_order:
        shard = index((z + dz) % DEPTH_Z, y, core)
        if dz:
            arrive(shard)
        for dy in range(1, ny):
            push(shard, index(z, (y + dy) % ny, core))
        push(shard, sibling)
    for dz in [0] + z_order:
        for dy in range(1, ny):
            shard = index((z + dz) % DEPTH_Z, (y + dy) % ny, core)
            arrive(shard)
            push(shard, sibling)
    for dz in [0] + z_order:
        for dy in range(ny):
            arrive(index((z + dz) % DEPTH_Z, (y + dy) % ny, 1 - core))
    for copy in started:
        copy.wait_send()


def gather_shards(*shards):
    replicas = lax.axis_size("rep")
    ny = replicas // (CORES * DEPTH_Z)
    copies = len(shards) * (DEPTH_Z - 1 + DEPTH_Z * ny + DEPTH_Z * (ny - 1))
    vmem = pl.BlockSpec(memory_space=pltpu.VMEM)
    return pl.pallas_call(
        functools.partial(gather_kernel, ny),
        out_shape=[jax.ShapeDtypeStruct((replicas,) + v.shape, v.dtype) for v in shards],
        in_specs=[vmem] * len(shards),
        out_specs=[vmem] * len(shards),
        scratch_shapes=[
            pltpu.SemaphoreType.DMA((copies,)),
            pltpu.SemaphoreType.DMA((len(shards), replicas)),
        ],
        compiler_params=pltpu.CompilerParams(
            collective_id=0, has_side_effects=True, vmem_limit_bytes=32 * 2**20
        ),
    )(*shards)


def sum_kernel(ny, routed, *refs):
    kinds = routed + 3
    terms = refs[:kinds]
    mate_out, slots_out, rest_out = refs[kinds : kinds + 3]
    from_core, part, from_y, summed, from_z, mate_sum, slot_sum = refs[kinds + 3 : kinds + 10]
    send, recv_core, recv_y, recv_z, recv_x = refs[kinds + 10 :]
    z, y, core, index = place(ny)
    sections = lax.axis_size("section")
    section = lax.axis_index("section")
    mate = (section + sections // 2) % sections
    following = (section + 1) % sections
    before = (section + sections - 1) % sections
    greet(ny, z, y, core, index, (mate, following, before))
    sibling = index(z, y, 1 - core)
    started = []

    def push(src, dst, recv, peer):
        copy = remote(src, dst, send.at[len(started)], recv, peer)
        copy.start()
        started.append(copy)
        return copy

    y_order = list(range(1, ny)) + [0]
    z_order = list(range(2, DEPTH_Z - 1)) + [1, DEPTH_Z - 1, 0]
    core_copies, y_copies, z_copies, totals = {}, {}, {}, {}
    for k in range(kinds):
        for dy in y_order:
            yy = (y + dy) % ny
            core_copies[k, dy] = push(
                terms[k].at[1 - core, yy], from_core.at[k, yy], recv_core.at[k, dy], sibling
            )

    def to_y(k):
        for dy in y_order[:-1]:
            yy = (y + dy) % ny
            core_copies[k, dy].wait_recv()
            part[k, dy - 1] = (
                terms[k][core, yy].astype(F32) + from_core[k, yy].astype(F32)
            ).astype(BF16)
            y_copies[k, dy] = push(
                part.at[k, dy - 1],
                from_y.at[k, dy - 1],
                recv_y.at[k, dy - 1],
                index(z, yy, core),
            )

    def to_z(k):
        core_copies[k, 0].wait_recv()
        for dy in y_order[:-1]:
            y_copies[k, dy].wait_recv()
        for dz in z_order:
            zz = (z + dz) % DEPTH_Z
            total = terms[k][core, y, zz].astype(F32) + from_core[k, y, zz].astype(F32)
            for dy in range(1, ny):
                total = total + from_y[k, dy - 1, zz].astype(F32)
            if dz:
                summed[k, dz - 1] = total.astype(BF16)
                z_copies[k, dz] = push(
                    summed.at[k, dz - 1],
                    from_z.at[k, dz - 1],
                    recv_z.at[k, dz - 1],
                    index(zz, y, core),
                )
        totals[k] = total

    x_copies = []

    def finish(k):
        total = totals[k]
        for dz in z_order[:-1]:
            z_copies[k, dz].wait_recv()
            total = total + from_z[k, dz - 1].astype(F32)
        if k == 0:
            mate_sum[...] = total
            x_copies.append(push(mate_sum, mate_out, recv_x.at[0], {"section": mate}))
        elif k <= routed:
            slot_sum[k - 1] = total.astype(BF16)
            x_copies.append(
                push(
                    slot_sum.at[k - 1],
                    slots_out.at[k - 1],
                    recv_x.at[k],
                    {"section": following},
                )
            )
        else:
            rest_out[k - routed - 1] = total

    for k in range(kinds + 2):
        if k < kinds:
            to_y(k)
        if 1 <= k <= kinds:
            to_z(k - 1)
        if k >= 2:
            finish(k - 2)
    for copy in x_copies:
        copy.wait_recv()
    for copy in started:
        copy.wait_send()


def lay_terms(terms):
    replicas, rows, features = terms.shape
    ny = replicas // (CORES * DEPTH_Z)
    width = features // QUARTERS
    laid = terms.reshape(DEPTH_Z, ny, CORES, rows, QUARTERS, width)
    return laid.transpose(2, 1, 0, 4, 3, 5).reshape(CORES, ny, DEPTH_Z, rows * QUARTERS, width)


def lay_back(value, rows):
    tall, width = value.shape[-2:]
    value = value.reshape(-1, QUARTERS, rows, width).transpose(0, 2, 1, 3)
    return value.reshape(-1, rows, QUARTERS * width)


def sum_terms(mate_terms, slot_terms, d_terms, own_terms):
    laid = [lay_terms(v) for v in (mate_terms, *slot_terms, d_terms, own_terms)]
    _, ny, _, tall, width = laid[0].shape
    routed = len(slot_terms)
    kinds = len(laid)
    rows = mate_terms.shape[1]
    copies = kinds * (ny + ny - 1 + DEPTH_Z - 1) + 1 + routed
    vmem = pl.BlockSpec(memory_space=pltpu.VMEM)
    mate, slots, rest = pl.pallas_call(
        functools.partial(sum_kernel, ny, routed),
        out_shape=[
            jax.ShapeDtypeStruct((tall, width), F32),
            jax.ShapeDtypeStruct((routed, tall, width), BF16),
            jax.ShapeDtypeStruct((2, tall, width), F32),
        ],
        in_specs=[vmem] * kinds,
        out_specs=[vmem] * 3,
        scratch_shapes=[
            pltpu.VMEM((kinds, ny, DEPTH_Z, tall, width), BF16),
            pltpu.VMEM((kinds, ny - 1, DEPTH_Z, tall, width), BF16),
            pltpu.VMEM((kinds, ny - 1, DEPTH_Z, tall, width), BF16),
            pltpu.VMEM((kinds, DEPTH_Z - 1, tall, width), BF16),
            pltpu.VMEM((kinds, DEPTH_Z - 1, tall, width), BF16),
            pltpu.VMEM((tall, width), F32),
            pltpu.VMEM((routed, tall, width), BF16),
            pltpu.SemaphoreType.DMA((copies,)),
            pltpu.SemaphoreType.DMA((kinds, ny)),
            pltpu.SemaphoreType.DMA((kinds, ny - 1)),
            pltpu.SemaphoreType.DMA((kinds, DEPTH_Z - 1)),
            pltpu.SemaphoreType.DMA((1 + routed,)),
        ],
        compiler_params=pltpu.CompilerParams(
            collective_id=1, has_side_effects=True, vmem_limit_bytes=40 * 2**20
        ),
    )(*laid)
    rest = lay_back(rest, rows)
    return lay_back(mate, rows)[0], lay_back(slots, rows), rest[0], rest[1]


def passed_along(value, by):
    peers = lax.axis_size("section")
    return lax.ppermute(value, "section", [(i, (i + by) % peers) for i in range(peers)])


def route_select(counts, replicas, blocks_dev, capacity):
    blocks = replicas * blocks_dev
    member = jnp.arange(replicas, dtype=jnp.int32)
    ahead = member[:, None] < member[None, :]
    row_start = jnp.sum(jnp.where(ahead[None], counts[:, :, None], 0), axis=1)
    column_start = jnp.sum(jnp.where(ahead[:, :, None], counts[:, None, :], 0), axis=0)
    row_total = row_start + counts
    block_ids = jnp.arange(blocks_dev, dtype=jnp.int32)
    inside = (block_ids[None, :, None] >= row_start[:, None, :]) & (
        block_ids[None, :, None] < row_total[:, None, :]
    )
    member_ids = jnp.arange(replicas, dtype=jnp.int32)
    slot = member_ids[None, None, :] * capacity + (
        column_start[:, None, :] + block_ids[None, :, None] - row_start[:, None, :]
    )
    target = jnp.sum(jnp.where(inside, slot, 0), axis=2).reshape(blocks)
    return target


def one_hot(row_ids, count):
    return (row_ids[:, None] == jnp.arange(count, dtype=jnp.int32)[None, :]).astype(BF16)


def mm(a, b):
    return jnp.dot(a, b, preferred_element_type=F32)


def mm_t(a, b):
    return lax.dot_general(a, b, (((1,), (1,)), ((), ())), preferred_element_type=F32)


def normalize(layer_rows, gain_row):
    values = layer_rows.astype(F32)
    row_scale = lax.rsqrt(jnp.mean(values * values, axis=1, keepdims=True) + epsilon)
    return values, row_scale, (values * row_scale * gain_row[None, :]).astype(BF16)


def low_rank(coefs, factors):
    high = coefs.astype(BF16)
    low = (coefs - high.astype(F32)).astype(BF16)
    return mm(jnp.concatenate((high, low), 1), jnp.concatenate((factors, factors), 0))


def per_device(layer_in, next_in, returned, norm_gain, gate_weight, up_weight, down_weight, wiring):
    replicas = lax.axis_size("rep")
    position = lax.axis_index("rep")
    partner_offset = lax.axis_size("section") // 2
    rows = layer_in.shape[1]
    features = layer_in.shape[2]
    blocks_dev = rows // BLK
    slot_rows = returned.shape[1]
    capacity = slot_rows // BLK
    tokens = rows * replicas
    gain = norm_gain[0]
    gate, up, down = gate_weight[0], up_weight[0], down_weight[0]
    factor = step_rate / tokens

    values, row_scale, normed_own = normalize(layer_in[0], gain)
    next_values, _, next_own = normalize(next_in[0], gain)
    next_mate = passed_along(next_own, partner_offset)
    later = passed_along(returned[0], -1)
    target = route_select(wiring[0], replicas, blocks_dev, capacity)
    width = features // QUARTERS
    mate_shard = next_mate.reshape(rows, QUARTERS, width).transpose(1, 0, 2)
    shards, mate_shards = gather_shards(
        jnp.concatenate((normed_own, next_own, later), 0),
        mate_shard.reshape(QUARTERS * rows, width),
    )
    tall = shards.shape[1]
    shards = shards.reshape(replicas * tall, features)
    mate_shards = mate_shards.reshape(replicas * QUARTERS * rows, width)
    token = jnp.arange(tokens, dtype=jnp.int32)
    member, inner = token // rows, token % rows
    target_rows = (target[:, None] * BLK + jnp.arange(BLK, dtype=jnp.int32)[None, :]).reshape(-1)
    slot_source = target_rows // slot_rows * tall + 2 * rows + target_rows % slot_rows
    picked = mm(
        one_hot(
            jnp.concatenate((slot_source, member * tall + inner, member * tall + rows + inner)),
            replicas * tall,
        ),
        shards,
    ).astype(BF16)
    mate_rows = member * QUARTERS * rows + inner
    nexts_mate = jnp.concatenate(
        [
            mm(one_hot(mate_rows + q * rows, replicas * QUARTERS * rows), mate_shards)
            for q in range(QUARTERS)
        ],
        1,
    ).astype(BF16)
    cotangent = picked[:tokens]
    normed = picked[tokens : 2 * tokens]
    lhs = jnp.concatenate((picked[tokens:], nexts_mate), 0)
    nexts = lhs[tokens:]

    gate_all = mm(lhs, gate)
    up_all = mm(lhs, up)
    gate_act, up_act = gate_all[:tokens], up_all[:tokens]
    sigmoid = jax.nn.sigmoid(gate_act)
    silu = gate_act * sigmoid
    hidden = (silu * up_act).astype(BF16)
    dhidden = mm_t(cotangent, down)
    d_gate = (dhidden * up_act * sigmoid * (1.0 + gate_act * (1.0 - sigmoid))).astype(BF16)
    d_up = (dhidden * silu).astype(BF16)

    coefs = factor * mm_t(nexts, normed)
    next_gate = 0.5 * (gate_all[tokens:] - low_rank(coefs, d_gate))
    next_up = 0.5 * (up_all[tokens:] - low_rank(coefs, d_up))
    to_mate = jnp.stack((next_gate[tokens:], next_up[tokens:])).astype(BF16)
    from_mate = passed_along(to_mate, partner_offset).astype(F32)

    dterm = (mm_t(d_gate, gate) + mm_t(d_up, up)).astype(BF16)
    term = mm(hidden, down)
    own = lax.dynamic_slice_in_dim(term, position * rows, rows, 0) + values
    term = lax.dynamic_update_slice_in_dim(term, own, position * rows, 0).astype(BF16)
    slot_ids = jnp.arange(replicas * slot_rows, dtype=jnp.int32)
    select = (slot_ids[:, None] == target_rows[None, :]).astype(BF16)
    slot_term = mm(select, term).astype(BF16).reshape(replicas, slot_rows, features)
    slot_terms = [slot_term[:, at : at + rows] for at in range(0, slot_rows, rows)]

    gate_next = next_gate[:tokens] + from_mate[0]
    up_next = next_up[:tokens] + from_mate[1]
    hidden_own = (jax.nn.silu(gate_next) * up_next).astype(BF16)
    hidden_mate = passed_along(hidden_own, partner_offset)
    hidden_both = jnp.concatenate((hidden_own, hidden_mate), 0)
    down_coefs = factor * mm_t(hidden_both, hidden)
    term_next = (0.5 * (mm(hidden_both, down) - low_rank(down_coefs, cotangent))).astype(BF16)
    term_next = term_next.reshape(2, replicas, rows, features)
    mate_sum, slots, dnormed, own_sum = sum_terms(
        term_next[1], slot_terms, dterm.reshape(replicas, rows, features), term_next[0]
    )
    next_out = (own_sum + mate_sum + next_values).astype(BF16)
    forwarded = slots.reshape(slot_rows, features)
    scaled = gain[None, :] * dnormed
    cotangent_own = lax.dynamic_slice_in_dim(cotangent, position * rows, rows, 0)
    input_grad = (
        cotangent_own.astype(F32)
        + row_scale * scaled
        - values * row_scale**3 * jnp.mean(values * scaled, axis=1, keepdims=True)
    ).astype(BF16)
    return (forwarded[None], input_grad[None], next_out[None])


def solution(mesh):
    in_specs = (
        P("section", "rep", None),
        P("section", "rep", None),
        P("section", "rep", None),
        P("section", None),
        P("section", None, "rep"),
        P("section", None, "rep"),
        P("section", "rep", None),
        P("section", None, None),
    )
    out_specs = (P("section", "rep", None), P("section", "rep", None), P("section", "rep", None))
    return jax.shard_map(
        per_device, mesh=mesh, in_specs=in_specs, out_specs=out_specs, check_vma=False
    )
```

time: 138 us -> 99.6 us (0.72)
  Pallas kernels: 65.8 us -> 50.5 us
  local copies, waits for them, and re-layouts: 22.9 us -> 11.5 us
  waiting for transfers between devices: 8.23 us -> 4.24 us
  other arithmetic: 9.73 us -> 6.92 us
  starting transfers between devices: 6.88 us -> 4.27 us
  matrix products: 23 us -> 20.4 us
    pallas_call x3 -> x2, Pallas kernels: 65.8 us -> 50.5 us  [the longest x1 26 us: sum_terms(): pl.pallas_call(functools.partial(sum_kernel, ny, routed), out_shape=[jax....]
    reshape x13 -> x11, local copies, waits for them, and re-layouts: 14.2 us -> 2.54 us  [the longest x5 1.64 us: lay_terms(): laid.transpose(2, 1, 0, 4, 3, 5)]
    ppermute x6 -> x4, waiting for transfers between devices: 8.23 us -> 4.24 us  [passed_along(): lax.ppermute(value, 'section', [(i, (i + by) % peers) for i in range(peer...]
    another operation x1 -> x7, local copies, waits for them, and re-layouts: 0.8 us -> 4.47 us  [the longest x6 3.81 us: lay_terms(): laid = terms.reshape(DEPTH_Z, ny, CORES, rows, QUARTERS, width)]
    ppermute x6 -> x4, starting transfers between devices: 6.88 us -> 4.27 us  [passed_along(): lax.ppermute(value, 'section', [(i, (i + by) % peers) for i in range(peer...]
    dot_general x8 -> x13, matrix products: 14.2 us -> 12.5 us  [mm(): return jnp.dot(a, b, preferred_element_type=F32)]
    slice x9 -> x4, local copies, waits for them, and re-layouts: 3.25 us -> 1.52 us  [the longest x1 0.89 us: per_device(): term_next[0]]
    concatenate x4 -> x0, local copies, waits for them, and re-layouts: 1.71 us -> none  [the longest x3 1.68 us: per_device(): jnp.concatenate((slot_term.reshape(replicas, slot_rows, features), dterm....]
  transfers between devices with their start and end apart: 6 -> 4, of which waited for: 3 -> 2; matrix products, arithmetic and copies ran while one was open for 15% -> 15% of each run, Pallas kernels for 30% -> 0%
where the time goes in v3:
time: 99.6 us; the launch traced here: 99 us
  Pallas kernels  50.5 us (51%)
  matrix products  20.4 us (20%)
  local copies, waits for them, and re-layouts  11.5 us (12%)
  other arithmetic  6.92 us (7%)
  starting transfers between devices  4.27 us (4%)
  waiting for transfers between devices  4.24 us (4%)
  between operations  1.12 us (1%)
    pallas_call x1, Pallas kernels, sum_terms(): pl.pallas_call(functools.partial(sum_kernel, ny, routed), out_shape=[jax....  26 us
    pallas_call x1, Pallas kernels, gather_shards(): pl.pallas_call(functools.partial(gather_kernel, ny), out_shape=[jax.Shape...  24.5 us
    dot_general x13, matrix products, mm(): return jnp.dot(a, b, preferred_element_type=F32)  12.5 us
    dot_general x5, matrix products, mm_t(): lax.dot_general(a, b, (((1,), (1,)), ((), ())), preferred_element_type=F32)  7.92 us
    ppermute x4, starting transfers between devices, passed_along(): lax.ppermute(value, 'section', [(i, (i + by) % peers) for i in range(peer...  4.27 us
    ppermute x4, waiting for transfers between devices, passed_along(): lax.ppermute(value, 'section', [(i, (i + by) % peers) for i in range(peer...  4.24 us
    another operation x6, local copies, waits for them, and re-layouts, lay_terms(): laid = terms.reshape(DEPTH_Z, ny, CORES, rows, QUARTERS, width)  3.81 us
    unnamed x24, local copies, waits for them, and re-layouts  2.09 us
  transfers between devices with their start and end apart: 4, of which 2 were waited for; matrix products, arithmetic and copies ran while one was open for 15% of the time, Pallas kernels for 0%

profile of v3, /device:TPU:0, one launch (start us, length us, event | category | flops | bytes accessed | tf_op | source)
XLA Modules:
  0.0 99.0 jit_solution(5798056729171109759)
XLA Ops:
  0.6 3.0 %collective-permute-start = (bf16[8,4096]{1,0:T(8,128)(2,1)}, bf16[8,4096]{1,0:T(8,128)(2,1)S(1)}, u32[]{:S(2)}, u32[]{:S(2)}) collective-permute-start(bf16[8,4096]{1,0:T(8,128)(2,1)} %bitcast.135), channel_id=1, source_target_pairs={{0,16},{16,0},{1,17},{17,1},{2,18},{18,2},{3,19},{19,3},{4,20},{20... | collective-permute-start | bytes 196616 | tf_op jit(solution)/shard_map/ppermute | solution.py:277
  3.6 0.9 fusion.67
  4.5 0.9 fusion.63
  5.4 0.5 multiply_multiply_fusion
  6.0 0.9 fusion.69
  6.9 0.1 collective-permute-start.1
  7.0 0.9 select_reduce_fusion.1
  7.9 0.7 bitcast_add_fusion
  8.6 0.1 select_reduce_fusion.2
  8.8 0.1 copy.25
  8.8 0.1 mul.177
  8.9 0.1 iota_add_fusion
  9.0 0.1 add.230
  9.1 0.1 pad_add_fusion
  9.2 1.6 %collective-permute-done.1 = bf16[4,4096]{1,0:T(4,128)(2,1)S(1)} collective-permute-done((bf16[4,4096]{1,0:T(4,128)(2,1)S(1)}, bf16[4,4096]{1,0:T(4,128)(2,1)S(1)}, u32[]{:S(2)}, u32[]{:S(2)}) %collective-permute-start.1) | collective-permute-done | bytes 32800 | tf_op jit(solution)/shard_map/ppermute | solution.py:277
  10.9 24.5 %shard_map.103 = (bf16[16,16,4096]{2,1,0:T(8,128)(2,1)S(1)}, bf16[16,16,1024]{2,1,0:T(8,128)(2,1)S(1)}) custom-call(bf16[16,4096]{1,0:T(8,128)(2,1)S(1)} %pad_maximum_fusion.4.a_ref, bf16[16,1024]{1,0:T(8,128)(2,1)S(1)} %reshape.210.b_ref), custom_call_target="tpu_custom_call" | custom-call | tf_op jit(solution)/shard_map/pallas_call | solution.py:106
  35.5 0.2 convolution_convert_fusion.5
  35.7 0.2 convolution_convert_fusion.2
  36.0 0.2 convolution_convert_fusion.3
  36.2 0.2 convolution_convert_fusion.4
  36.5 0.6 convolution_convert_fusion
  37.2 0.5 fusion.97
  37.7 0.2 slice-done.4
  37.9 1.3 %slice-done.5 = s8[3145728]{0:T(1024)(128)(4,1)S(1)} async-done(((s8[7340032]{0:T(1024)(128)(4,1)}), s8[3145728]{0:T(1024)(128)(4,1)S(1)}, s32[]{:S(2)}) %slice-start.5) | async-done | bytes 3145752
  39.2 1.8 %fusion.12 = f32[192,896]{1,0:T(8,128)S(1)} fusion(bf16[1,4096,896]{2,1,0:T(8,128)(2,1)S(1)} %bitcast.119, bf16[64,1024]{1,0:T(8,128)(2,1)S(1)} %convolution_convert_fusion.2, bf16[64,1024]{1,0:T(8,128)(2,1)S(1)} %convolution_convert_fusion.3, bf16[64,1024]{1,0:T(8,128)(2,1)S(1)} %convolution_convert_fusion.4, ...), kind=kOutput, calls=%fused_computation.12 | convolution fusion | flops 1417150464 | bytes 9601024 | tf_op jit(solution)/shard_map/dot_general | solution.py:304
  41.0 0.3 slice-done.3
  41.3 1.9 %fusion.2 = f32[192,896]{1,0:T(8,128)S(1)} fusion(bf16[1,4096,896]{2,1,0:T(8,128)(2,1)S(1)} %bitcast.117, bf16[64,1024]{1,0:T(8,128)(2,1)S(1)} %convolution_convert_fusion.2, bf16[64,1024]{1,0:T(8,128)(2,1)S(1)} %convolution_convert_fusion.3, bf16[64,1024]{1,0:T(8,128)(2,1)S(1)} %convolution_convert_fusion.4, ...), kind=kOutput, calls=%fused_computation.2 | convolution fusion | flops 1417150464 | bytes 9601024 | tf_op jit(solution)/shard_map/dot_general | solution.py:304
  43.2 0.3 slice-done.1
  43.5 2.4 %multiply_convert_fusion.2 = (bf16[64,896]{1,0:T(8,128)(2,1)S(1)}, bf16[64,896]{1,0:T(8,128)(2,1)S(1)}, bf16[64,896]{1,0:T(8,128)(2,1)S(1)}) fusion(f32[192,896]{1,0:T(8,128)S(1)} %fusion.12, f32[192,896]{1,0:T(8,128)S(1)} %fusion.2, bf16[1,896,4096]{2,1,0:T(8,128)(2,1)S(1)} %bitcast.115, bf16[192,4096]{1,0:T(8,128)(2,1)S(1)} %convolution_convert_fusion), kind=kOutput, calls=%fused_computation.69 | convolution fusion | flops 470622208 | bytes 8667136 | tf_op jit(solution)/shard_map/dot_general | solution.py:308
  45.8 0.3 fusion.31
  46.1 0.2 fusion.30
  46.4 0.6 collective-permute-start.2
  47.0 1.4 %fusion.4 = f32[64,4096]{1,0:T(8,128)S(1)} fusion(bf16[64,896]{1,0:T(8,128)(2,1)S(1)} %get-tuple-element.18, bf16[1,896,4096]{2,1,0:T(8,128)(2,1)S(1)} %bitcast.115), kind=kOutput, calls=%fused_computation.4 | convolution fusion | flops 469762048 | bytes 8503296 | tf_op jit(solution)/shard_map/dot_general | solution.py:304
  48.5 0.4 fusion.23
  49.0 0.5 fusion.96
  49.5 2.3 %fusion = f32[64,4096]{1,0:T(8,128)S(1)} fusion(bf16[64,896]{1,0:T(8,128)(2,1)S(1)} %get-tuple-element.23, bf16[1,4096,896]{2,1,0:T(8,128)(2,1)S(1)} %bitcast.117), kind=kOutput, calls=%fused_computation | convolution fusion | flops 469762048 | bytes 8503296 | tf_op jit(solution)/shard_map/dot_general | solution.py:308
  51.8 2.6 %collective-permute-done.2 = bf16[2,64,896]{2,1,0:T(8,128)(2,1)S(1)} collective-permute-done((bf16[2,64,896]{2,1,0:T(8,128)(2,1)S(1)}, bf16[2,64,896]{2,1,0:T(8,128)(2,1)S(1)}, u32[]{:S(2)}, u32[]{:S(2)}) %collective-permute-start.2) | collective-permute-done | bytes 229408 | tf_op jit(solution)/shard_map/ppermute | solution.py:277
  54.5 0.1 fusion.49
  54.6 0.6 collective-permute-start.3
  55.2 2.5 %fusion.27 = bf16[64,4096]{1,0:T(8,128)(2,1)S(1)} fusion(f32[64,4096]{1,0:T(8,128)S(1)} %fusion, bf16[64,896]{1,0:T(8,128)(2,1)S(1)} %get-tuple-element.17, bf16[1,4096,896]{2,1,0:T(8,128)(2,1)S(1)} %bitcast.119), kind=kOutput, calls=%fused_computation.21 | convolution fusion | flops 470286336 | bytes 9027584 | tf_op jit(solution)/shard_map/dot_general | solution.py:308
  57.7 0.4 reshape.226
  58.1 0.3 copy.29
  58.4 0.1 reshape.216.refs_1_
  58.5 0.4 reshape.227
  58.9 0.3 copy.31
  59.2 0.1 reshape.218.refs_2_
  59.3 0.4 reshape_reshape.3
  59.7 0.3 copy.45
  60.0 0.1 reshape.219.refs_3_
  60.1 0.2 subtract_convert_fusion
  60.3 0.5 fusion.41
  60.8 4.4 %fusion.20 = bf16[128,4096]{1,0:T(8,128)(2,1)S(1)} fusion(f32[128,4096]{1,0:T(8,128)S(1)} %fusion.41, bf16[1,896,4096]{2,1,0:T(8,128)(2,1)} %param.14, bf16[64,896]{1,0:T(8,128)(2,1)S(1)} %collective-permute-done.3, bf16[64,896]{1,0:T(8,128)(2,1)S(1)} %fusion.49), kind=kOutput, calls=%fused_computation.17 | convolution fusion | flops 941555712 | bytes 10715136 | tf_op jit(solution)/shard_map/dot_general | solution.py:304
  65.2 0.9 fusion.95
  66.1 0.4 reshape_squeeze.6
  66.5 0.3 copy.46
  66.7 0.1 reshape.213.refs_0_
  66.9 1.4 %reshape_squeeze.7 = bf16[4,2,2,4,4,1024]{5,4,3,2,1,0:T(4,128)(2,1)S(1)} reshape(bf16[64,4096]{1,0:T(8,128)(2,1)} %get-tuple-element.19) | data formatting | bytes 1048576 | tf_op jit(solution)/shard_map/reshape;squeeze | solution.py:226
  68.3 1.1 %copy.44 = bf16[4,2,2,4,4,1024]{5,3,4,0,1,2:T(4,128)(2,1)} copy(bf16[4,2,2,4,4,1024]{5,4,3,2,1,0:T(4,128)(2,1)S(1)} %reshape_squeeze.7) | data formatting | bytes 1048576 | tf_op jit(solution)/shard_map/reshape;squeeze | solution.py:226
  69.4 1.2 %reshape.220.refs_4_ = bf16[2,2,4,16,1024]{4,3,2,1,0:T(8,128)(2,1)S(1)} reshape(bf16[2,2,4,4,4,1024]{5,4,3,2,1,0:T(4,128)(2,1)} %bitcast.124) | data formatting | bytes 1048576 | tf_op jit(solution)/shard_map/reshape | solution.py:227
  70.6 26.0 %shard_map.104 = (f32[16,1024]{1,0:T(8,128)S(1)}, bf16[2,16,1024]{2,1,0:T(8,128)(2,1)S(1)}, f32[2,16,1024]{2,1,0:T(8,128)S(1)}) custom-call(bf16[2,2,4,16,1024]{4,3,2,1,0:T(8,128)(2,1)S(1)} %reshape.213.refs_0_, bf16[2,2,4,16,1024]{4,3,2,1,0:T(8,128)(2,1)S(1)} %reshape.216.refs_1_, bf16[2,2,4,16,1024]{4,3,2,1,0:T(8,128)(2,1)S(1)} %reshape.218.refs_2_, ...), custom_call_target="tpu_custom_call" | custom-call | tf_op jit(solution)/shard_map/pallas_call | solution.py:244
  96.7 0.7 broadcast_in_dim_reshape_reshape.3
  97.5 0.1 fusion.74
  97.6 0.6 fusion.66
  98.3 0.7 fusion.83
  (46 shorter events, 0.6 us)
Async XLA Ops:
  0.6 10.2 %collective-permute-start = (bf16[8,4096]{1,0:T(8,128)(2,1)}, bf16[8,4096]{1,0:T(8,128)(2,1)S(1)}, u32[]{:S(2)}, u32[]{:S(2)}) collective-permute-start(bf16[8,4096]{1,0:T(8,128)(2,1)} %bitcast.135), channel_id=1, source_target_pairs={{0,16},{16,0},{1,17},{17,1},{2,18},{18,2},{3,19},{19,3},{4,20},{20... | collective-permute-start | bytes 196616 | tf_op jit(solution)/shard_map/ppermute | solution.py:277
  6.0 1.0 %copy-start.3 = (f32[4]{0:T(128)}, f32[4]{0:T(128)S(1)}, u32[]{:S(2)}) copy-start(f32[4]{0:T(128)S(1)} %get-tuple-element.31) | copy-start | bytes 52
  6.9 4.0 %collective-permute-start.1 = (bf16[4,4096]{1,0:T(4,128)(2,1)S(1)}, bf16[4,4096]{1,0:T(4,128)(2,1)S(1)}, u32[]{:S(2)}, u32[]{:S(2)}) collective-permute-start(bf16[4,4096]{1,0:T(4,128)(2,1)S(1)} %get-tuple-element.29), channel_id=1, source_target_pairs={{0,16},{16,0},{1,17},{17,1},{2,18},{18,2},{3,19},{19,3},{4,20},{20... | collective-permute-start | bytes 98312 | tf_op jit(solution)/shard_map/ppermute | solution.py:277
  35.7 2.2 %slice-start.4 = ((s8[7340032]{0:T(1024)(128)(4,1)}), s8[4194304]{0:T(1024)(128)(4,1)S(1)}, s32[]{:S(2)}) async-start(s8[7340032]{0:T(1024)(128)(4,1)} %bitcast.118), calls=%async_computation.4 | async-start | bytes 8388608
  37.1 2.1 %slice-start.5 = ((s8[7340032]{0:T(1024)(128)(4,1)}), s8[3145728]{0:T(1024)(128)(4,1)S(1)}, s32[]{:S(2)}) async-start(s8[7340032]{0:T(1024)(128)(4,1)} %bitcast.118), calls=%async_computation.5 | async-start | bytes 6291456
  37.2 3.9 %slice-start.2 = ((s8[7340032]{0:T(1024)(128)(4,1)}), s8[4194304]{0:T(1024)(128)(4,1)S(1)}, s32[]{:S(2)}) async-start(s8[7340032]{0:T(1024)(128)(4,1)} %bitcast.116), calls=%async_computation.2 | async-start | bytes 8388608
  39.2 2.1 %slice-start.3 = ((s8[7340032]{0:T(1024)(128)(4,1)}), s8[3145728]{0:T(1024)(128)(4,1)S(1)}, s32[]{:S(2)}) async-start(s8[7340032]{0:T(1024)(128)(4,1)} %bitcast.116), calls=%async_computation.3 | async-start | bytes 6291456
  39.2 4.0 %slice-start = ((s8[7340032]{0:T(1024)(128)(4,1)}), s8[4194304]{0:T(1024)(128)(4,1)S(1)}, s32[]{:S(2)}) async-start(s8[7340032]{0:T(1024)(128)(4,1)} %bitcast.114), calls=%async_computation | async-start | bytes 8388608
  41.3 2.1 %slice-start.1 = ((s8[7340032]{0:T(1024)(128)(4,1)}), s8[3145728]{0:T(1024)(128)(4,1)S(1)}, s32[]{:S(2)}) async-start(s8[7340032]{0:T(1024)(128)(4,1)} %bitcast.114), calls=%async_computation.1 | async-start | bytes 6291456
  46.4 8.0 %collective-permute-start.2 = (bf16[2,64,896]{2,1,0:T(8,128)(2,1)S(1)}, bf16[2,64,896]{2,1,0:T(8,128)(2,1)S(1)}, u32[]{:S(2)}, u32[]{:S(2)}) collective-permute-start(bf16[2,64,896]{2,1,0:T(8,128)(2,1)S(1)} %pad_maximum_fusion), channel_id=1, source_target_pairs={{0,16},{16,0},{1,17},{17,1},{2,18},{18,2},{3,19},{19,3},{4,20},{20... | collective-permute-start | bytes 688136 | tf_op jit(solution)/shard_map/ppermute | solution.py:277
  47.0 1.4 %copy-start = (bf16[1,4,4096]{2,1,0:T(4,128)(2,1)S(1)}, bf16[1,4,4096]{2,1,0:T(4,128)(2,1)}, u32[]{:S(2)}) copy-start(bf16[1,4,4096]{2,1,0:T(4,128)(2,1)} %param.8) | copy-start | bytes 98308
  54.6 5.6 %collective-permute-start.3 = (bf16[64,896]{1,0:T(8,128)(2,1)S(1)}, bf16[64,896]{1,0:T(8,128)(2,1)S(1)}, u32[]{:S(2)}, u32[]{:S(2)}) collective-permute-start(bf16[64,896]{1,0:T(8,128)(2,1)S(1)} %fusion.49), channel_id=1, source_target_pairs={{0,16},{16,0},{1,17},{17,1},{2,18},{18,2},{3,19},{19,3},{4,20},{20... | collective-permute-start | bytes 344072 | tf_op jit(solution)/shard_map/ppermute | solution.py:277
  70.5 26.9 %copy-start.2 = (f32[1,4096]{1,0:T(1,128)S(1)}, f32[1,4096]{1,0:T(1,128)}, u32[]{:S(2)}) copy-start(f32[1,4096]{1,0:T(1,128)} %param.11) | copy-start | bytes 49156
  70.6 27.1 %copy-start.1 = (bf16[1,4,4096]{2,1,0:T(4,128)(2,1)S(1)}, bf16[1,4,4096]{2,1,0:T(4,128)(2,1)}, u32[]{:S(2)}) copy-start(bf16[1,4,4096]{2,1,0:T(4,128)(2,1)} %param.9) | copy-start | bytes 98308
  70.6 27.7 %copy-start.4 = (f32[4]{0:T(128)S(1)}, f32[4]{0:T(128)}, u32[]{:S(2)}) copy-start(f32[4]{0:T(128)} %copy-done.3) | copy-start | bytes 52
  70.6 27.7 %copy-start.5 = (f32[4]{0:T(128)S(1)}, f32[4]{0:T(128)}, u32[]{:S(2)}) copy-start(f32[4]{0:T(128)} %get-tuple-element.30) | copy-start | bytes 52

commit v4 on v3

v4 whole, which is shorter than its diff:
```python
import functools

import jax
import jax.numpy as jnp
from jax import lax
from jax.experimental import pallas as pl
from jax.experimental.pallas import tpu as pltpu
from jax.sharding import PartitionSpec as P

BLK = 2
epsilon = 1e-05
step_rate = 0.5
F32 = jnp.float32
BF16 = jnp.bfloat16


QUARTERS = 4
CORES = 2
DEPTH_Z = 4


def place(ny):
    me = lax.axis_index("rep")

    def index(z, y, core):
        return (z * ny + y) * CORES + core

    return me // (CORES * ny), (me // CORES) % ny, me % CORES, index


def greet(ny, z, y, core, index, across=()):
    barrier = pltpu.get_barrier_semaphore()
    peers = [{"rep": index((z + d) % DEPTH_Z, y, core)} for d in range(1, DEPTH_Z)]
    peers += [{"rep": index(z, (y + d) % ny, core)} for d in range(1, ny)]
    peers += [{"rep": index(z, y, 1 - core)}]
    peers += [{"section": section} for section in across]
    for peer in peers:
        pl.semaphore_signal(
            barrier, inc=1, device_id=peer, device_id_type=pl.DeviceIdType.MESH
        )
    pl.semaphore_wait(barrier, len(peers))


def remote(src, dst, send, recv, peer):
    return pltpu.make_async_remote_copy(
        src_ref=src,
        dst_ref=dst,
        send_sem=send,
        recv_sem=recv,
        device_id=peer if isinstance(peer, dict) else {"rep": peer},
        device_id_type=pl.DeviceIdType.MESH,
    )


def routing_matrices(counts, rows, blocks_dev, capacity, groups):
    replicas = counts.shape[0]
    tokens = replicas * rows

    def iota(shape, axis):
        return lax.broadcasted_iota(jnp.int32, shape, axis)

    square = (replicas, replicas)
    counts = counts.astype(F32)
    ahead = (iota(square, 0) < iota(square, 1)).astype(F32)
    behind = (iota(square, 1) < iota(square, 0)).astype(F32)
    row_start = mm(counts, ahead)
    column_start = mm(behind, counts)
    receiver = iota(square, 1).astype(F32)
    spread = jnp.ones((replicas, tokens), F32)
    target = (iota((tokens, tokens), 0) % BLK).astype(F32)
    owner = iota((tokens, replicas), 0) // rows == iota((tokens, replicas), 1)
    block = iota((tokens, replicas), 0) % rows // BLK
    for b in range(blocks_dev):
        inside = (row_start <= b) & (row_start + counts > b)
        slot = jnp.where(inside, receiver * capacity + column_start + b - row_start, 0.0)
        rows_of = (owner & (block == b)).astype(F32)
        target = target + BLK * mm(rows_of, mm(slot, spread))
    lane = iota((tokens, tokens), 1)
    place_of = lane // rows * (rows * groups) + lane % rows
    return [(target == (place_of + g * rows).astype(F32)).astype(F32) for g in range(groups)]


def gather_kernel(
    ny, rows, blocks_dev, head_ref, back_ref, wiring_ref, head, back, mates, select, send, send_x, recv
):
    z, y, core, index = place(ny)
    sections = lax.axis_size("section")
    section = lax.axis_index("section")
    mate = (section + sections // 2) % sections
    following = (section + 1) % sections
    before = (section + sections - 1) % sections
    greet(ny, z, y, core, index, (mate, following, before))
    me = index(z, y, core)
    sibling = index(z, y, 1 - core)
    outs = (head, back, mates)
    width = mates.shape[2]

    def hop(kind, way, shard, peer):
        out = outs[kind].at[shard]
        return remote(out, out, send.at[kind, way, shard], recv.at[kind, shard], peer)

    def over_x(shard):
        return remote(
            head.at[shard, :, pl.ds(width, width)],
            mates.at[shard],
            send_x.at[shard],
            recv.at[2, shard],
            {"section": mate},
        )

    def arrive(kind, shard):
        hop(kind, 0, shard, sibling).wait_recv()

    back_copy = remote(
        back_ref, back.at[me], send_x.at[send_x.shape[0] - 1], recv.at[1, me], {"section": before}
    )
    head[me] = head_ref[...]
    back_copy.start()

    def arrivals(d):
        for step in (1, -1) if d else (0,):
            yield step, z - step * d, (z - step * d >= 0) & (z - step * d < DEPTH_Z)

    def onward(kind, d, step, zz, act):
        shard = index(zz, y, core)
        for way, to in enumerate((1, -1)):
            if step in (0, to):

                @pl.when((z + to >= 0) & (z + to < DEPTH_Z))
                def _():
                    act(hop(kind, way, shard, index(z + to, y, core)))

        for dy in range(1, ny):
            act(hop(kind, 2 + dy, shard, index(z, (y + dy) % ny, core)))
        act(hop(kind, 2, shard, sibling))
        if kind == 0:
            act(over_x(shard))

    def along_z(d):
        for kind in range(2):
            for step, zz, there in arrivals(d):

                @pl.when(there)
                def _():
                    if d or kind:
                        arrive(kind, index(zz, y, core))
                    onward(kind, d, step, zz, lambda copy: copy.start())

    def from_y(d):
        for kind in range(2):
            for step, zz, there in arrivals(d):

                @pl.when(there)
                def _():
                    for dy in range(1, ny):
                        shard = index(zz, (y + dy) % ny, core)
                        arrive(kind, shard)
                        hop(kind, 2, shard, sibling).start()
                        if kind == 0:
                            over_x(shard).start()

    along_z(0)
    matrices = routing_matrices(
        wiring_ref[...], rows, blocks_dev, select.shape[0] * rows // BLK, select.shape[0]
    )
    for g, matrix in enumerate(matrices):
        select[g] = matrix.astype(BF16)
    for d in range(1, DEPTH_Z):
        along_z(d)
        from_y(d - 1)
    from_y(DEPTH_Z - 1)
    every = [(dz, dy) for dy in range(ny) for dz in range(DEPTH_Z)]
    for dz, dy in every:
        shard = index((z + dz) % DEPTH_Z, (y + dy) % ny, core)
        arrive(2, shard)
        hop(2, 2, shard, sibling).start()
    for kind in range(3):
        for dz, dy in every:
            arrive(kind, index((z + dz) % DEPTH_Z, (y + dy) % ny, 1 - core))
    back_copy.wait_send()
    for kind in range(2):
        for d in range(DEPTH_Z):
            for step, zz, there in arrivals(d):

                @pl.when(there)
                def _():
                    onward(kind, d, step, zz, lambda copy: copy.wait_send())
                    for dy in range(1, ny):
                        shard = index(zz, (y + dy) % ny, core)
                        hop(kind, 2, shard, sibling).wait_send()
                        if kind == 0:
                            over_x(shard).wait_send()

    for dz, dy in every:
        hop(2, 2, index((z + dz) % DEPTH_Z, (y + dy) % ny, core), sibling).wait_send()


def gather_shards(head, back, wiring, rows, blocks_dev):
    replicas = lax.axis_size("rep")
    ny = replicas // (CORES * DEPTH_Z)
    tokens = replicas * rows
    tall, wide = head.shape
    groups = back.shape[1] // (wide // 2)
    vmem = pl.BlockSpec(memory_space=pltpu.VMEM)
    return pl.pallas_call(
        functools.partial(gather_kernel, ny, rows, blocks_dev),
        out_shape=[
            jax.ShapeDtypeStruct((replicas,) + head.shape, BF16),
            jax.ShapeDtypeStruct((replicas,) + back.shape, BF16),
            jax.ShapeDtypeStruct((replicas, tall, wide // 2), BF16),
            jax.ShapeDtypeStruct((groups, tokens, tokens), BF16),
        ],
        in_specs=[vmem] * 3,
        out_specs=[vmem] * 4,
        scratch_shapes=[
            pltpu.SemaphoreType.DMA((3, 2 + ny, replicas)),
            pltpu.SemaphoreType.DMA((replicas + 1,)),
            pltpu.SemaphoreType.DMA((3, replicas)),
        ],
        compiler_params=pltpu.CompilerParams(
            collective_id=0, has_side_effects=True, vmem_limit_bytes=32 * 2**20
        ),
    )(head, back, wiring)


def sum_kernel(ny, routed, *refs):
    kinds = routed + 3
    terms = refs[:kinds]
    slots_out, rest_out = refs[kinds : kinds + 2]
    from_core, part, from_y, summed, from_z, to_x, from_x, slot_sum = refs[kinds + 2 : kinds + 10]
    send, recv_core, recv_y, recv_z, recv_x, recv_slot = refs[kinds + 10 :]
    z, y, core, index = place(ny)
    sections = lax.axis_size("section")
    section = lax.axis_index("section")
    mate = (section + sections // 2) % sections
    following = (section + 1) % sections
    before = (section + sections - 1) % sections
    greet(ny, z, y, core, index, (mate, following, before))
    sibling = index(z, y, 1 - core)
    started = []

    def push(src, dst, recv, peer):
        copy = remote(src, dst, send.at[len(started)], recv, peer)
        copy.start()
        started.append(copy)
        return copy

    y_order = list(range(1, ny)) + [0]
    z_order = list(range(2, DEPTH_Z - 1)) + [1, DEPTH_Z - 1, 0]
    core_copies, y_copies, z_copies, totals = {}, {}, {}, {}
    for k in range(kinds):
        for dy in y_order:
            yy = (y + dy) % ny
            core_copies[k, dy] = push(
                terms[k].at[1 - core, yy], from_core.at[k, yy], recv_core.at[k, dy], sibling
            )

    x_copies = {}
    for dy in y_order:
        yy = (y + dy) % ny
        core_copies[0, dy].wait_recv()
        to_x[yy] = (terms[0][core, yy].astype(F32) + from_core[0, yy].astype(F32)).astype(BF16)
        x_copies[dy] = push(to_x.at[yy], from_x.at[yy], recv_x.at[dy], {"section": mate})

    def pair_sum(k, yy, zz=slice(None)):
        total = terms[k][core, yy, zz].astype(F32) + from_core[k, yy, zz].astype(F32)
        if k == kinds - 1:
            total = total + from_x[yy, zz].astype(F32)
        return total

    def to_y(k):
        for dy in y_order[:-1]:
            yy = (y + dy) % ny
            core_copies[k, dy].wait_recv()
            if k == kinds - 1:
                x_copies[dy].wait_recv()
            part[k, dy - 1] = pair_sum(k, yy).astype(BF16)
            y_copies[k, dy] = push(
                part.at[k, dy - 1],
                from_y.at[k, dy - 1],
                recv_y.at[k, dy - 1],
                index(z, yy, core),
            )

    def to_z(k):
        core_copies[k, 0].wait_recv()
        if k == kinds - 1:
            x_copies[0].wait_recv()
        for dy in y_order[:-1]:
            y_copies[k, dy].wait_recv()
        for dz in z_order:
            zz = (z + dz) % DEPTH_Z
            total = pair_sum(k, y, zz)
            for dy in range(1, ny):
                total = total + from_y[k, dy - 1, zz].astype(F32)
            if dz:
                summed[k, dz - 1] = total.astype(BF16)
                z_copies[k, dz] = push(
                    summed.at[k, dz - 1],
                    from_z.at[k, dz - 1],
                    recv_z.at[k, dz - 1],
                    index(zz, y, core),
                )
        totals[k] = total

    slot_copies = []

    def finish(k):
        total = totals[k]
        for dz in z_order[:-1]:
            z_copies[k, dz].wait_recv()
            total = total + from_z[k, dz - 1].astype(F32)
        if k <= routed:
            slot_sum[k - 1] = total.astype(BF16)
            slot_copies.append(
                push(
                    slot_sum.at[k - 1],
                    slots_out.at[k - 1],
                    recv_slot.at[k - 1],
                    {"section": following},
                )
            )
        else:
            rest_out[k - routed - 1] = total

    for k in range(1, kinds + 2):
        if k < kinds:
            to_y(k)
        if 2 <= k <= kinds:
            to_z(k - 1)
        if k >= 3:
            finish(k - 2)
    for copy in slot_copies:
        copy.wait_recv()
    for copy in started:
        copy.wait_send()


def lay_terms(terms):
    replicas, rows, features = terms.shape
    ny = replicas // (CORES * DEPTH_Z)
    width = features // QUARTERS
    laid = terms.reshape(DEPTH_Z, ny, CORES, rows, QUARTERS, width)
    return laid.transpose(2, 1, 0, 4, 3, 5).reshape(CORES, ny, DEPTH_Z, rows * QUARTERS, width)


def lay_back(value, rows):
    tall, width = value.shape[-2:]
    value = value.reshape(-1, QUARTERS, rows, width).transpose(0, 2, 1, 3)
    return value.reshape(-1, rows, QUARTERS * width)


def sum_terms(mate_terms, slot_terms, d_terms, own_terms):
    laid = [lay_terms(v) for v in (mate_terms, *slot_terms, d_terms, own_terms)]
    _, ny, _, tall, width = laid[0].shape
    routed = len(slot_terms)
    kinds = len(laid)
    rows = mate_terms.shape[1]
    copies = kinds * (ny + ny - 1 + DEPTH_Z - 1) + ny + routed
    vmem = pl.BlockSpec(memory_space=pltpu.VMEM)
    slots, rest = pl.pallas_call(
        functools.partial(sum_kernel, ny, routed),
        out_shape=[
            jax.ShapeDtypeStruct((routed, tall, width), BF16),
            jax.ShapeDtypeStruct((2, tall, width), F32),
        ],
        in_specs=[vmem] * kinds,
        out_specs=[vmem] * 2,
        scratch_shapes=[
            pltpu.VMEM((kinds, ny, DEPTH_Z, tall, width), BF16),
            pltpu.VMEM((kinds, ny - 1, DEPTH_Z, tall, width), BF16),
            pltpu.VMEM((kinds, ny - 1, DEPTH_Z, tall, width), BF16),
            pltpu.VMEM((kinds, DEPTH_Z - 1, tall, width), BF16),
            pltpu.VMEM((kinds, DEPTH_Z - 1, tall, width), BF16),
            pltpu.VMEM((ny, DEPTH_Z, tall, width), BF16),
            pltpu.VMEM((ny, DEPTH_Z, tall, width), BF16),
            pltpu.VMEM((routed, tall, width), BF16),
            pltpu.SemaphoreType.DMA((copies,)),
            pltpu.SemaphoreType.DMA((kinds, ny)),
            pltpu.SemaphoreType.DMA((kinds, ny - 1)),
            pltpu.SemaphoreType.DMA((kinds, DEPTH_Z - 1)),
            pltpu.SemaphoreType.DMA((ny,)),
            pltpu.SemaphoreType.DMA((routed,)),
        ],
        compiler_params=pltpu.CompilerParams(
            collective_id=1, has_side_effects=True, vmem_limit_bytes=40 * 2**20
        ),
    )(*laid)
    rest = lay_back(rest, rows)
    return lay_back(slots, rows), rest[0], rest[1]


def passed_along(value, by):
    peers = lax.axis_size("section")
    return lax.ppermute(value, "section", [(i, (i + by) % peers) for i in range(peers)])


def one_hot(row_ids, count):
    return (row_ids[:, None] == jnp.arange(count, dtype=jnp.int32)[None, :]).astype(BF16)


def mm(a, b):
    return jnp.dot(a, b, preferred_element_type=F32)


def mm_t(a, b):
    return lax.dot_general(a, b, (((1,), (1,)), ((), ())), preferred_element_type=F32)


def normalize(layer_rows, gain_row):
    values = layer_rows.astype(F32)
    row_scale = lax.rsqrt(jnp.mean(values * values, axis=1, keepdims=True) + epsilon)
    return values, row_scale, (values * row_scale * gain_row[None, :]).astype(BF16)


def low_rank(coefs, factors):
    high = coefs.astype(BF16)
    low = (coefs - high.astype(F32)).astype(BF16)
    return mm(jnp.concatenate((high, low), 1), jnp.concatenate((factors, factors), 0))


def per_device(layer_in, next_in, returned, norm_gain, gate_weight, up_weight, down_weight, wiring):
    replicas = lax.axis_size("rep")
    position = lax.axis_index("rep")
    partner_offset = lax.axis_size("section") // 2
    rows = layer_in.shape[1]
    features = layer_in.shape[2]
    blocks_dev = rows // BLK
    slot_rows = returned.shape[1]
    tokens = rows * replicas
    gain = norm_gain[0]
    gate, up, down = gate_weight[0], up_weight[0], down_weight[0]
    factor = step_rate / tokens

    values, row_scale, normed_own = normalize(layer_in[0], gain)
    next_values, _, next_own = normalize(next_in[0], gain)
    width = features // QUARTERS

    def quartered(value):
        groups = value.reshape(-1, rows, QUARTERS, width).transpose(2, 1, 0, 3)
        return groups.reshape(QUARTERS * rows, -1)

    head, back, mates, select = gather_shards(
        quartered(jnp.concatenate((normed_own, next_own), 0)),
        quartered(returned[0]),
        wiring[0],
        rows,
        blocks_dev,
    )
    token = jnp.arange(tokens, dtype=jnp.int32)
    quarter_rows = token // rows * QUARTERS * rows + token % rows

    def compact(value):
        flat = value.reshape(replicas * QUARTERS * rows, -1)
        parts = [
            mm(one_hot(quarter_rows + q * rows, flat.shape[0]), flat).astype(BF16)
            for q in range(QUARTERS)
        ]
        return [
            jnp.concatenate([part[:, at : at + width] for part in parts], 1)
            for at in range(0, flat.shape[1], width)
        ]

    normed, nexts_own = compact(head)
    (nexts_mate,) = compact(mates)
    slots = jnp.concatenate(compact(back), 0)
    groups = select.shape[0]
    cotangent = mm(select.transpose(1, 0, 2).reshape(tokens, groups * tokens), slots).astype(BF16)
    lhs = jnp.concatenate((normed, nexts_own, nexts_mate), 0)
    nexts = lhs[tokens:]

    gate_all = mm(lhs, gate)
    up_all = mm(lhs, up)
    gate_act, up_act = gate_all[:tokens], up_all[:tokens]
    sigmoid = jax.nn.sigmoid(gate_act)
    silu = gate_act * sigmoid
    hidden = (silu * up_act).astype(BF16)
    dhidden = mm_t(cotangent, down)
    d_gate = (dhidden * up_act * sigmoid * (1.0 + gate_act * (1.0 - sigmoid))).astype(BF16)
    d_up = (dhidden * silu).astype(BF16)

    coefs = factor * mm_t(nexts, normed)
    next_gate = 0.5 * (gate_all[tokens:] - low_rank(coefs, d_gate))
    next_up = 0.5 * (up_all[tokens:] - low_rank(coefs, d_up))
    to_mate = jnp.stack((next_gate[tokens:], next_up[tokens:])).astype(BF16)
    from_mate = passed_along(to_mate, partner_offset).astype(F32)

    dterm = (mm_t(d_gate, gate) + mm_t(d_up, up)).astype(BF16)
    term = mm(hidden, down)
    own = lax.dynamic_slice_in_dim(term, position * rows, rows, 0) + values
    term = lax.dynamic_update_slice_in_dim(term, own, position * rows, 0).astype(BF16)
    slot_terms = [
        lax.dot_general(
            select[g], term, (((0,), (0,)), ((), ())), preferred_element_type=F32
        )
        .astype(BF16)
        .reshape(replicas, rows, features)
        for g in range(groups)
    ]

    gate_next = next_gate[:tokens] + from_mate[0]
    up_next = next_up[:tokens] + from_mate[1]
    hidden_own = (jax.nn.silu(gate_next) * up_next).astype(BF16)
    hidden_mate = passed_along(hidden_own, partner_offset)
    hidden_both = jnp.concatenate((hidden_own, hidden_mate), 0)
    down_coefs = factor * mm_t(hidden_both, hidden)
    term_next = (0.5 * (mm(hidden_both, down) - low_rank(down_coefs, cotangent))).astype(BF16)
    term_next = term_next.reshape(2, replicas, rows, features)
    slots, dnormed, own_sum = sum_terms(
        term_next[1], slot_terms, dterm.reshape(replicas, rows, features), term_next[0]
    )
    next_out = (own_sum + next_values).astype(BF16)
    forwarded = slots.reshape(slot_rows, features)
    scaled = gain[None, :] * dnormed
    cotangent_own = lax.dynamic_slice_in_dim(cotangent, position * rows, rows, 0)
    input_grad = (
        cotangent_own.astype(F32)
        + row_scale * scaled
        - values * row_scale**3 * jnp.mean(values * scaled, axis=1, keepdims=True)
    ).astype(BF16)
    return (forwarded[None], input_grad[None], next_out[None])


def solution(mesh):
    in_specs = (
        P("section", "rep", None),
        P("section", "rep", None),
        P("section", "rep", None),
        P("section", None),
        P("section", None, "rep"),
        P("section", None, "rep"),
        P("section", "rep", None),
        P("section", None, None),
    )
    out_specs = (P("section", "rep", None), P("section", "rep", None), P("section", "rep", None))
    return jax.shard_map(
        per_device, mesh=mesh, in_specs=in_specs, out_specs=out_specs, check_vma=False
    )
```

time: 99.6 us -> 115 us (1.15)
  matrix products: 20.4 us -> 34.5 us
  local copies, waits for them, and re-layouts: 11.5 us -> 18.5 us
  waiting for transfers between devices: 4.24 us -> 1.81 us
  starting transfers between devices: 4.27 us -> 2.1 us
  Pallas kernels: 50.5 us -> 48.4 us
    dot_general x13 -> x20, matrix products: 12.5 us -> 22 us  [mm(): return jnp.dot(a, b, preferred_element_type=F32)]
    slice x3 -> x9, local copies, waits for them, and re-layouts: 0.63 us -> 6.04 us  [the longest x8 6.03 us: compact(): part[:, at:at + width]]
    dot_general x5, matrix products: 7.92 us -> 11.9 us  [mm_t(): lax.dot_general(a, b, (((1,), (1,)), ((), ())), preferred_element_type=F32)]
    pallas_call x1, Pallas kernels: 26 us -> 22.2 us  [sum_terms(): pl.pallas_call(functools.partial(sum_kernel, ny, routed), out_shape=[jax....]
    ppermute x4 -> x2, waiting for transfers between devices: 4.24 us -> 1.81 us  [passed_along(): lax.ppermute(value, 'section', [(i, (i + by) % peers) for i in range(peer...]
    ppermute x4 -> x2, starting transfers between devices: 4.27 us -> 2.1 us  [passed_along(): lax.ppermute(value, 'section', [(i, (i + by) % peers) for i in range(peer...]
    pallas_call x1, Pallas kernels: 24.5 us -> 26.3 us  [gather_shards(): pl.pallas_call(functools.partial(gather_kernel, ny, rows, blocks_dev), ou...]
    another operation x6 -> x10, local copies, waits for them, and re-layouts: 3.81 us -> 5.1 us  [lay_terms(): laid = terms.reshape(DEPTH_Z, ny, CORES, rows, QUARTERS, width)]
  transfers between devices with their start and end apart: 4 -> 2, of which waited for: 2 -> 1; matrix products, arithmetic and copies ran while one was open for 15% -> 11% of each run, Pallas kernels for 0% -> 0%
where the time goes in v4:
time: 115 us; the launch traced here: 114 us
  Pallas kernels  48.4 us (42%)
  matrix products  34.5 us (30%)
  local copies, waits for them, and re-layouts  18.5 us (16%)
  other arithmetic  7.2 us (6%)
  starting transfers between devices  2.1 us (2%)
  waiting for transfers between devices  1.81 us (2%)
  between operations  1.23 us (1%)
    pallas_call x1, Pallas kernels, gather_shards(): pl.pallas_call(functools.partial(gather_kernel, ny, rows, blocks_dev), ou...  26.3 us
    pallas_call x1, Pallas kernels, sum_terms(): pl.pallas_call(functools.partial(sum_kernel, ny, routed), out_shape=[jax....  22.2 us
    dot_general x20, matrix products, mm(): return jnp.dot(a, b, preferred_element_type=F32)  22 us
    dot_general x5, matrix products, mm_t(): lax.dot_general(a, b, (((1,), (1,)), ((), ())), preferred_element_type=F32)  11.9 us
    slice x8, local copies, waits for them, and re-layouts, compact(): part[:, at:at + width]  6.03 us
    another operation x10, local copies, waits for them, and re-layouts, lay_terms(): laid = terms.reshape(DEPTH_Z, ny, CORES, rows, QUARTERS, width)  5.1 us
    unnamed x36, local copies, waits for them, and re-layouts  2.92 us
  transfers between devices with their start and end apart: 2, of which 1 were waited for; matrix products, arithmetic and copies ran while one was open for 11% of the time, Pallas kernels for 0%

profile of v4, /device:TPU:0, one launch (start us, length us, event | category | flops | bytes accessed | tf_op | source)
XLA Modules:
  0.0 113.9 jit_solution(5633039320267409892)
XLA Ops:
  0.7 0.9 fusion.93
  1.6 0.9 fusion.89
  2.5 0.9 fusion.95
  3.6 0.9 reshape_squeeze.9
  4.6 0.7 copy-done
  5.2 26.3 %shard_map.103 = (bf16[16,16,2048]{2,1,0:T(8,128)(2,1)S(1)}, bf16[16,16,2048]{2,1,0:T(8,128)(2,1)S(1)}, bf16[16,16,1024]{2,1,0:T(8,128)(2,1)S(1)}, bf16[2,64,64]{2,1,0:T(8,128)(2,1)S(1)}) custom-call(bf16[16,2048]{1,0:T(8,128)(2,1)S(1)} %bitcast.139, bf16[16,2048]{1,0:T(8,128)(2,1)S(1)} %bitcast.140, s32[16,16]{1,0:T(8,128)S(1)} %bitcast.142), custom_call_target="tpu_custom_call" | custom-call | tf_op jit(solution)/shard_map/pallas_call | solution.py:205
  31.5 1.0 convolution_convert_fusion.3
  32.6 1.0 convolution_convert_fusion.4
  33.6 0.9 convolution_convert_fusion.11
  34.5 0.9 convolution_convert_fusion.12
  35.4 1.0 convolution_convert_fusion.5
  36.4 0.9 convolution_convert_fusion.13
  37.3 1.1 convolution_convert_fusion.6
  38.3 0.9 convolution_convert_fusion.14
  39.2 1.0 convolution_convert_fusion.7
  40.3 1.0 convolution_convert_fusion.8
  41.3 1.1 convolution_convert_fusion.9
  42.4 0.3 convolution_convert_fusion.10
  42.9 1.1 fusion.138
  44.0 1.0 fusion.137
  45.0 1.0 fusion.136
  46.0 1.0 fusion.135
  46.9 1.0 fusion.134
  47.9 1.0 fusion.133
  49.1 0.5 fusion.140
  49.6 1.6 %slice-done.5 = s8[4194304]{0:T(1024)(128)(4,1)S(1)} async-done(((s8[7340032]{0:T(1024)(128)(4,1)}), s8[4194304]{0:T(1024)(128)(4,1)S(1)}, s32[]{:S(2)}) %slice-start.5) | async-done | bytes 4194328
  51.2 1.8 %fusion.12 = f32[192,896]{1,0:T(8,128)S(1)} fusion(bf16[1,4096,896]{2,1,0:T(8,128)(2,1)S(1)} %bitcast.148, bf16[64,1024]{1,0:T(8,128)(2,1)S(1)} %copy-done.7, bf16[64,1024]{1,0:T(8,128)(2,1)S(1)} %copy-done.8, bf16[64,1024]{1,0:T(8,128)(2,1)S(1)} %copy-done.9, bf16[64,1024]{1,0:T(8,128)(2,1)S(1)} %copy-done.10, bf16[64,1024]{1,0:T(8,128)(2,1)S(1)} %get-tuple-element.29, ...), kind=kOutput, calls=%fused_computation.12 | convolution fusion | flops 1428160512 | bytes 9601024 | tf_op jit(solution)/shard_map/dot_general | solution.py:403
  53.0 0.5 slice-done.3
  53.5 1.8 %fusion.2 = f32[192,896]{1,0:T(8,128)S(1)} fusion(bf16[1,4096,896]{2,1,0:T(8,128)(2,1)S(1)} %bitcast.146, bf16[64,1024]{1,0:T(8,128)(2,1)S(1)} %copy-done.7, bf16[64,1024]{1,0:T(8,128)(2,1)S(1)} %copy-done.8, bf16[64,1024]{1,0:T(8,128)(2,1)S(1)} %copy-done.9, bf16[64,1024]{1,0:T(8,128)(2,1)S(1)} %copy-done.10, bf16[64,1024]{1,0:T(8,128)(2,1)S(1)} %get-tuple-element.29, ...), kind=kOutput, calls=%fused_computation.2 | convolution fusion | flops 1428160512 | bytes 9601024 | tf_op jit(solution)/shard_map/dot_general | solution.py:403
  55.4 0.3 convolution_convert_fusion.2
  55.7 2.4 %multiply_convert_fusion.2 = (bf16[64,896]{1,0:T(8,128)(2,1)S(1)}, bf16[64,896]{1,0:T(8,128)(2,1)S(1)}, bf16[64,896]{1,0:T(8,128)(2,1)S(1)}) fusion(f32[192,896]{1,0:T(8,128)S(1)} %fusion.12, f32[192,896]{1,0:T(8,128)S(1)} %fusion.2, bf16[64,4096]{1,0:T(8,128)(2,1)S(1)} %convolution_convert_fusion.2, bf16[1,896,4096]{2,1,0:T(8,128)(2,1)S(1)} %bitcast.144), kind=kOutput, calls=%fused_computation.107 | convolution fusion | flops 470622208 | bytes 8667136 | tf_op jit(solution)/shard_map/dot_general | solution.py:407
  58.1 0.3 fusion.30
  58.4 0.3 fusion.29
  58.7 0.8 pad_maximum_fusion
  59.5 1.2 %collective-permute-start = (bf16[2,64,896]{2,1,0:T(8,128)(2,1)}, bf16[2,64,896]{2,1,0:T(8,128)(2,1)}, u32[]{:S(2)}, u32[]{:S(2)}) collective-permute-start(bf16[2,64,896]{2,1,0:T(8,128)(2,1)} %pad_maximum_fusion), channel_id=1, source_target_pairs={{0,16},{16,0},{1,17},{17,1},{2,18},{18,2},{3,19},{19,3},{4,20},{20... | collective-permute-start | bytes 688136 | tf_op jit(solution)/shard_map/ppermute | solution.py:395
  60.7 2.3 %fusion = f32[64,4096]{1,0:T(8,128)S(1)} fusion(bf16[64,896]{1,0:T(8,128)(2,1)S(1)} %get-tuple-element.21, bf16[1,4096,896]{2,1,0:T(8,128)(2,1)S(1)} %bitcast.146), kind=kOutput, calls=%fused_computation | convolution fusion | flops 469762048 | bytes 8503296 | tf_op jit(solution)/shard_map/dot_general | solution.py:407
  63.1 1.4 %fusion.4 = f32[64,4096]{1,0:T(8,128)S(1)} fusion(bf16[64,896]{1,0:T(8,128)(2,1)S(1)} %get-tuple-element.18, bf16[1,896,4096]{2,1,0:T(8,128)(2,1)S(1)} %bitcast.144), kind=kOutput, calls=%fused_computation.4 | convolution fusion | flops 469762048 | bytes 8503296 | tf_op jit(solution)/shard_map/dot_general | solution.py:403
  64.5 5.6 %fusion.26 = bf16[64,4096]{1,0:T(8,128)(2,1)S(1)} fusion(f32[64,4096]{1,0:T(8,128)S(1)} %fusion, bf16[64,896]{1,0:T(8,128)(2,1)S(1)} %get-tuple-element.17, bf16[1,4096,896]{2,1,0:T(8,128)(2,1)} %param.12), kind=kOutput, calls=%fused_computation.18 | convolution fusion | flops 470286336 | bytes 9027584 | tf_op jit(solution)/shard_map/dot_general | solution.py:407
  70.2 0.3 convolution_convert_fusion.1
  70.5 1.0 convert_element_type.158
  71.5 1.1 fusion.76
  72.6 0.9 collective-permute-start.1
  73.5 0.3 convolution_convert_fusion
  73.8 0.4 reshape_reshape.9
  74.2 0.3 copy.38
  74.6 0.4 reshape_reshape.10
  75.0 0.3 copy.37
  75.4 0.4 reshape_reshape.11
  75.8 0.3 copy.36
  76.2 1.8 %collective-permute-done.1 = bf16[64,896]{1,0:T(8,128)(2,1)} collective-permute-done((bf16[64,896]{1,0:T(8,128)(2,1)S(1)}, bf16[64,896]{1,0:T(8,128)(2,1)}, u32[]{:S(2)}, u32[]{:S(2)}) %collective-permute-start.1) | collective-permute-done | bytes 114720 | tf_op jit(solution)/shard_map/ppermute | solution.py:395
  78.0 1.1 subtract_convert_fusion
  79.1 0.5 fusion.61
  79.6 4.4 %fusion.20 = bf16[128,4096]{1,0:T(8,128)(2,1)S(1)} fusion(f32[128,4096]{1,0:T(8,128)S(1)} %fusion.61, bf16[1,896,4096]{2,1,0:T(8,128)(2,1)} %param.14, bf16[64,896]{1,0:T(8,128)(2,1)} %collective-permute-done.1, bf16[64,896]{1,0:T(8,128)(2,1)S(1)} %fusion.76), kind=kOutput, calls=%fused_computation.16 | convolution fusion | flops 941555712 | bytes 10715136 | tf_op jit(solution)/shard_map/dot_general | solution.py:403
  84.0 0.9 fusion.130
  84.9 0.4 reshape_squeeze.10
  85.3 0.3 copy.39
  85.7 1.4 %reshape_squeeze.11 = bf16[4,2,2,4,4,1024]{5,4,3,2,1,0:T(4,128)(2,1)S(1)} reshape(bf16[64,4096]{1,0:T(8,128)(2,1)} %get-tuple-element.19) | data formatting | bytes 1048576 | tf_op jit(solution)/shard_map/reshape;squeeze | solution.py:343
  87.2 1.1 copy.35
  88.2 1.2 %reshape.131.refs_4_ = bf16[2,2,4,16,1024]{4,3,2,1,0:T(8,128)(2,1)S(1)} reshape(bf16[2,2,4,4,4,1024]{5,4,3,2,1,0:T(4,128)(2,1)} %bitcast.153) | data formatting | bytes 1048576 | tf_op jit(solution)/shard_map/reshape | solution.py:344
  89.4 22.2 %shard_map.104 = (bf16[2,16,1024]{2,1,0:T(8,128)(2,1)S(1)}, f32[2,16,1024]{2,1,0:T(8,128)S(1)}) custom-call(bf16[2,2,4,16,1024]{4,3,2,1,0:T(8,128)(2,1)S(1)} %reshape.127.refs_0_, bf16[2,2,4,16,1024]{4,3,2,1,0:T(8,128)(2,1)S(1)} %reshape.128.refs_1_, bf16[2,2,4,16,1024]{4,3,2,1,0:T(8,128)(2,1)S(1)} %reshape.129.refs_2_, ...), custom_call_target="tpu_custom_call" | custom-call | tf_op jit(solution)/shard_map/pallas_call | solution.py:361
  111.6 0.7 broadcast_in_dim_reshape_reshape.3
  112.4 0.1 fusion.100
  112.5 0.6 fusion.92
  113.2 0.7 fusion.116
  (60 shorter events, 1.2 us)
Async XLA Ops:
  4.5 0.7 copy-start
  38.3 11.2 %slice-start.4 = ((s8[7340032]{0:T(1024)(128)(4,1)}), s8[3145728]{0:T(1024)(128)(4,1)S(1)}, s32[]{:S(2)}) async-start(s8[7340032]{0:T(1024)(128)(4,1)} %bitcast.147), calls=%async_computation.4 | async-start | bytes 6291456
  42.9 6.1 %copy-start.3 = (bf16[64,2048]{1,0:T(8,128)(2,1)S(1)}, bf16[64,2048]{1,0:T(8,128)(2,1)}, u32[]{:S(2)}) copy-start(bf16[64,2048]{1,0:T(8,128)(2,1)} %convolution_convert_fusion.9) | copy-start | bytes 786436
  42.9 6.1 %copy-start.7 = (bf16[64,1024]{1,0:T(8,128)(2,1)S(1)}, bf16[64,1024]{1,0:T(8,128)(2,1)}, u32[]{:S(2)}) copy-start(bf16[64,1024]{1,0:T(8,128)(2,1)} %convolution_convert_fusion.11) | copy-start | bytes 393220
  42.9 6.1 %copy-start.8 = (bf16[64,1024]{1,0:T(8,128)(2,1)S(1)}, bf16[64,1024]{1,0:T(8,128)(2,1)}, u32[]{:S(2)}) copy-start(bf16[64,1024]{1,0:T(8,128)(2,1)} %convolution_convert_fusion.12) | copy-start | bytes 393220
  42.9 6.1 %copy-start.9 = (bf16[64,1024]{1,0:T(8,128)(2,1)S(1)}, bf16[64,1024]{1,0:T(8,128)(2,1)}, u32[]{:S(2)}) copy-start(bf16[64,1024]{1,0:T(8,128)(2,1)} %convolution_convert_fusion.13) | copy-start | bytes 393220
  42.9 6.1 %copy-start.10 = (bf16[64,1024]{1,0:T(8,128)(2,1)S(1)}, bf16[64,1024]{1,0:T(8,128)(2,1)}, u32[]{:S(2)}) copy-start(bf16[64,1024]{1,0:T(8,128)(2,1)} %convolution_convert_fusion.14) | copy-start | bytes 393220
  49.0 2.2 %slice-start.5 = ((s8[7340032]{0:T(1024)(128)(4,1)}), s8[4194304]{0:T(1024)(128)(4,1)S(1)}, s32[]{:S(2)}) async-start(s8[7340032]{0:T(1024)(128)(4,1)} %bitcast.147), calls=%async_computation.5 | async-start | bytes 8388608
  49.0 4.0 %slice-start.2 = ((s8[7340032]{0:T(1024)(128)(4,1)}), s8[4194304]{0:T(1024)(128)(4,1)S(1)}, s32[]{:S(2)}) async-start(s8[7340032]{0:T(1024)(128)(4,1)} %bitcast.145), calls=%async_computation.2 | async-start | bytes 8388608
  51.2 2.4 %slice-start.3 = ((s8[7340032]{0:T(1024)(128)(4,1)}), s8[3145728]{0:T(1024)(128)(4,1)S(1)}, s32[]{:S(2)}) async-start(s8[7340032]{0:T(1024)(128)(4,1)} %bitcast.145), calls=%async_computation.3 | async-start | bytes 6291456
  51.2 4.5 %slice-start = ((s8[7340032]{0:T(1024)(128)(4,1)}), s8[4194304]{0:T(1024)(128)(4,1)S(1)}, s32[]{:S(2)}) async-start(s8[7340032]{0:T(1024)(128)(4,1)} %bitcast.143), calls=%async_computation | async-start | bytes 8388608
  53.5 2.2 %slice-start.1 = ((s8[7340032]{0:T(1024)(128)(4,1)}), s8[3145728]{0:T(1024)(128)(4,1)S(1)}, s32[]{:S(2)}) async-start(s8[7340032]{0:T(1024)(128)(4,1)} %bitcast.143), calls=%async_computation.1 | async-start | bytes 6291456
  58.3 4.7 %copy-start.1 = (f32[128,896]{1,0:T(8,128)}, f32[128,896]{1,0:T(8,128)S(1)}, u32[]{:S(2)}) copy-start(f32[128,896]{1,0:T(8,128)S(1)} %fusion.30) | copy-start | bytes 1376260
  58.6 4.4 %copy-start.2 = (f32[128,896]{1,0:T(8,128)}, f32[128,896]{1,0:T(8,128)S(1)}, u32[]{:S(2)}) copy-start(f32[128,896]{1,0:T(8,128)S(1)} %fusion.29) | copy-start | bytes 1376260
  59.5 11.1 %collective-permute-start = (bf16[2,64,896]{2,1,0:T(8,128)(2,1)}, bf16[2,64,896]{2,1,0:T(8,128)(2,1)}, u32[]{:S(2)}, u32[]{:S(2)}) collective-permute-start(bf16[2,64,896]{2,1,0:T(8,128)(2,1)} %pad_maximum_fusion), channel_id=1, source_target_pairs={{0,16},{16,0},{1,17},{17,1},{2,18},{18,2},{3,19},{19,3},{4,20},{20... | collective-permute-start | bytes 688136 | tf_op jit(solution)/shard_map/ppermute | solution.py:395
  64.5 5.6 %copy-start.4 = (bf16[1,4,4096]{2,1,0:T(4,128)(2,1)S(1)}, bf16[1,4,4096]{2,1,0:T(4,128)(2,1)}, u32[]{:S(2)}) copy-start(bf16[1,4,4096]{2,1,0:T(4,128)(2,1)} %param.8) | copy-start | bytes 98308
  72.6 5.4 %collective-permute-start.1 = (bf16[64,896]{1,0:T(8,128)(2,1)S(1)}, bf16[64,896]{1,0:T(8,128)(2,1)}, u32[]{:S(2)}, u32[]{:S(2)}) collective-permute-start(bf16[64,896]{1,0:T(8,128)(2,1)S(1)} %fusion.76), channel_id=1, source_target_pairs={{0,16},{16,0},{1,17},{17,1},{2,18},{18,2},{3,19},{19,3},{4,20},{20... | collective-permute-start | bytes 344072 | tf_op jit(solution)/shard_map/ppermute | solution.py:395
  85.7 26.7 %copy-start.6 = (f32[1,4096]{1,0:T(1,128)S(1)}, f32[1,4096]{1,0:T(1,128)}, u32[]{:S(2)}) copy-start(f32[1,4096]{1,0:T(1,128)} %param.11) | copy-start | bytes 49156
  87.1 25.4 %copy-start.5 = (bf16[1,4,4096]{2,1,0:T(4,128)(2,1)S(1)}, bf16[1,4,4096]{2,1,0:T(4,128)(2,1)}, u32[]{:S(2)}) copy-start(bf16[1,4,4096]{2,1,0:T(4,128)(2,1)} %param.9) | copy-start | bytes 98308

commit v5 on v4

--- a/solution.py
+++ b/solution.py
@@ -66,8 +66,11 @@
     row_start = mm(counts, ahead)
     column_start = mm(behind, counts)
     receiver = iota(square, 1).astype(F32)
-    spread = jnp.ones((replicas, tokens), F32)
-    target = (iota((tokens, tokens), 0) % BLK).astype(F32)
+    raw = tokens * QUARTERS
+    spread = jnp.ones((replicas, raw), F32)
+    spread_down = jnp.ones((groups * tokens, replicas), F32)
+    target = (iota((tokens, raw), 0) % BLK).astype(F32)
+    target_down = (iota((groups * tokens, tokens), 1) % BLK).astype(F32)
     owner = iota((tokens, replicas), 0) // rows == iota((tokens, replicas), 1)
     block = iota((tokens, replicas), 0) % rows // BLK
     for b in range(blocks_dev):
@@ -75,13 +78,29 @@
         slot = jnp.where(inside, receiver * capacity + column_start + b - row_start, 0.0)
         rows_of = (owner & (block == b)).astype(F32)
         target = target + BLK * mm(rows_of, mm(slot, spread))
-    lane = iota((tokens, tokens), 1)
-    place_of = lane // rows * (rows * groups) + lane % rows
-    return [(target == (place_of + g * rows).astype(F32)).astype(F32) for g in range(groups)]
+        target_down = target_down + BLK * mm_t(mm_t(spread_down, slot), rows_of)
+    lane = iota((tokens, raw), 1)
+    quarter = lane % (QUARTERS * rows) // rows
+    slot_row = lane // (QUARTERS * rows) * (rows * groups) + lane % rows
+    picks = [
+        [
+            ((target == (slot_row + g * rows).astype(F32)) & (quarter == q)).astype(F32)
+            for g in range(groups)
+        ]
+        for q in range(QUARTERS)
+    ]
+    line = iota((groups * tokens, tokens), 0)
+    inner = line % tokens
+    sent = inner // rows * (rows * groups) + line // tokens * rows + inner % rows
+    own = iota((tokens, raw), 0)
+    own = own // rows * (QUARTERS * rows) + own % rows
+    compact = [(lane == own + q * rows).astype(F32) for q in range(QUARTERS)]
+    return picks, compact, (target_down == sent.astype(F32)).astype(F32)
 
 
 def gather_kernel(
-    ny, rows, blocks_dev, head_ref, back_ref, wiring_ref, head, back, mates, select, send, send_x, recv
+    ny, rows, blocks_dev, head_ref, back_ref, wiring_ref, lhs, cotangent, select,
+    head, back, mates, send, send_x, recv
 ):
     z, y, core, index = place(ny)
     sections = lax.axis_size("section")
@@ -160,11 +179,12 @@
                             over_x(shard).start()
 
     along_z(0)
-    matrices = routing_matrices(
-        wiring_ref[...], rows, blocks_dev, select.shape[0] * rows // BLK, select.shape[0]
-    )
-    for g, matrix in enumerate(matrices):
-        select[g] = matrix.astype(BF16)
+    tokens = cotangent.shape[0]
+    groups = back.shape[2] // width
+    picks, compact, sent = routing_matrices(
+        wiring_ref[...], rows, blocks_dev, groups * rows // BLK, groups
+    )
+    select[...] = sent.astype(BF16)
     for d in range(1, DEPTH_Z):
         along_z(d)
         from_y(d - 1)
@@ -177,6 +197,19 @@
     for kind in range(3):
         for dz, dy in every:
             arrive(kind, index((z + dz) % DEPTH_Z, (y + dy) % ny, 1 - core))
+    flat = [out[...].reshape(tokens * QUARTERS, out.shape[2]) for out in outs]
+    for q in range(QUARTERS):
+        columns = slice(q * width, (q + 1) * width)
+        pick = compact[q].astype(BF16)
+        both = mm(pick, flat[0]).astype(BF16)
+        lhs[:tokens, columns] = both[:, :width]
+        lhs[tokens : 2 * tokens, columns] = both[:, width:]
+        lhs[2 * tokens :, columns] = mm(pick, flat[2]).astype(BF16)
+        cot = sum(
+            mm(picks[q][g].astype(BF16), flat[1][:, g * width : (g + 1) * width])
+            for g in range(groups)
+        )
+        cotangent[:, columns] = cot.astype(BF16)
     back_copy.wait_send()
     for kind in range(2):
         for d in range(DEPTH_Z):
@@ -205,20 +238,22 @@
     return pl.pallas_call(
         functools.partial(gather_kernel, ny, rows, blocks_dev),
         out_shape=[
-            jax.ShapeDtypeStruct((replicas,) + head.shape, BF16),
-            jax.ShapeDtypeStruct((replicas,) + back.shape, BF16),
-            jax.ShapeDtypeStruct((replicas, tall, wide // 2), BF16),
-            jax.ShapeDtypeStruct((groups, tokens, tokens), BF16),
+            jax.ShapeDtypeStruct((3 * tokens, QUARTERS * wide // 2), BF16),
+            jax.ShapeDtypeStruct((tokens, QUARTERS * wide // 2), BF16),
+            jax.ShapeDtypeStruct((groups * tokens, tokens), BF16),
         ],
         in_specs=[vmem] * 3,
-        out_specs=[vmem] * 4,
+        out_specs=[vmem] * 3,
         scratch_shapes=[
+            pltpu.VMEM((replicas,) + head.shape, BF16),
+            pltpu.VMEM((replicas,) + back.shape, BF16),
+            pltpu.VMEM((replicas, tall, wide // 2), BF16),
             pltpu.SemaphoreType.DMA((3, 2 + ny, replicas)),
             pltpu.SemaphoreType.DMA((replicas + 1,)),
             pltpu.SemaphoreType.DMA((3, replicas)),
         ],
         compiler_params=pltpu.CompilerParams(
-            collective_id=0, has_side_effects=True, vmem_limit_bytes=32 * 2**20
+            collective_id=0, has_side_effects=True, vmem_limit_bytes=20 * 2**20
         ),
     )(head, back, wiring)
 
@@ -383,7 +418,7 @@
             pltpu.SemaphoreType.DMA((routed,)),
         ],
         compiler_params=pltpu.CompilerParams(
-            collective_id=1, has_side_effects=True, vmem_limit_bytes=40 * 2**20
+            collective_id=1, has_side_effects=True, vmem_limit_bytes=20 * 2**20
         ),
     )(*laid)
     rest = lay_back(rest, rows)
@@ -393,10 +428,6 @@
 def passed_along(value, by):
     peers = lax.axis_size("section")
     return lax.ppermute(value, "section", [(i, (i + by) % peers) for i in range(peers)])
-
-
-def one_hot(row_ids, count):
-    return (row_ids[:, None] == jnp.arange(count, dtype=jnp.int32)[None, :]).astype(BF16)
 
 
 def mm(a, b):
@@ -440,33 +471,14 @@
         groups = value.reshape(-1, rows, QUARTERS, width).transpose(2, 1, 0, 3)
         return groups.reshape(QUARTERS * rows, -1)
 
-    head, back, mates, select = gather_shards(
+    lhs, cotangent, select = gather_shards(
         quartered(jnp.concatenate((normed_own, next_own), 0)),
         quartered(returned[0]),
         wiring[0],
         rows,
         blocks_dev,
     )
-    token = jnp.arange(tokens, dtype=jnp.int32)
-    quarter_rows = token // rows * QUARTERS * rows + token % rows
-
-    def compact(value):
-        flat = value.reshape(replicas * QUARTERS * rows, -1)
-        parts = [
-            mm(one_hot(quarter_rows + q * rows, flat.shape[0]), flat).astype(BF16)
-            for q in range(QUARTERS)
-        ]
-        return [
-            jnp.concatenate([part[:, at : at + width] for part in parts], 1)
-            for at in range(0, flat.shape[1], width)
-        ]
-
-    normed, nexts_own = compact(head)
-    (nexts_mate,) = compact(mates)
-    slots = jnp.concatenate(compact(back), 0)
-    groups = select.shape[0]
-    cotangent = mm(select.transpose(1, 0, 2).reshape(tokens, groups * tokens), slots).astype(BF16)
-    lhs = jnp.concatenate((normed, nexts_own, nexts_mate), 0)
+    normed = lhs[:tokens]
     nexts = lhs[tokens:]
 
     gate_all = mm(lhs, gate)
@@ -489,14 +501,7 @@
     term = mm(hidden, down)
     own = lax.dynamic_slice_in_dim(term, position * rows, rows, 0) + values
     term = lax.dynamic_update_slice_in_dim(term, own, position * rows, 0).astype(BF16)
-    slot_terms = [
-        lax.dot_general(
-            select[g], term, (((0,), (0,)), ((), ())), preferred_element_type=F32
-        )
-        .astype(BF16)
-        .reshape(replicas, rows, features)
-        for g in range(groups)
-    ]
+    slot_terms = mm(select, term).astype(BF16).reshape(-1, replicas, rows, features)
 
     gate_next = next_gate[:tokens] + from_mate[0]
     up_next = next_up[:tokens] + from_mate[1]

time: 115 us -> 100 us (0.87)
  local copies, waits for them, and re-layouts: 18.5 us -> 10.6 us
  matrix products: 34.5 us -> 29.2 us
  waiting for transfers between devices: 1.81 us -> 0.01 us
    dot_general x20 -> x8, matrix products: 22 us -> 14.2 us  [mm(): return jnp.dot(a, b, preferred_element_type=F32)]
    slice x8 -> x0, local copies, waits for them, and re-layouts: 6.03 us -> none  [compact(): part[:, at:at + width]]
    dot_general x5, matrix products: 11.9 us -> 15 us  [mm_t(): lax.dot_general(a, b, (((1,), (1,)), ((), ())), preferred_element_type=F32)]
    unnamed x36 -> x20, local copies, waits for them, and re-layouts: 2.92 us -> 1.03 us
    ppermute x2, waiting for transfers between devices: 1.81 us -> 0.01 us  [passed_along(): lax.ppermute(value, 'section', [(i, (i + by) % peers) for i in range(peer...]
    pallas_call x1, Pallas kernels: 26.3 us -> 27.5 us  [gather_shards(): pl.pallas_call(functools.partial(gather_kernel, ny, rows, blocks_dev), ou...]
  transfers between devices with their start and end apart: 2 -> 2, of which waited for: 1 -> 0; matrix products, arithmetic and copies ran while one was open for 11% -> 15% of each run, Pallas kernels for 0% -> 0%
where the time goes in v5:
time: 100 us; the launch traced here: 99.7 us
  Pallas kernels  49.3 us (49%)
  matrix products  29.2 us (29%)
  local copies, waits for them, and re-layouts  10.6 us (11%)
  other arithmetic  7.09 us (7%)
  starting transfers between devices  2.44 us (2%)
  between operations  1.07 us (1%)
    pallas_call x1, Pallas kernels, gather_shards(): pl.pallas_call(functools.partial(gather_kernel, ny, rows, blocks_dev), ou...  27.5 us
    pallas_call x1, Pallas kernels, sum_terms(): pl.pallas_call(functools.partial(sum_kernel, ny, routed), out_shape=[jax....  21.8 us
    dot_general x5, matrix products, mm_t(): lax.dot_general(a, b, (((1,), (1,)), ((), ())), preferred_element_type=F32)  15 us
    dot_general x8, matrix products, mm(): return jnp.dot(a, b, preferred_element_type=F32)  14.2 us
    another operation x10, local copies, waits for them, and re-layouts, lay_terms(): laid = terms.reshape(DEPTH_Z, ny, CORES, rows, QUARTERS, width)  5.1 us
    ppermute x2, starting transfers between devices, passed_along(): lax.ppermute(value, 'section', [(i, (i + by) % peers) for i in range(peer...  2.44 us
  transfers between devices with their start and end apart: 2, of which 0 were waited for; matrix products, arithmetic and copies ran while one was open for 15% of the time, Pallas kernels for 0%

profile of v5, /device:TPU:0, one launch (start us, length us, event | category | flops | bytes accessed | tf_op | source)
XLA Modules:
  0.0 99.7 jit_solution(15228740086225702679)
XLA Ops:
  0.6 0.9 fusion.53
  1.5 0.9 fusion.57
  2.5 0.9 fusion.59
  3.4 0.1 copy.11
  3.5 0.9 reshape_squeeze.9
  4.4 0.1 copy.12
  4.5 0.0 copy-start
  4.5 0.7 copy-done
  5.2 27.5 %shard_map.103 = (bf16[192,4096]{1,0:T(8,128)(2,1)S(1)}, bf16[64,4096]{1,0:T(8,128)(2,1)S(1)}, bf16[128,64]{1,0:T(8,128)(2,1)S(1)}) custom-call(bf16[16,2048]{1,0:T(8,128)(2,1)S(1)} %bitcast.107, bf16[16,2048]{1,0:T(8,128)(2,1)S(1)} %bitcast.108, s32[16,16]{1,0:T(8,128)S(1)} %bitcast.109), custom_call_target="tpu_custom_call" | custom-call | tf_op jit(solution)/shard_map/pallas_call | solution.py:238
  32.7 0.0 slice-start.2
  32.7 0.5 fusion.77
  33.2 0.0 slice-start.3
  33.2 0.0 slice-start
  33.2 5.2 %fusion.12 = f32[192,896]{1,0:T(8,128)S(1)} fusion(bf16[192,4096]{1,0:T(8,128)(2,1)S(1)} %get-tuple-element.8, bf16[1,4096,896]{2,1,0:T(8,128)(2,1)} %param.12), kind=kOutput, calls=%fused_computation.12 | convolution fusion | flops 1409286144 | bytes 9601024 | tf_op jit(solution)/shard_map/dot_general | solution.py:434
  38.4 0.0 slice-done.2
  38.4 0.0 slice-done.3
  38.5 0.0 slice-start.1
  38.5 1.8 %fusion.2 = f32[192,896]{1,0:T(8,128)S(1)} fusion(bf16[192,4096]{1,0:T(8,128)(2,1)S(1)} %get-tuple-element.8, bf16[1,4096,896]{2,1,0:T(8,128)(2,1)S(1)} %bitcast.113), kind=kOutput, calls=%fused_computation.2 | convolution fusion | flops 1409286144 | bytes 9601024 | tf_op jit(solution)/shard_map/dot_general | solution.py:434
  40.3 0.0 slice-done
  40.3 0.3 slice-done.1
  40.6 2.4 %multiply_convert_fusion.2 = (bf16[64,896]{1,0:T(8,128)(2,1)S(1)}, bf16[64,896]{1,0:T(8,128)(2,1)S(1)}, bf16[64,896]{1,0:T(8,128)(2,1)S(1)}) fusion(f32[192,896]{1,0:T(8,128)S(1)} %fusion.12, f32[192,896]{1,0:T(8,128)S(1)} %fusion.2, bf16[64,4096]{1,0:T(8,128)(2,1)S(1)} %get-tuple-element.9, bf16[1,896,4096]{2,1,0:T(8,128)(2,1)S(1)} %bitcast.111), kind=kOutput, calls=%fused_computation.56 | convolution fusion | flops 470622208 | bytes 8667136 | tf_op jit(solution)/shard_map/dot_general | solution.py:438
  42.9 0.2 fusion.29
  43.2 0.2 fusion.30
  43.5 0.0 copy-start.1
  43.5 0.0 copy-start.2
  43.5 0.8 pad_maximum_fusion
  44.3 1.2 %collective-permute-start = (bf16[2,64,896]{2,1,0:T(8,128)(2,1)}, bf16[2,64,896]{2,1,0:T(8,128)(2,1)}, u32[]{:S(2)}, u32[]{:S(2)}) collective-permute-start(bf16[2,64,896]{2,1,0:T(8,128)(2,1)} %pad_maximum_fusion), channel_id=1, source_target_pairs={{0,16},{16,0},{1,17},{17,1},{2,18},{18,2},{3,19},{19,3},{4,20},{20... | collective-permute-start | bytes 688136 | tf_op jit(solution)/shard_map/ppermute | solution.py:430
  45.6 0.0 copy-done.1
  45.6 1.4 %fusion.4 = f32[64,4096]{1,0:T(8,128)S(1)} fusion(bf16[64,896]{1,0:T(8,128)(2,1)S(1)} %get-tuple-element.16, bf16[1,896,4096]{2,1,0:T(8,128)(2,1)S(1)} %bitcast.111), kind=kOutput, calls=%fused_computation.4 | convolution fusion | flops 469762048 | bytes 8503296 | tf_op jit(solution)/shard_map/dot_general | solution.py:434
  47.1 0.4 convolution_convert_fusion
  47.5 0.1 fusion.75
  47.6 5.4 %fusion = f32[64,4096]{1,0:T(8,128)S(1)} fusion(bf16[64,896]{1,0:T(8,128)(2,1)S(1)} %get-tuple-element.21, bf16[1,4096,896]{2,1,0:T(8,128)(2,1)} %param.13), kind=kOutput, calls=%fused_computation | convolution fusion | flops 469762048 | bytes 8503296 | tf_op jit(solution)/shard_map/dot_general | solution.py:438
  53.0 0.0 collective-permute-done
  53.0 1.0 convert_element_type.91
  54.0 1.0 %fusion.40 = bf16[64,896]{1,0:T(8,128)(2,1)S(1)} fusion(f32[2,64,896]{2,1,0:T(8,128)S(1)} %convert_element_type.91, f32[128,896]{1,0:T(8,128)} %copy-done.1, f32[128,896]{1,0:T(8,128)S(1)} %fusion.29), kind=kLoop, calls=%fused_computation.41 | loop fusion | flops 458752 | bytes 1032192 | tf_op jit(solution)/shard_map/convert_element_type | solution.py:508
  55.0 1.2 %collective-permute-start.1 = (bf16[64,896]{1,0:T(8,128)(2,1)S(1)}, bf16[64,896]{1,0:T(8,128)(2,1)}, u32[]{:S(2)}, u32[]{:S(2)}) collective-permute-start(bf16[64,896]{1,0:T(8,128)(2,1)S(1)} %fusion.40), channel_id=1, source_target_pairs={{0,16},{16,0},{1,17},{17,1},{2,18},{18,2},{3,19},{19,3},{4,20},{20... | collective-permute-start | bytes 344072 | tf_op jit(solution)/shard_map/ppermute | solution.py:430
  56.2 5.6 %fusion.26 = bf16[64,4096]{1,0:T(8,128)(2,1)S(1)} fusion(f32[64,4096]{1,0:T(8,128)S(1)} %fusion, bf16[64,896]{1,0:T(8,128)(2,1)S(1)} %get-tuple-element.15, bf16[1,4096,896]{2,1,0:T(8,128)(2,1)} %param.12), kind=kOutput, calls=%fused_computation.19 | convolution fusion | flops 470286336 | bytes 9027584 | tf_op jit(solution)/shard_map/dot_general | solution.py:438
  61.8 0.4 reshape_reshape.3
  62.2 0.3 copy.27
  62.5 0.1 reshape.88.refs_3_
  62.6 0.4 reshape_unstack.6
  63.0 0.3 copy.29
  63.3 0.1 reshape.86.refs_1_
  63.4 0.4 reshape_unstack.7
  63.8 0.3 copy.28
  64.1 0.1 reshape.87.refs_2_
  64.2 0.0 collective-permute-done.1
  64.2 1.1 %subtract_convert_fusion = (bf16[128,64]{0,1:T(8,128)(2,1)S(1)}, bf16[128,64]{0,1:T(8,128)(2,1)S(1)}) fusion(bf16[64,896]{1,0:T(8,128)(2,1)S(1)} %get-tuple-element.16, bf16[64,896]{1,0:T(8,128)(2,1)} %collective-permute-done.1, bf16[64,896]{1,0:T(8,128)(2,1)S(1)} %fusion.40), kind=kOutput, calls=%fused_computation.87 | convolution fusion | flops 15179776 | bytes 376832 | tf_op jit(solution)/shard_map/dot_general | solution.py:438
  65.3 0.5 fusion.31
  65.8 4.4 %fusion.20 = bf16[128,4096]{1,0:T(8,128)(2,1)S(1)} fusion(f32[128,4096]{1,0:T(8,128)S(1)} %fusion.31, bf16[1,896,4096]{2,1,0:T(8,128)(2,1)} %param.14, bf16[64,896]{1,0:T(8,128)(2,1)} %collective-permute-done.1, bf16[64,896]{1,0:T(8,128)(2,1)S(1)} %fusion.40), kind=kOutput, calls=%fused_computation.16 | convolution fusion | flops 941555712 | bytes 10715136 | tf_op jit(solution)/shard_map/dot_general | solution.py:434
  70.2 0.0 copy-start.4
  70.3 0.0 copy-start.3
  70.3 0.9 fusion.74
  71.1 0.4 reshape_squeeze.10
  71.5 0.3 copy.30
  71.8 0.1 reshape.85.refs_0_
  71.9 1.4 %reshape_squeeze.11 = bf16[4,2,2,4,4,1024]{5,4,3,2,1,0:T(4,128)(2,1)S(1)} reshape(bf16[64,4096]{1,0:T(8,128)(2,1)} %get-tuple-element.17) | data formatting | bytes 1048576 | tf_op jit(solution)/shard_map/reshape;squeeze | solution.py:378
  73.4 1.1 %copy.26 = bf16[4,2,2,4,4,1024]{5,3,4,0,1,2:T(4,128)(2,1)} copy(bf16[4,2,2,4,4,1024]{5,4,3,2,1,0:T(4,128)(2,1)S(1)} %reshape_squeeze.11) | data formatting | bytes 1048576 | tf_op jit(solution)/shard_map/reshape;squeeze | solution.py:378
  74.4 1.2 %reshape.89.refs_4_ = bf16[2,2,4,16,1024]{4,3,2,1,0:T(8,128)(2,1)S(1)} reshape(bf16[2,2,4,4,4,1024]{5,4,3,2,1,0:T(4,128)(2,1)} %bitcast.118) | data formatting | bytes 1048576 | tf_op jit(solution)/shard_map/reshape | solution.py:379
  75.6 21.8 %shard_map.104 = (bf16[2,16,1024]{2,1,0:T(8,128)(2,1)S(1)}, f32[2,16,1024]{2,1,0:T(8,128)S(1)}) custom-call(bf16[2,2,4,16,1024]{4,3,2,1,0:T(8,128)(2,1)S(1)} %reshape.85.refs_0_, bf16[2,2,4,16,1024]{4,3,2,1,0:T(8,128)(2,1)S(1)} %reshape.86.refs_1_, bf16[2,2,4,16,1024]{4,3,2,1,0:T(8,128)(2,1)S(1)} %reshape.87.refs_2_, ...), custom_call_target="tpu_custom_call" | custom-call | tf_op jit(solution)/shard_map/pallas_call | solution.py:396
  97.5 0.1 fusion.64
  97.6 0.6 fusion.56
  98.3 0.7 broadcast_in_dim_reshape_reshape.3
  99.0 0.7 fusion.68
  (18 shorter events, 0.3 us)
Async XLA Ops:
  4.5 0.7 copy-start
  32.7 5.7 %slice-start.2 = ((s8[7340032]{0:T(1024)(128)(4,1)}), s8[4194304]{0:T(1024)(128)(4,1)S(1)}, s32[]{:S(2)}) async-start(s8[7340032]{0:T(1024)(128)(4,1)} %bitcast.112), calls=%async_computation.2 | async-start | bytes 8388608
  33.2 5.2 %slice-start.3 = ((s8[7340032]{0:T(1024)(128)(4,1)}), s8[3145728]{0:T(1024)(128)(4,1)S(1)}, s32[]{:S(2)}) async-start(s8[7340032]{0:T(1024)(128)(4,1)} %bitcast.112), calls=%async_computation.3 | async-start | bytes 6291456
  33.2 7.1 %slice-start = ((s8[7340032]{0:T(1024)(128)(4,1)}), s8[4194304]{0:T(1024)(128)(4,1)S(1)}, s32[]{:S(2)}) async-start(s8[7340032]{0:T(1024)(128)(4,1)} %bitcast.110), calls=%async_computation | async-start | bytes 8388608
  38.5 2.1 %slice-start.1 = ((s8[7340032]{0:T(1024)(128)(4,1)}), s8[3145728]{0:T(1024)(128)(4,1)S(1)}, s32[]{:S(2)}) async-start(s8[7340032]{0:T(1024)(128)(4,1)} %bitcast.110), calls=%async_computation.1 | async-start | bytes 6291456
  43.5 2.1 %copy-start.1 = (f32[128,896]{1,0:T(8,128)}, f32[128,896]{1,0:T(8,128)S(1)}, u32[]{:S(2)}) copy-start(f32[128,896]{1,0:T(8,128)S(1)} %fusion.30) | copy-start | bytes 1376260
  43.5 3.5 %copy-start.2 = (bf16[1,4,4096]{2,1,0:T(4,128)(2,1)S(1)}, bf16[1,4,4096]{2,1,0:T(4,128)(2,1)}, u32[]{:S(2)}) copy-start(bf16[1,4,4096]{2,1,0:T(4,128)(2,1)} %param.8) | copy-start | bytes 98308
  44.3 8.7 %collective-permute-start = (bf16[2,64,896]{2,1,0:T(8,128)(2,1)}, bf16[2,64,896]{2,1,0:T(8,128)(2,1)}, u32[]{:S(2)}, u32[]{:S(2)}) collective-permute-start(bf16[2,64,896]{2,1,0:T(8,128)(2,1)} %pad_maximum_fusion), channel_id=1, source_target_pairs={{0,16},{16,0},{1,17},{17,1},{2,18},{18,2},{3,19},{19,3},{4,20},{20... | collective-permute-start | bytes 688136 | tf_op jit(solution)/shard_map/ppermute | solution.py:430
  55.0 9.2 %collective-permute-start.1 = (bf16[64,896]{1,0:T(8,128)(2,1)S(1)}, bf16[64,896]{1,0:T(8,128)(2,1)}, u32[]{:S(2)}, u32[]{:S(2)}) collective-permute-start(bf16[64,896]{1,0:T(8,128)(2,1)S(1)} %fusion.40), channel_id=1, source_target_pairs={{0,16},{16,0},{1,17},{17,1},{2,18},{18,2},{3,19},{19,3},{4,20},{20... | collective-permute-start | bytes 344072 | tf_op jit(solution)/shard_map/ppermute | solution.py:430
  70.2 27.2 %copy-start.4 = (f32[1,4096]{1,0:T(1,128)S(1)}, f32[1,4096]{1,0:T(1,128)}, u32[]{:S(2)}) copy-start(f32[1,4096]{1,0:T(1,128)} %param.11) | copy-start | bytes 49156
  70.3 27.4 %copy-start.3 = (bf16[1,4,4096]{2,1,0:T(4,128)(2,1)S(1)}, bf16[1,4,4096]{2,1,0:T(4,128)(2,1)}, u32[]{:S(2)}) copy-start(bf16[1,4,4096]{2,1,0:T(4,128)(2,1)} %param.9) | copy-start | bytes 98308

commit v6 on v5

--- a/solution.py
+++ b/solution.py
@@ -253,7 +253,7 @@
             pltpu.SemaphoreType.DMA((3, replicas)),
         ],
         compiler_params=pltpu.CompilerParams(
-            collective_id=0, has_side_effects=True, vmem_limit_bytes=20 * 2**20
+            collective_id=0, has_side_effects=True, vmem_limit_bytes=32 * 2**20
         ),
     )(head, back, wiring)
 
@@ -418,7 +418,7 @@
             pltpu.SemaphoreType.DMA((routed,)),
         ],
         compiler_params=pltpu.CompilerParams(
-            collective_id=1, has_side_effects=True, vmem_limit_bytes=20 * 2**20
+            collective_id=1, has_side_effects=True, vmem_limit_bytes=40 * 2**20
         ),
     )(*laid)
     rest = lay_back(rest, rows)

time: 100 us -> 100 us (level)
  no operation moved by 1% of the time
where the time goes in v6:
time: 100 us; the launch traced here: 99.7 us
  Pallas kernels  49.3 us (49%)
  matrix products  29.2 us (29%)
  local copies, waits for them, and re-layouts  10.6 us (11%)
  other arithmetic  7.09 us (7%)
  starting transfers between devices  2.44 us (2%)
  between operations  1.07 us (1%)
    pallas_call x1, Pallas kernels, gather_shards(): pl.pallas_call(functools.partial(gather_kernel, ny, rows, blocks_dev), ou...  27.5 us
    pallas_call x1, Pallas kernels, sum_terms(): pl.pallas_call(functools.partial(sum_kernel, ny, routed), out_shape=[jax....  21.8 us
    dot_general x5, matrix products, mm_t(): lax.dot_general(a, b, (((1,), (1,)), ((), ())), preferred_element_type=F32)  15 us
    dot_general x8, matrix products, mm(): return jnp.dot(a, b, preferred_element_type=F32)  14.2 us
    another operation x10, local copies, waits for them, and re-layouts, lay_terms(): laid = terms.reshape(DEPTH_Z, ny, CORES, rows, QUARTERS, width)  5.1 us
    ppermute x2, starting transfers between devices, passed_along(): lax.ppermute(value, 'section', [(i, (i + by) % peers) for i in range(peer...  2.44 us
  transfers between devices with their start and end apart: 2, of which 0 were waited for; matrix products, arithmetic and copies ran while one was open for 15% of the time, Pallas kernels for 0%

profile of v6, /device:TPU:0, one launch (start us, length us, event | category | flops | bytes accessed | tf_op | source)
XLA Modules:
  0.0 99.7 jit_solution(11579334288886720140)
XLA Ops:
  0.6 0.9 fusion.53
  1.5 0.9 fusion.57
  2.5 0.9 fusion.59
  3.4 0.1 copy.11
  3.5 0.9 reshape_squeeze.9
  4.4 0.1 copy.12
  4.5 0.0 copy-start
  4.5 0.7 copy-done
  5.2 27.5 %shard_map.103 = (bf16[192,4096]{1,0:T(8,128)(2,1)S(1)}, bf16[64,4096]{1,0:T(8,128)(2,1)S(1)}, bf16[128,64]{1,0:T(8,128)(2,1)S(1)}) custom-call(bf16[16,2048]{1,0:T(8,128)(2,1)S(1)} %bitcast.107, bf16[16,2048]{1,0:T(8,128)(2,1)S(1)} %bitcast.108, s32[16,16]{1,0:T(8,128)S(1)} %bitcast.109), custom_call_target="tpu_custom_call" | custom-call | tf_op jit(solution)/shard_map/pallas_call | solution.py:238
  32.7 0.0 slice-start.2
  32.7 0.5 fusion.77
  33.2 0.0 slice-start.3
  33.2 0.0 slice-start
  33.2 5.2 %fusion.12 = f32[192,896]{1,0:T(8,128)S(1)} fusion(bf16[192,4096]{1,0:T(8,128)(2,1)S(1)} %get-tuple-element.8, bf16[1,4096,896]{2,1,0:T(8,128)(2,1)} %param.12), kind=kOutput, calls=%fused_computation.12 | convolution fusion | flops 1409286144 | bytes 9601024 | tf_op jit(solution)/shard_map/dot_general | solution.py:434
  38.4 0.0 slice-done.2
  38.4 0.0 slice-done.3
  38.5 0.0 slice-start.1
  38.5 1.8 %fusion.2 = f32[192,896]{1,0:T(8,128)S(1)} fusion(bf16[192,4096]{1,0:T(8,128)(2,1)S(1)} %get-tuple-element.8, bf16[1,4096,896]{2,1,0:T(8,128)(2,1)S(1)} %bitcast.113), kind=kOutput, calls=%fused_computation.2 | convolution fusion | flops 1409286144 | bytes 9601024 | tf_op jit(solution)/shard_map/dot_general | solution.py:434
  40.3 0.0 slice-done
  40.3 0.3 slice-done.1
  40.6 2.4 %multiply_convert_fusion.2 = (bf16[64,896]{1,0:T(8,128)(2,1)S(1)}, bf16[64,896]{1,0:T(8,128)(2,1)S(1)}, bf16[64,896]{1,0:T(8,128)(2,1)S(1)}) fusion(f32[192,896]{1,0:T(8,128)S(1)} %fusion.12, f32[192,896]{1,0:T(8,128)S(1)} %fusion.2, bf16[64,4096]{1,0:T(8,128)(2,1)S(1)} %get-tuple-element.9, bf16[1,896,4096]{2,1,0:T(8,128)(2,1)S(1)} %bitcast.111), kind=kOutput, calls=%fused_computation.56 | convolution fusion | flops 470622208 | bytes 8667136 | tf_op jit(solution)/shard_map/dot_general | solution.py:438
  42.9 0.2 fusion.29
  43.2 0.2 fusion.30
  43.5 0.0 copy-start.1
  43.5 0.0 copy-start.2
  43.5 0.8 pad_maximum_fusion
  44.3 1.2 %collective-permute-start = (bf16[2,64,896]{2,1,0:T(8,128)(2,1)}, bf16[2,64,896]{2,1,0:T(8,128)(2,1)}, u32[]{:S(2)}, u32[]{:S(2)}) collective-permute-start(bf16[2,64,896]{2,1,0:T(8,128)(2,1)} %pad_maximum_fusion), channel_id=1, source_target_pairs={{0,16},{16,0},{1,17},{17,1},{2,18},{18,2},{3,19},{19,3},{4,20},{20... | collective-permute-start | bytes 688136 | tf_op jit(solution)/shard_map/ppermute | solution.py:430
  45.6 0.0 copy-done.1
  45.6 1.4 %fusion.4 = f32[64,4096]{1,0:T(8,128)S(1)} fusion(bf16[64,896]{1,0:T(8,128)(2,1)S(1)} %get-tuple-element.16, bf16[1,896,4096]{2,1,0:T(8,128)(2,1)S(1)} %bitcast.111), kind=kOutput, calls=%fused_computation.4 | convolution fusion | flops 469762048 | bytes 8503296 | tf_op jit(solution)/shard_map/dot_general | solution.py:434
  47.1 0.4 convolution_convert_fusion
  47.5 0.1 fusion.75
  47.6 5.4 %fusion = f32[64,4096]{1,0:T(8,128)S(1)} fusion(bf16[64,896]{1,0:T(8,128)(2,1)S(1)} %get-tuple-element.21, bf16[1,4096,896]{2,1,0:T(8,128)(2,1)} %param.13), kind=kOutput, calls=%fused_computation | convolution fusion | flops 469762048 | bytes 8503296 | tf_op jit(solution)/shard_map/dot_general | solution.py:438
  53.0 0.0 collective-permute-done
  53.0 1.0 convert_element_type.91
  54.0 1.0 %fusion.40 = bf16[64,896]{1,0:T(8,128)(2,1)S(1)} fusion(f32[2,64,896]{2,1,0:T(8,128)S(1)} %convert_element_type.91, f32[128,896]{1,0:T(8,128)} %copy-done.1, f32[128,896]{1,0:T(8,128)S(1)} %fusion.29), kind=kLoop, calls=%fused_computation.41 | loop fusion | flops 458752 | bytes 1032192 | tf_op jit(solution)/shard_map/convert_element_type | solution.py:508
  55.0 1.2 %collective-permute-start.1 = (bf16[64,896]{1,0:T(8,128)(2,1)S(1)}, bf16[64,896]{1,0:T(8,128)(2,1)}, u32[]{:S(2)}, u32[]{:S(2)}) collective-permute-start(bf16[64,896]{1,0:T(8,128)(2,1)S(1)} %fusion.40), channel_id=1, source_target_pairs={{0,16},{16,0},{1,17},{17,1},{2,18},{18,2},{3,19},{19,3},{4,20},{20... | collective-permute-start | bytes 344072 | tf_op jit(solution)/shard_map/ppermute | solution.py:430
  56.2 5.6 %fusion.26 = bf16[64,4096]{1,0:T(8,128)(2,1)S(1)} fusion(f32[64,4096]{1,0:T(8,128)S(1)} %fusion, bf16[64,896]{1,0:T(8,128)(2,1)S(1)} %get-tuple-element.15, bf16[1,4096,896]{2,1,0:T(8,128)(2,1)} %param.12), kind=kOutput, calls=%fused_computation.19 | convolution fusion | flops 470286336 | bytes 9027584 | tf_op jit(solution)/shard_map/dot_general | solution.py:438
  61.8 0.4 reshape_reshape.3
  62.2 0.3 copy.27
  62.5 0.1 reshape.88.refs_3_
  62.6 0.4 reshape_unstack.6
  63.0 0.3 copy.29
  63.3 0.1 reshape.86.refs_1_
  63.4 0.4 reshape_unstack.7
  63.8 0.3 copy.28
  64.1 0.1 reshape.87.refs_2_
  64.2 0.0 collective-permute-done.1
  64.2 1.1 %subtract_convert_fusion = (bf16[128,64]{0,1:T(8,128)(2,1)S(1)}, bf16[128,64]{0,1:T(8,128)(2,1)S(1)}) fusion(bf16[64,896]{1,0:T(8,128)(2,1)S(1)} %get-tuple-element.16, bf16[64,896]{1,0:T(8,128)(2,1)} %collective-permute-done.1, bf16[64,896]{1,0:T(8,128)(2,1)S(1)} %fusion.40), kind=kOutput, calls=%fused_computation.87 | convolution fusion | flops 15179776 | bytes 376832 | tf_op jit(solution)/shard_map/dot_general | solution.py:438
  65.3 0.5 fusion.31
  65.8 4.4 %fusion.20 = bf16[128,4096]{1,0:T(8,128)(2,1)S(1)} fusion(f32[128,4096]{1,0:T(8,128)S(1)} %fusion.31, bf16[1,896,4096]{2,1,0:T(8,128)(2,1)} %param.14, bf16[64,896]{1,0:T(8,128)(2,1)} %collective-permute-done.1, bf16[64,896]{1,0:T(8,128)(2,1)S(1)} %fusion.40), kind=kOutput, calls=%fused_computation.16 | convolution fusion | flops 941555712 | bytes 10715136 | tf_op jit(solution)/shard_map/dot_general | solution.py:434
  70.2 0.0 copy-start.4
  70.3 0.0 copy-start.3
  70.3 0.9 fusion.74
  71.1 0.4 reshape_squeeze.10
  71.5 0.3 copy.30
  71.8 0.1 reshape.85.refs_0_
  71.9 1.4 %reshape_squeeze.11 = bf16[4,2,2,4,4,1024]{5,4,3,2,1,0:T(4,128)(2,1)S(1)} reshape(bf16[64,4096]{1,0:T(8,128)(2,1)} %get-tuple-element.17) | data formatting | bytes 1048576 | tf_op jit(solution)/shard_map/reshape;squeeze | solution.py:378
  73.4 1.1 %copy.26 = bf16[4,2,2,4,4,1024]{5,3,4,0,1,2:T(4,128)(2,1)} copy(bf16[4,2,2,4,4,1024]{5,4,3,2,1,0:T(4,128)(2,1)S(1)} %reshape_squeeze.11) | data formatting | bytes 1048576 | tf_op jit(solution)/shard_map/reshape;squeeze | solution.py:378
  74.4 1.2 %reshape.89.refs_4_ = bf16[2,2,4,16,1024]{4,3,2,1,0:T(8,128)(2,1)S(1)} reshape(bf16[2,2,4,4,4,1024]{5,4,3,2,1,0:T(4,128)(2,1)} %bitcast.118) | data formatting | bytes 1048576 | tf_op jit(solution)/shard_map/reshape | solution.py:379
  75.6 21.8 %shard_map.104 = (bf16[2,16,1024]{2,1,0:T(8,128)(2,1)S(1)}, f32[2,16,1024]{2,1,0:T(8,128)S(1)}) custom-call(bf16[2,2,4,16,1024]{4,3,2,1,0:T(8,128)(2,1)S(1)} %reshape.85.refs_0_, bf16[2,2,4,16,1024]{4,3,2,1,0:T(8,128)(2,1)S(1)} %reshape.86.refs_1_, bf16[2,2,4,16,1024]{4,3,2,1,0:T(8,128)(2,1)S(1)} %reshape.87.refs_2_, ...), custom_call_target="tpu_custom_call" | custom-call | tf_op jit(solution)/shard_map/pallas_call | solution.py:396
  97.5 0.1 fusion.64
  97.6 0.6 fusion.56
  98.3 0.7 broadcast_in_dim_reshape_reshape.3
  99.0 0.7 fusion.68
  (18 shorter events, 0.3 us)
Async XLA Ops:
  4.5 0.7 copy-start
  32.7 5.7 %slice-start.2 = ((s8[7340032]{0:T(1024)(128)(4,1)}), s8[4194304]{0:T(1024)(128)(4,1)S(1)}, s32[]{:S(2)}) async-start(s8[7340032]{0:T(1024)(128)(4,1)} %bitcast.112), calls=%async_computation.2 | async-start | bytes 8388608
  33.2 5.2 %slice-start.3 = ((s8[7340032]{0:T(1024)(128)(4,1)}), s8[3145728]{0:T(1024)(128)(4,1)S(1)}, s32[]{:S(2)}) async-start(s8[7340032]{0:T(1024)(128)(4,1)} %bitcast.112), calls=%async_computation.3 | async-start | bytes 6291456
  33.2 7.1 %slice-start = ((s8[7340032]{0:T(1024)(128)(4,1)}), s8[4194304]{0:T(1024)(128)(4,1)S(1)}, s32[]{:S(2)}) async-start(s8[7340032]{0:T(1024)(128)(4,1)} %bitcast.110), calls=%async_computation | async-start | bytes 8388608
  38.5 2.1 %slice-start.1 = ((s8[7340032]{0:T(1024)(128)(4,1)}), s8[3145728]{0:T(1024)(128)(4,1)S(1)}, s32[]{:S(2)}) async-start(s8[7340032]{0:T(1024)(128)(4,1)} %bitcast.110), calls=%async_computation.1 | async-start | bytes 6291456
  43.5 2.1 %copy-start.1 = (f32[128,896]{1,0:T(8,128)}, f32[128,896]{1,0:T(8,128)S(1)}, u32[]{:S(2)}) copy-start(f32[128,896]{1,0:T(8,128)S(1)} %fusion.30) | copy-start | bytes 1376260
  43.5 3.5 %copy-start.2 = (bf16[1,4,4096]{2,1,0:T(4,128)(2,1)S(1)}, bf16[1,4,4096]{2,1,0:T(4,128)(2,1)}, u32[]{:S(2)}) copy-start(bf16[1,4,4096]{2,1,0:T(4,128)(2,1)} %param.8) | copy-start | bytes 98308
  44.3 8.7 %collective-permute-start = (bf16[2,64,896]{2,1,0:T(8,128)(2,1)}, bf16[2,64,896]{2,1,0:T(8,128)(2,1)}, u32[]{:S(2)}, u32[]{:S(2)}) collective-permute-start(bf16[2,64,896]{2,1,0:T(8,128)(2,1)} %pad_maximum_fusion), channel_id=1, source_target_pairs={{0,16},{16,0},{1,17},{17,1},{2,18},{18,2},{3,19},{19,3},{4,20},{20... | collective-permute-start | bytes 688136 | tf_op jit(solution)/shard_map/ppermute | solution.py:430
  55.0 9.2 %collective-permute-start.1 = (bf16[64,896]{1,0:T(8,128)(2,1)S(1)}, bf16[64,896]{1,0:T(8,128)(2,1)}, u32[]{:S(2)}, u32[]{:S(2)}) collective-permute-start(bf16[64,896]{1,0:T(8,128)(2,1)S(1)} %fusion.40), channel_id=1, source_target_pairs={{0,16},{16,0},{1,17},{17,1},{2,18},{18,2},{3,19},{19,3},{4,20},{20... | collective-permute-start | bytes 344072 | tf_op jit(solution)/shard_map/ppermute | solution.py:430
  70.2 27.2 %copy-start.4 = (f32[1,4096]{1,0:T(1,128)S(1)}, f32[1,4096]{1,0:T(1,128)}, u32[]{:S(2)}) copy-start(f32[1,4096]{1,0:T(1,128)} %param.11) | copy-start | bytes 49156
  70.3 27.4 %copy-start.3 = (bf16[1,4,4096]{2,1,0:T(4,128)(2,1)S(1)}, bf16[1,4,4096]{2,1,0:T(4,128)(2,1)}, u32[]{:S(2)}) copy-start(bf16[1,4,4096]{2,1,0:T(4,128)(2,1)} %param.9) | copy-start | bytes 98308
